TPU v7x, 32 devices: a whole 2x2x4 slice. The times are simulated.
32 devices in a mesh: groups: 2 (over x), tok: 16 (over z, y, core).
Axes of the slice: x: 2, y: 2, z: 4, core: 2. Of those that a mesh axis runs over, the one named last changes fastest.
Arguments:
- inputs_act: bfloat16 [2, 4096, 14336], P(None, ('groups', 'tok')), parts along dimension 1, may hold values from -6 to 6
- out_grads: bfloat16 [2, 4096, 4096], P(None, ('groups', 'tok')), parts along dimension 1, may hold values from -6 to 6
- example_ids: int32 [4096], P(('groups', 'tok')), parts along dimension 0, may hold values from 0 to 255, as said below
- proj_in: bfloat16 [14336, 64], replicated, may hold values from -0.046875 to 0.046875
- proj_out: bfloat16 [4096, 64], replicated, may hold values from -0.09375 to 0.09375
- query_sketch: bfloat16 [2, 128, 4096], P(None, ('groups', 'tok')), parts along dimension 1, may hold values from -6 to 6
- ckpt_weight: float32 [2], replicated, may hold values from 0.3 to 3
Outputs:
- scores: float32 [512, 64], P(('groups', 'tok')), parts along dimension 0
There are 2 independent parts, one for each index of `groups`. A program takes and returns all parts, laid end to end along the dimension named above; an argument that names none is the same for every part. Nothing has to cross between parts.
Inputs may be any that keep to these rules, and one draw needn't show every extreme that they name: `example_ids`: tokens 128 * k to 128 * k + 127 name only examples 16 * k to 16 * k + 15, never falling, each of those named by at least one token.
All inputs are finite; a program needn't handle non-finite values.
Results may differ from a plain program's by a relative error of at most 0.0003.
Values may be sent and summed in bfloat16 or wider, within the bound.
No kernel may reach another device: no remote copies, remote signals or barrier semaphores. Data moves between devices by JAX's collectives and lax.ppermute only.
A program may use at most 64 MiB of HBM per device.

v0:
```python
import jax
import jax.numpy as jnp
from jax import lax
from jax.sharding import PartitionSpec as P

EX_DEV = 16


def damped_inverse(factor):
    size = factor.shape[0]
    eye = jnp.eye(size, dtype=jnp.float32)
    damped = factor + 0.05 * (jnp.trace(factor) / size) * eye
    lower = jnp.linalg.cholesky(damped)
    return jax.scipy.linalg.cho_solve((lower, True), eye)


def local(inputs_act, out_grads, example_ids, proj_in, proj_out, query_sketch, ckpt_weight):
    ckpts = inputs_act.shape[0]
    tok_rows = inputs_act.shape[1]
    side = proj_in.shape[1]
    q_rows = query_sketch.shape[1]
    local_ids = example_ids - lax.axis_index("tok") * EX_DEV
    onehot = (local_ids[None, :] == jnp.arange(EX_DEV, dtype=jnp.int32)[:, None]).astype(
        jnp.float32
    )
    total = tok_rows * lax.axis_size("tok")
    sketches = []
    fact_list_a = []
    fact_list_s = []
    for step in range(ckpts):
        act_side = jnp.dot(inputs_act[step], proj_in, preferred_element_type=jnp.float32)
        grad_side = jnp.dot(out_grads[step], proj_out, preferred_element_type=jnp.float32)
        fact_list_a.append(jnp.dot(act_side.T, act_side, precision=lax.Precision.HIGHEST) / total)
        fact_list_s.append(jnp.dot(grad_side.T, grad_side, precision=lax.Precision.HIGHEST) / total)
        outer = (grad_side[:, :, None] * act_side[:, None, :]).reshape(tok_rows, side * side)
        sketches.append(jnp.dot(onehot, outer, precision=lax.Precision.HIGHEST))
    summed_a, summed_s = lax.psum((jnp.stack(fact_list_a), jnp.stack(fact_list_s)), "tok")
    inverses_a = [damped_inverse(summed_a[step]) for step in range(ckpts)]
    inverses_s = [damped_inverse(summed_s[step]) for step in range(ckpts)]
    precs = []
    for step in range(ckpts):
        queries = query_sketch[step].astype(jnp.float32).reshape(q_rows, side, side)
        prec = jnp.einsum(
            "ij,qjk,kl->qil",
            inverses_s[step],
            queries,
            inverses_a[step],
            precision=lax.Precision.HIGHEST,
        )
        precs.append(prec.reshape(q_rows, side * side))
    scores = jnp.zeros((EX_DEV, q_rows * lax.axis_size("tok")), jnp.float32)
    for step in range(ckpts):
        sketch = sketches[step]
        inner = jnp.dot(
            sketch,
            lax.all_gather(precs[step], "tok", axis=0, tiled=True).T,
            precision=lax.Precision.HIGHEST,
        )
        scores = scores + ckpt_weight[step] / side * inner
    return scores


def solution(mesh):
    return jax.shard_map(
        local,
        mesh=mesh,
        in_specs=(
            P(None, ("groups", "tok"), None),
            P(None, ("groups", "tok"), None),
            P(("groups", "tok")),
            P(),
            P(),
            P(None, ("groups", "tok"), None),
            P(),
        ),
        out_specs=P(("groups", "tok"), None),
        check_vma=False,
    )
```

profile of v0, /device:TPU:0, one launch (start us, length us, event | category | flops | bytes accessed | tf_op | source)
XLA Modules:
  0.0 230.1 jit_solution(9468389548295291633)
XLA Ops:
  6.5 2.0 fusion.13
  8.5 2.0 fusion.11
  10.5 3.8 %fusion.2 = f32[128,64]{0,1:T(8,128)S(1)} fusion(bf16[14336,64]{0,1:T(8,128)(2,1)S(1)} %copy-done, bf16[2,128,14336]{2,1,0:T(8,128)(2,1)} %param.10), kind=kOutput, calls=%fused_computation.2 | convolution fusion | flops 234881024 | bytes 5537792 | tf_op jit(solution)/shard_map/dot_general | solution.py:31
  14.4 1.5 fusion
  18.2 89.7 %all-reduce.3.cloned.1.call-done = (f32[2,64,64]{1,2,0:T(8,128)}, f32[2,64,64]{1,2,0:T(8,128)}) async-done(((f32[2,64,64]{1,2,0:T(8,128)}, f32[2,64,64]{1,2,0:T(8,128)}), (f32[2,64,64]{1,2,0:T(8,128)}, f32[2,64,64]{1,2,0:T(8,128)})) %all-reduce.3.cloned.1.call-update) | async-done | bytes 65552 | tf_op jit(solution)/shard_map/psum | solution.py:37
  107.9 1.4 select_reduce_fusion.4
  110.5 1.4 select_reduce_fusion.5
  113.1 0.8 select_add_fusion
  114.0 5.8 %cholesky.74 = f32[64,64]{1,0:T(8,128)S(1)} custom-call(f32[64,64]{1,0:T(8,128)S(1)} %fusion.40), custom_call_target="Cholesky" | custom-call | tf_op jit(solution)/shard_map/jit(cholesky)/cholesky | solution.py:13
  119.9 0.6 compare_reduce_fusion.3
  120.6 0.7 fusion.25
  121.2 4.9 %custom-call.10 = f32[1,64,64]{1,2,0:T(8,128)S(1)} custom-call(f32[1,64,64]{2,1,0:T(8,128)S(1)} %fusion.25), custom_call_target="InvertDiagBlocksLowerTriangular" | custom-call | tf_op jit(solution)/shard_map/jit(_cho_solve)/triangular_solve | solution.py:14
  126.6 5.8 %cholesky.85 = f32[64,64]{1,0:T(8,128)S(1)} custom-call(f32[64,64]{1,0:T(8,128)S(1)} %fusion.37), custom_call_target="Cholesky" | custom-call | tf_op jit(solution)/shard_map/jit(cholesky)/cholesky | solution.py:13
  132.5 0.6 compare_reduce_fusion.2
  133.2 0.7 fusion.26
  133.8 4.9 %custom-call.11 = f32[1,64,64]{1,2,0:T(8,128)S(1)} custom-call(f32[1,64,64]{2,1,0:T(8,128)S(1)} %fusion.26), custom_call_target="InvertDiagBlocksLowerTriangular" | custom-call | tf_op jit(solution)/shard_map/jit(_cho_solve)/triangular_solve | solution.py:14
  139.6 0.7 reshape.45
  140.7 5.8 %cholesky.96 = f32[64,64]{1,0:T(8,128)S(1)} custom-call(f32[64,64]{1,0:T(8,128)S(1)} %fusion.34), custom_call_target="Cholesky" | custom-call | tf_op jit(solution)/shard_map/jit(cholesky)/cholesky | solution.py:13
  147.2 0.7 fusion.27
  147.9 4.9 %custom-call.12 = f32[1,64,64]{1,2,0:T(8,128)S(1)} custom-call(f32[1,64,64]{2,1,0:T(8,128)S(1)} %fusion.27), custom_call_target="InvertDiagBlocksLowerTriangular" | custom-call | tf_op jit(solution)/shard_map/jit(_cho_solve)/triangular_solve | solution.py:14
  152.9 5.8 %cholesky.107 = f32[64,64]{1,0:T(8,128)S(1)} custom-call(f32[64,64]{1,0:T(8,128)S(1)} %fusion.31), custom_call_target="Cholesky" | custom-call | tf_op jit(solution)/shard_map/jit(cholesky)/cholesky | solution.py:13
  159.4 0.7 fusion.28
  160.1 4.9 %custom-call.13 = f32[1,64,64]{1,2,0:T(8,128)S(1)} custom-call(f32[1,64,64]{2,1,0:T(8,128)S(1)} %fusion.28), custom_call_target="InvertDiagBlocksLowerTriangular" | custom-call | tf_op jit(solution)/shard_map/jit(_cho_solve)/triangular_solve | solution.py:14
  166.2 0.7 reshape.47
  169.5 1.1 fusion.42
  170.6 1.1 fusion.41
  171.6 9.6 %all-gather.5.cloned.1.call-done = f32[16,4,4096]{2,1,0:T(4,128)} async-done(((f32[1,4,4096]{2,1,0:T(4,128)}), f32[16,4,4096]{2,1,0:T(4,128)}) %all-gather.5.cloned.1.call-update) | async-done | bytes 1048592 | tf_op jit(solution)/shard_map/all_gather | solution.py:56
  181.2 1.6 reshape.46
  182.8 0.9 convolution_multiply_fusion.5
  183.7 36.7 %all-gather.7.cloned.1.call-done = f32[16,4,4096]{2,1,0:T(4,128)} async-done(((f32[1,4,4096]{2,1,0:T(4,128)}), f32[16,4,4096]{2,1,0:T(4,128)}) %all-gather.7.cloned.1.call-update) | async-done | bytes 1048592 | tf_op jit(solution)/shard_map/all_gather | solution.py:56
  220.4 1.6 reshape.48
  222.0 1.5 fusion.10
  (55 shorter events, 8.0 us)
Async XLA Ops:
  6.5 4.0 %copy-start = (bf16[14336,64]{0,1:T(8,128)(2,1)S(1)}, bf16[14336,64]{0,1:T(8,128)(2,1)}, u32[]{:S(2)}) copy-start(bf16[14336,64]{0,1:T(8,128)(2,1)} %param.13) | copy-start | bytes 5505028
  6.5 101.4 %all-reduce.3.cloned.1.call-start = ((), (), s32[]{:S(2)}) async-start(), calls=%async_computation.2 | async-start | bytes 262144 | tf_op jit(solution)/shard_map/psum | solution.py:37
  8.5 5.9 %copy-start.3 = (bf16[2,128,14336]{2,1,0:T(8,128)(2,1)S(1)}, bf16[2,128,14336]{2,1,0:T(8,128)(2,1)}, u32[]{:S(2)}) copy-start(bf16[2,128,14336]{2,1,0:T(8,128)(2,1)} %param.10) | copy-start | bytes 22020100
  14.4 3.6 %copy-start.1 = (bf16[2,4,4096]{2,1,0:T(4,128)(2,1)S(1)}, bf16[2,4,4096]{2,1,0:T(4,128)(2,1)}, u32[]{:S(2)}) copy-start(bf16[2,4,4096]{2,1,0:T(4,128)(2,1)} %param.15) | copy-start | bytes 196612
  17.9 149.1 %copy-start.2 = (f32[2]{0:T(128)S(1)}, f32[2]{0:T(128)}, u32[]{:S(2)}) copy-start(f32[2]{0:T(128)} %param.16) | copy-start | bytes 28
  17.9 151.1 %copy-start.4 = (s32[128]{0:T(128)S(1)}, s32[128]{0:T(128)}, u32[]{:S(2)}) copy-start(s32[128]{0:T(128)} %param.12) | copy-start | bytes 1540
  17.9 163.3 %all-gather.5.cloned.1.call-start = ((), (), s32[]{:S(2)}) async-start(), calls=%async_computation | async-start | bytes 1114112 | tf_op jit(solution)/shard_map/all_gather | solution.py:56
  140.4 80.1 %all-gather.7.cloned.1.call-start = ((), (), s32[]{:S(2)}) async-start(), calls=%async_computation.1 | async-start | bytes 1114112 | tf_op jit(solution)/shard_map/all_gather | solution.py:56
Sparse Core Ops, SparseCore 0:
  18.0 89.8 all-reduce.2
  140.5 40.7 all-gather.4
  183.4 36.9 all-gather.6
where the time goes:
time: 231 us; the launch traced here: 230 us
  waiting for transfers between devices  136 us (59%)
  other arithmetic  53.7 us (23%)
  between operations  17.2 us (7%)
  matrix products  17.1 us (7%)
  local copies, waits for them, and re-layouts  5.79 us (3%)
    psum x1, waiting for transfers between devices, local(): lax.psum((jnp.stack(fact_list_a), jnp.stack(fact_list_s)), 'tok')  89.7 us
    all_gather x2, waiting for transfers between devices, local(): lax.all_gather(precs[step], 'tok', axis=0, tiled=True)  46.2 us
    another operation x12, other arithmetic, damped_inverse(): lower = jnp.linalg.cholesky(damped)  26.1 us
    another operation x8, other arithmetic, damped_inverse(): return jax.scipy.linalg.cho_solve((lower, True), eye)  22.2 us
    dot_general x2, matrix products, local(): jnp.dot(inputs_act[step], proj_in, preferred_element_type=jnp.float32)  5.29 us
    unnamed x14, local copies, waits for them, and re-layouts  4.64 us
  transfers between devices with their start and end apart: 3, of which 3 were waited for; matrix products, arithmetic and copies ran while one was open for 14% of the time, Pallas kernels for 0%

commit v1 on v0

v1 whole, which is shorter than its diff:
```python
import functools

import jax
import jax.numpy as jnp
from jax import lax
from jax.experimental import pallas as pl
from jax.experimental.pallas import tpu as pltpu
from jax.sharding import PartitionSpec as P

EX_DEV = 16
HIGH = lax.Precision.HIGHEST
F32 = jnp.float32
BF16 = jnp.bfloat16
VMEM = pl.BlockSpec(memory_space=pltpu.VMEM)
ANY = pl.BlockSpec(memory_space=pl.ANY)


def nt(x, y, precision=None):
    return lax.dot_general(
        x, y, (((1,), (1,)), ((), ())), precision=precision, preferred_element_type=F32
    )


def project_kernel(chunks, act, grad, ids, pin, pout, keep, send, act_v, grad_v, pin_v, pout_v, sems):
    ckpts, rows, depth = act.shape
    side = pin.shape[0]
    step = depth // chunks
    copies = [
        pltpu.make_async_copy(pout, pout_v, sems.at[0]),
        pltpu.make_async_copy(grad, grad_v, sems.at[1]),
    ]
    for k in range(chunks):
        span = pl.ds(k * step, step)
        copies.append(pltpu.make_async_copy(pin.at[:, span], pin_v.at[:, span], sems.at[2 + 2 * k]))
        copies.append(
            pltpu.make_async_copy(act.at[:, :, span], act_v.at[:, :, span], sems.at[3 + 2 * k])
        )
    for copy in copies:
        copy.start()
    copies[0].wait()
    copies[1].wait()
    s = nt(grad_v[...].reshape(ckpts * rows, -1), pout_v[...])
    a = jnp.zeros((ckpts * rows, side), F32)
    for k in range(chunks):
        copies[2 + 2 * k].wait()
        copies[3 + 2 * k].wait()
        span = slice(k * step, (k + 1) * step)
        a = a + nt(act_v[:, :, span].reshape(ckpts * rows, step), pin_v[:, span])
    both = jnp.concatenate([a, s], axis=1)
    odd = lax.rem(lax.axis_index("tok"), 2)
    first, second = both[:rows], both[rows:]
    keep[...] = jnp.where(odd == 0, first, second)
    send[0:rows, :] = jnp.where(odd == 0, second, first)
    send[rows : rows + 8, :] = jnp.broadcast_to(ids[...].astype(F32), (8, rows))


def project(act, grad, ids, pin, pout):
    ckpts, rows, depth = act.shape
    side, width = pout.shape
    chunks = 8
    return pl.pallas_call(
        functools.partial(project_kernel, chunks),
        out_shape=(
            jax.ShapeDtypeStruct((rows, 2 * side), F32),
            jax.ShapeDtypeStruct((rows + 8, 2 * side), F32),
        ),
        in_specs=[ANY, ANY, VMEM, ANY, ANY],
        out_specs=(VMEM, VMEM),
        scratch_shapes=[
            pltpu.VMEM((ckpts, rows, depth), BF16),
            pltpu.VMEM((ckpts, rows, width), BF16),
            pltpu.VMEM((side, depth), BF16),
            pltpu.VMEM((side, width), BF16),
            pltpu.SemaphoreType.DMA((2 + 2 * chunks,)),
        ],
        compiler_params=pltpu.CompilerParams(vmem_limit_bytes=40 * 2**20),
        name="project",
    )(act, grad, ids, pin, pout)


def factor_kernel(total, mine, other, out):
    rows, lanes = mine.shape
    side = lanes // 2
    x = jnp.concatenate([mine[...], other[0:rows, :]], axis=0)
    g = lax.dot_general(
        x, x, (((0,), (0,)), ((), ())), precision=HIGH, preferred_element_type=F32
    )
    lane = lax.broadcasted_iota(jnp.int32, (side, lanes), 1)
    out[...] = jnp.where(lane < side, g[:side], g[side:]) * (1.0 / total)


def inverse_kernel(g, out):
    side, lanes = g.shape
    lane = lax.broadcasted_iota(jnp.int32, (side, lanes), 1)
    row = lax.broadcasted_iota(jnp.int32, (side, lanes), 0)
    left = lane < side
    local = jnp.where(left, lane, lane - side)
    m = g[...]
    diag = jnp.sum(jnp.where(local == row, m, 0.0), axis=0, keepdims=True)
    lead = left[:1]
    tr_a = jnp.sum(jnp.where(lead, diag, 0.0), axis=1, keepdims=True)
    tr_s = jnp.sum(jnp.where(lead, 0.0, diag), axis=1, keepdims=True)
    damp = 0.05 * (jnp.where(lead, tr_a, tr_s) / side)
    m = m + jnp.where(local == row, damp, 0.0)
    for k in range(side):
        col = jnp.where(left, m[:, k : k + 1], m[:, side + k : side + k + 1])
        pivot = 1.0 / col[k : k + 1]
        mark = local[:1] == k
        line = jnp.where(mark, 1.0, m[k : k + 1]) * pivot
        here = row == k
        m = jnp.where(here, 0.0, jnp.where(local == k, 0.0, m)) - jnp.where(here, -1.0, col) * line
    out[...] = m


def split(x):
    hi = x.astype(BF16)
    return hi, (x - hi.astype(F32)).astype(BF16)


def score_kernel(q_rows, masks, inv, mine, other, ids, queries, weight, keep, send):
    rows, lanes = mine.shape
    side = lanes // 2
    ckpt = lax.rem(lax.axis_index("tok"), 2)
    me = lax.axis_index("tok")
    x = jnp.concatenate([mine[...], other[0:rows, :]], axis=0)
    lane = lax.broadcasted_iota(jnp.int32, (side, lanes), 1)
    left = lane < side
    p = inv[...]
    ai = jnp.where(left, p, pltpu.roll(p, side, 1))
    si = jnp.where(left, 0.0, p)
    aa = jnp.dot(
        x,
        jnp.concatenate([ai, jnp.zeros_like(ai)], axis=0),
        precision=HIGH,
        preferred_element_type=F32,
    )
    st = nt(si, x, HIGH)
    a_hi, a_lo = split(aa)
    s_hi, s_lo = split(st)
    s_hi, s_lo = s_hi.astype(F32), s_lo.astype(F32)
    example = lax.broadcasted_iota(jnp.int32, (EX_DEV, rows), 0)
    own_ids = ids[...] - me * EX_DEV
    near = me + 1 - 2 * ckpt
    far_ids = other[rows : rows + 1, :].astype(jnp.int32) - near * EX_DEV
    parts = []
    for block, which in enumerate((own_ids, far_ids)):
        mask = (which == example).astype(F32)
        span = slice(block * rows, (block + 1) * rows)
        lhs = jnp.concatenate(
            [
                (v[:, None, span] * mask[None]).reshape(side * EX_DEV, rows).astype(BF16)
                for v in (s_hi, s_lo)
            ],
            axis=1,
        )
        rhs = jnp.concatenate(
            [
                jnp.concatenate([a_hi[span], a_lo[span]], axis=1),
                jnp.concatenate([a_hi[span], jnp.zeros_like(a_lo[span])], axis=1),
            ],
            axis=0,
        )
        both = jnp.dot(lhs, rhs, preferred_element_type=F32)
        both = (both[:, :lanes] + both[:, lanes:]).reshape(side // 2, 2, EX_DEV, lanes)
        first = lax.broadcasted_iota(jnp.int32, (EX_DEV, lanes), 1) < side
        parts.append(
            jnp.concatenate(
                [jnp.where(first, both[j, 0], both[j, 1]) for j in range(side // 2)], axis=1
            )
        )
    sketch = jnp.concatenate(parts, axis=0)
    k_hi, k_lo = split(sketch)
    inner = nt(jnp.concatenate([k_hi, k_lo], axis=0), queries[...])
    inner = inner[: 2 * EX_DEV] + inner[2 * EX_DEV :]
    count = queries.shape[0]
    src = lax.broadcasted_iota(jnp.int32, (count, count), 0)
    dst = lax.broadcasted_iota(jnp.int32, (count, count), 1)
    shift = q_rows.bit_length() - 1
    block = me
    for bit, mask in enumerate(masks):
        block = block ^ ((src >> (shift + bit)) & 1) * mask
    order = (block * q_rows + (src & (q_rows - 1)) == dst).astype(F32)
    scores = jnp.dot(inner, order, precision=HIGH, preferred_element_type=F32)
    scores = scores * (weight[ckpt] / side)
    keep[...] = scores[:EX_DEV]
    send[...] = scores[EX_DEV:]


def local(inputs_act, out_grads, example_ids, proj_in, proj_out, query_sketch, ckpt_weight):
    rows = inputs_act.shape[1]
    side = proj_in.shape[1]
    q_rows = query_sketch.shape[1]
    devices = lax.axis_size("tok")
    total = rows * devices
    me = lax.axis_index("tok")

    def swap(x, mask):
        return lax.ppermute(x, "tok", [(i, i ^ mask) for i in range(devices)])

    ids = example_ids.reshape(1, rows)
    even = lax.rem(me, 2) == 0
    q_keep = jnp.where(even, query_sketch[0], query_sketch[1])
    q_send = jnp.where(even, query_sketch[1], query_sketch[0])
    mine, send = project(inputs_act, out_grads, ids, proj_in.T, proj_out.T)
    other = swap(send, 1)
    queries = jnp.concatenate([q_keep, swap(q_send, 1)], axis=0)
    g = pl.pallas_call(
        functools.partial(factor_kernel, total),
        out_shape=jax.ShapeDtypeStruct((side, 2 * side), F32),
        in_specs=[VMEM, VMEM],
        out_specs=VMEM,
        name="factor",
    )(mine, other)
    masks = [1]
    while devices >> len(masks) > 1:
        masks.append(devices >> len(masks))
    for mask in masks[1:]:
        g = g + swap(g, mask)
        queries = jnp.concatenate([queries, swap(queries, mask)], axis=0)
    inv = pl.pallas_call(
        inverse_kernel,
        out_shape=jax.ShapeDtypeStruct((side, 2 * side), F32),
        in_specs=[VMEM],
        out_specs=VMEM,
        name="inverse",
    )(g)
    keep, send = pl.pallas_call(
        functools.partial(score_kernel, q_rows, tuple(masks)),
        out_shape=(
            jax.ShapeDtypeStruct((EX_DEV, q_rows * devices), F32),
            jax.ShapeDtypeStruct((EX_DEV, q_rows * devices), F32),
        ),
        in_specs=[VMEM] * 5 + [pl.BlockSpec(memory_space=pltpu.SMEM)],
        out_specs=(VMEM, VMEM),
        compiler_params=pltpu.CompilerParams(vmem_limit_bytes=40 * 2**20),
        name="score",
    )(inv, mine, other, ids, queries, ckpt_weight)
    return keep + swap(send, 1)


def solution(mesh):
    return jax.shard_map(
        local,
        mesh=mesh,
        in_specs=(
            P(None, ("groups", "tok"), None),
            P(None, ("groups", "tok"), None),
            P(("groups", "tok")),
            P(),
            P(),
            P(None, ("groups", "tok"), None),
            P(),
        ),
        out_specs=P(("groups", "tok"), None),
        check_vma=False,
    )
```

time: 231 us -> 64.4 us (0.28)
  waiting for transfers between devices: 136 us -> 19.8 us
  other arithmetic: 53.7 us -> 2.95 us
  Pallas kernels: 0 us -> 17.7 us
  between operations: 17.2 us -> 0.08 us
  matrix products: 17.1 us -> 0 us
  starting transfers between devices: 0.27 us -> 11.5 us
  local copies, waits for them, and re-layouts: 5.79 us -> 11.7 us
    psum x1 -> x0, waiting for transfers between devices: 89.7 us -> none  [local(): lax.psum((jnp.stack(fact_list_a), jnp.stack(fact_list_s)), 'tok')]
    another operation x22 -> x0, other arithmetic: 49.5 us -> none  [the longest x12 26.1 us: damped_inverse(): lower = jnp.linalg.cholesky(damped)]
    all_gather x2 -> x0, waiting for transfers between devices: 46.2 us -> none  [local(): lax.all_gather(precs[step], 'tok', axis=0, tiled=True)]
    ppermute x0 -> x9, waiting for transfers between devices: none -> 19.8 us  [swap(): return lax.ppermute(x, 'tok', [(i, i ^ mask) for i in range(devices)])]
    pallas_call x0 -> x4, Pallas kernels: none -> 17.7 us  [the longest x1 7.26 us: local(): pl.pallas_call(inverse_kernel, out_shape=jax.ShapeDtypeStruct((side, 2 *...]
    dot_general x16 -> x0, matrix products: 15.5 us -> none  [the longest x2 5.29 us: local(): jnp.dot(inputs_act[step], proj_in, preferred_element_type=jnp.float32)]
    ppermute x0 -> x9, starting transfers between devices: none -> 11.5 us  [swap(): return lax.ppermute(x, 'tok', [(i, i ^ mask) for i in range(devices)])]
    unnamed x14 -> x24, local copies, waits for them, and re-layouts: 4.64 us -> 11.6 us
  transfers between devices with their start and end apart: 3 -> 9, of which waited for: 3 -> 8; matrix products, arithmetic and copies ran while one was open for 14% -> 2% of each run, Pallas kernels for 0% -> 25%
where the time goes in v1:
time: 64.4 us; the launch traced here: 63.7 us
  waiting for transfers between devices  19.8 us (31%)
  Pallas kernels  17.7 us (27%)
  local copies, waits for them, and re-layouts  11.7 us (18%)
  starting transfers between devices  11.5 us (18%)
  other arithmetic  2.95 us (5%)
    ppermute x9, waiting for transfers between devices, swap(): return lax.ppermute(x, 'tok', [(i, i ^ mask) for i in range(devices)])  19.8 us
    unnamed x24, local copies, waits for them, and re-layouts  11.6 us
    ppermute x9, starting transfers between devices, swap(): return lax.ppermute(x, 'tok', [(i, i ^ mask) for i in range(devices)])  11.5 us
    pallas_call x1, Pallas kernels, local(): pl.pallas_call(inverse_kernel, out_shape=jax.ShapeDtypeStruct((side, 2 *...  7.26 us
    pallas_call x1, Pallas kernels, project(): pl.pallas_call(functools.partial(project_kernel, chunks), out_shape=(jax....  6.79 us
    pallas_call x1, Pallas kernels, local(): pl.pallas_call(functools.partial(factor_kernel, total), out_shape=jax.Sha...  1.85 us
    pallas_call x1, Pallas kernels, local(): pl.pallas_call(functools.partial(score_kernel, q_rows, tuple(masks)), out...  1.77 us
    add x3, other arithmetic, local(): g = g + swap(g, mask)  1.39 us
  transfers between devices with their start and end apart: 9, of which 8 were waited for; matrix products, arithmetic and copies ran while one was open for 2% of the time, Pallas kernels for 25%

profile of v1, /device:TPU:0, one launch (start us, length us, event | category | flops | bytes accessed | tf_op | source)
XLA Modules:
  0.0 63.7 jit_solution(7873675755302127136)
XLA Ops:
  0.0 0.8 %select_bitcast_fusion = (bf16[4,4096]{1,0:T(4,128)(2,1)S(1)}, bf16[4,4096]{1,0:T(4,128)(2,1)S(1)}) fusion(pred[]{:T(512)S(6)} %eq.3, bf16[2,4,4096]{2,1,0:T(4,128)(2,1)} %param.12), kind=kLoop, calls=%fused_computation.3 | loop fusion | flops 32768 | bytes 131073 | tf_op jit(solution)/shard_map/jit(_where)/select_n | solution.py:203
  0.8 0.5 collective-permute-start.4
  1.3 0.9 %collective-permute-done.4 = bf16[4,4096]{1,0:T(4,128)(2,1)S(1)} collective-permute-done((bf16[4,4096]{1,0:T(4,128)(2,1)S(1)}, bf16[4,4096]{1,0:T(4,128)(2,1)S(1)}, u32[]{:S(2)}, u32[]{:S(2)}) %collective-permute-start.4) | collective-permute-done | bytes 32800 | tf_op jit(solution)/shard_map/ppermute | solution.py:198
  2.2 4.0 %collective-permute-start.5 = (bf16[8,4096]{1,0:T(8,128)(2,1)S(1)}, bf16[8,4096]{1,0:T(8,128)(2,1)S(1)}, u32[]{:S(2)}, u32[]{:S(2)}) collective-permute-start(bf16[8,4096]{1,0:T(8,128)(2,1)S(1)} %pad_maximum_fusion.2), channel_id=1, source_target_pairs={{0,8},{1,9},{2,10},{3,11},{4,12},{5,13},{6,14},{7,15},{8,0},{9,1},... | collective-permute-start | bytes 196616 | tf_op jit(solution)/shard_map/ppermute | solution.py:198
  6.2 3.8 %collective-permute-done.5 = bf16[8,4096]{1,0:T(8,128)(2,1)S(1)} collective-permute-done((bf16[8,4096]{1,0:T(8,128)(2,1)S(1)}, bf16[8,4096]{1,0:T(8,128)(2,1)S(1)}, u32[]{:S(2)}, u32[]{:S(2)}) %collective-permute-start.5) | collective-permute-done | bytes 65568 | tf_op jit(solution)/shard_map/ppermute | solution.py:198
  10.1 0.8 %collective-permute-start.6 = (bf16[16,4096]{1,0:T(8,128)(2,1)S(1)}, bf16[16,4096]{1,0:T(8,128)(2,1)S(1)}, u32[]{:S(2)}, u32[]{:S(2)}) collective-permute-start(bf16[16,4096]{1,0:T(8,128)(2,1)S(1)} %pad_maximum_fusion.1), channel_id=1, source_target_pairs={{0,4},{1,5},{2,6},{3,7},{4,0},{5,1},{6,2},{7,3},{8,12},{9,13},{10,... | collective-permute-start | bytes 393224 | tf_op jit(solution)/shard_map/ppermute | solution.py:198
  10.9 4.2 %collective-permute-done.6 = bf16[16,4096]{1,0:T(8,128)(2,1)S(1)} collective-permute-done((bf16[16,4096]{1,0:T(8,128)(2,1)S(1)}, bf16[16,4096]{1,0:T(8,128)(2,1)S(1)}, u32[]{:S(2)}, u32[]{:S(2)}) %collective-permute-start.6) | collective-permute-done | bytes 131104 | tf_op jit(solution)/shard_map/ppermute | solution.py:198
  15.2 1.7 %collective-permute-start.7 = (bf16[32,4096]{1,0:T(8,128)(2,1)S(1)}, bf16[32,4096]{1,0:T(8,128)(2,1)S(1)}, u32[]{:S(2)}, u32[]{:S(2)}) collective-permute-start(bf16[32,4096]{1,0:T(8,128)(2,1)S(1)} %pad_maximum_fusion), channel_id=1, source_target_pairs={{0,2},{1,3},{2,0},{3,1},{4,6},{5,7},{6,4},{7,5},{8,10},{9,11},{10,... | collective-permute-start | bytes 786440 | tf_op jit(solution)/shard_map/ppermute | solution.py:198
  16.9 3.1 %copy-done = bf16[2,128,14336]{2,1,0:T(8,128)(2,1)S(1)} copy-done((bf16[2,128,14336]{2,1,0:T(8,128)(2,1)S(1)}, bf16[2,128,14336]{2,1,0:T(8,128)(2,1)}, u32[]{:S(2)}) %copy-start) | copy-done | bytes 7340056
  20.0 1.6 %copy-done.1 = bf16[2,128,4096]{2,1,0:T(8,128)(2,1)S(1)} copy-done((bf16[2,128,4096]{2,1,0:T(8,128)(2,1)S(1)}, bf16[2,128,4096]{2,1,0:T(8,128)(2,1)}, u32[]{:S(2)}) %copy-start.1) | copy-done | bytes 2097176
  21.6 1.5 %copy-done.2 = bf16[14336,64]{0,1:T(8,128)(2,1)S(1)} copy-done((bf16[14336,64]{0,1:T(8,128)(2,1)S(1)}, bf16[14336,64]{0,1:T(8,128)(2,1)}, u32[]{:S(2)}) %copy-start.2) | copy-done | bytes 1835032
  23.1 1.0 %copy-done.3 = bf16[4096,64]{0,1:T(8,128)(2,1)S(1)} copy-done((bf16[4096,64]{0,1:T(8,128)(2,1)S(1)}, bf16[4096,64]{0,1:T(8,128)(2,1)}, u32[]{:S(2)}) %copy-start.3) | copy-done | bytes 524312
  24.2 0.7 %copy-done.9 = s32[128]{0:T(128)S(1)} copy-done((s32[128]{0:T(128)S(1)}, s32[128]{0:T(128)}, u32[]{:S(2)}) %copy-start.9) | copy-done | bytes 536
  24.8 6.8 %project.1 = (f32[128,128]{1,0:T(8,128)S(1)}, f32[136,128]{1,0:T(8,128)S(1)}) custom-call(bf16[2,128,14336]{2,1,0:T(8,128)(2,1)S(1)} %copy-done, bf16[2,128,4096]{2,1,0:T(8,128)(2,1)S(1)} %copy-done.1, s32[1,128]{1,0:T(1,128)S(1)} %bitcast.9, bf16[64,14336]{1,0:T(8,128)(2,1)S(1)} %bitcast.7, bf16[64,4096]{1,0:T(8,128)(2,1)S(1)} %bitcast.8), custom_call_target="tpu_custom_call" | custom-call | tf_op jit(solution)/shard_map/project/pallas_call | solution.py:61
  31.6 0.6 copy-done.6
  32.2 1.3 %collective-permute-done.other = f32[136,128]{1,0:T(8,128)S(1)} collective-permute-done((f32[136,128]{1,0:T(8,128)S(1)}, f32[136,128]{1,0:T(8,128)S(1)}, u32[]{:S(2)}, u32[]{:S(2)}) %collective-permute-start) | collective-permute-done | bytes 69664 | tf_op jit(solution)/shard_map/ppermute | solution.py:198
  33.5 0.6 copy-done.4
  34.1 1.9 %factor.1 = f32[64,128]{1,0:T(8,128)} custom-call(f32[128,128]{1,0:T(8,128)} %copy-done.6, f32[136,128]{1,0:T(8,128)} %copy-done.4), custom_call_target="tpu_custom_call" | custom-call | tf_op jit(solution)/shard_map/factor/pallas_call | solution.py:207
  36.0 2.6 %collective-permute-start.1 = (f32[64,128]{1,0:T(8,128)}, f32[64,128]{1,0:T(8,128)S(1)}, u32[]{:S(2)}, u32[]{:S(2)}) collective-permute-start(f32[64,128]{1,0:T(8,128)} %factor.1), channel_id=1, source_target_pairs={{0,8},{1,9},{2,10},{3,11},{4,12},{5,13},{6,14},{7,15},{8,0},{9,1},... | collective-permute-start | bytes 98312 | tf_op jit(solution)/shard_map/ppermute | solution.py:198
  38.6 2.4 %collective-permute-done.1 = f32[64,128]{1,0:T(8,128)S(1)} collective-permute-done((f32[64,128]{1,0:T(8,128)}, f32[64,128]{1,0:T(8,128)S(1)}, u32[]{:S(2)}, u32[]{:S(2)}) %collective-permute-start.1) | collective-permute-done | bytes 32800 | tf_op jit(solution)/shard_map/ppermute | solution.py:198
  41.0 0.8 %add.12 = f32[64,128]{1,0:T(8,128)S(1)} add(f32[64,128]{1,0:T(8,128)} %factor.1, f32[64,128]{1,0:T(8,128)S(1)} %collective-permute-done.1) | non-fusion elementwise | flops 8192 | bytes 98304 | tf_op jit(solution)/shard_map/add | solution.py:218
  41.8 1.5 %collective-permute-start.2 = (f32[64,128]{1,0:T(8,128)S(1)}, f32[64,128]{1,0:T(8,128)S(1)}, u32[]{:S(2)}, u32[]{:S(2)}) collective-permute-start(f32[64,128]{1,0:T(8,128)S(1)} %add.12), channel_id=1, source_target_pairs={{0,4},{1,5},{2,6},{3,7},{4,0},{5,1},{6,2},{7,3},{8,12},{9,13},{10,... | collective-permute-start | bytes 98312 | tf_op jit(solution)/shard_map/ppermute | solution.py:198
  43.2 2.5 %collective-permute-done.2 = f32[64,128]{1,0:T(8,128)S(1)} collective-permute-done((f32[64,128]{1,0:T(8,128)S(1)}, f32[64,128]{1,0:T(8,128)S(1)}, u32[]{:S(2)}, u32[]{:S(2)}) %collective-permute-start.2) | collective-permute-done | bytes 32800 | tf_op jit(solution)/shard_map/ppermute | solution.py:198
  46.0 3.6 %collective-permute-done.3 = f32[64,128]{1,0:T(8,128)S(1)} collective-permute-done((f32[64,128]{1,0:T(8,128)S(1)}, f32[64,128]{1,0:T(8,128)S(1)}, u32[]{:S(2)}, u32[]{:S(2)}) %collective-permute-start.3) | collective-permute-done | bytes 32800 | tf_op jit(solution)/shard_map/ppermute | solution.py:198
  49.6 0.6 add.14.g
  50.2 7.3 %inverse.1.inv = f32[64,128]{1,0:T(8,128)} custom-call(f32[64,128]{1,0:T(8,128)} %add.14.g), custom_call_target="tpu_custom_call" | custom-call | tf_op jit(solution)/shard_map/inverse/pallas_call | solution.py:220
  57.7 0.9 %copy-done.5 = f32[136,128]{1,0:T(8,128)S(1)} copy-done((f32[136,128]{1,0:T(8,128)S(1)}, f32[136,128]{1,0:T(8,128)}, u32[]{:S(2)}) %copy-start.5) | copy-done | bytes 69656
  58.6 0.8 %copy-done.7 = f32[128,128]{1,0:T(8,128)S(1)} copy-done((f32[128,128]{1,0:T(8,128)S(1)}, f32[128,128]{1,0:T(8,128)}, u32[]{:S(2)}) %copy-start.7) | copy-done | bytes 65560
  59.4 0.8 %copy-done.8 = f32[64,128]{1,0:T(8,128)S(1)} copy-done((f32[64,128]{1,0:T(8,128)S(1)}, f32[64,128]{1,0:T(8,128)}, u32[]{:S(2)}) %copy-start.8) | copy-done | bytes 32792
  60.1 1.8 %score.1 = (f32[16,64]{1,0:T(8,128)S(1)}, f32[16,64]{1,0:T(8,128)S(1)}) custom-call(f32[64,128]{1,0:T(8,128)S(1)} %copy-done.8, f32[128,128]{1,0:T(8,128)S(1)} %copy-done.7, f32[136,128]{1,0:T(8,128)S(1)} %copy-done.5, s32[1,128]{1,0:T(1,128)S(1)} %bitcast.10, bf16[64,4096]{1,0:T(8,128)(2,1)S(1)} %concatenate.18.queries, f32[2]{0:T(128)S(1)} %copy-done.11), custom_call_target="tpu_custom_call" | custom-call | tf_op jit(solution)/shard_map/score/pallas_call | solution.py:227
  61.9 1.2 %collective-permute-done.8 = f32[16,64]{1,0:T(8,128)S(1)} collective-permute-done((f32[16,64]{1,0:T(8,128)S(1)}, f32[16,64]{1,0:T(8,128)S(1)}, u32[]{:S(2)}, u32[]{:S(2)}) %collective-permute-start.8) | collective-permute-done | bytes 4128 | tf_op jit(solution)/shard_map/ppermute | solution.py:198
  63.1 0.6 add.15
  (23 shorter events, 0.7 us)
Async XLA Ops:
  0.8 1.4 %collective-permute-start.4 = (bf16[4,4096]{1,0:T(4,128)(2,1)S(1)}, bf16[4,4096]{1,0:T(4,128)(2,1)S(1)}, u32[]{:S(2)}, u32[]{:S(2)}) collective-permute-start(bf16[4,4096]{1,0:T(4,128)(2,1)S(1)} %get-tuple-element.13), channel_id=1, source_target_pairs={{0,1},{1,0},{2,3},{3,2},{4,5},{5,4},{6,7},{7,6},{8,9},{9,8},{10,11... | collective-permute-start | bytes 98312 | tf_op jit(solution)/shard_map/ppermute | solution.py:198
  2.2 7.8 %collective-permute-start.5 = (bf16[8,4096]{1,0:T(8,128)(2,1)S(1)}, bf16[8,4096]{1,0:T(8,128)(2,1)S(1)}, u32[]{:S(2)}, u32[]{:S(2)}) collective-permute-start(bf16[8,4096]{1,0:T(8,128)(2,1)S(1)} %pad_maximum_fusion.2), channel_id=1, source_target_pairs={{0,8},{1,9},{2,10},{3,11},{4,12},{5,13},{6,14},{7,15},{8,0},{9,1},... | collective-permute-start | bytes 196616 | tf_op jit(solution)/shard_map/ppermute | solution.py:198
  10.1 5.0 %collective-permute-start.6 = (bf16[16,4096]{1,0:T(8,128)(2,1)S(1)}, bf16[16,4096]{1,0:T(8,128)(2,1)S(1)}, u32[]{:S(2)}, u32[]{:S(2)}) collective-permute-start(bf16[16,4096]{1,0:T(8,128)(2,1)S(1)} %pad_maximum_fusion.1), channel_id=1, source_target_pairs={{0,4},{1,5},{2,6},{3,7},{4,0},{5,1},{6,2},{7,3},{8,12},{9,13},{10,... | collective-permute-start | bytes 393224 | tf_op jit(solution)/shard_map/ppermute | solution.py:198
  15.2 42.3 %collective-permute-start.7 = (bf16[32,4096]{1,0:T(8,128)(2,1)S(1)}, bf16[32,4096]{1,0:T(8,128)(2,1)S(1)}, u32[]{:S(2)}, u32[]{:S(2)}) collective-permute-start(bf16[32,4096]{1,0:T(8,128)(2,1)S(1)} %pad_maximum_fusion), channel_id=1, source_target_pairs={{0,2},{1,3},{2,0},{3,1},{4,6},{5,7},{6,4},{7,5},{8,10},{9,11},{10,... | collective-permute-start | bytes 786440 | tf_op jit(solution)/shard_map/ppermute | solution.py:198
  16.9 3.1 %copy-start = (bf16[2,128,14336]{2,1,0:T(8,128)(2,1)S(1)}, bf16[2,128,14336]{2,1,0:T(8,128)(2,1)}, u32[]{:S(2)}) copy-start(bf16[2,128,14336]{2,1,0:T(8,128)(2,1)} %act.1) | copy-start | bytes 22020100
  20.0 1.6 %copy-start.1 = (bf16[2,128,4096]{2,1,0:T(8,128)(2,1)S(1)}, bf16[2,128,4096]{2,1,0:T(8,128)(2,1)}, u32[]{:S(2)}) copy-start(bf16[2,128,4096]{2,1,0:T(8,128)(2,1)} %grad.1) | copy-start | bytes 6291460
  21.6 1.5 %copy-start.2 = (bf16[14336,64]{0,1:T(8,128)(2,1)S(1)}, bf16[14336,64]{0,1:T(8,128)(2,1)}, u32[]{:S(2)}) copy-start(bf16[14336,64]{0,1:T(8,128)(2,1)} %param.10) | copy-start | bytes 5505028
  23.1 1.0 %copy-start.3 = (bf16[4096,64]{0,1:T(8,128)(2,1)S(1)}, bf16[4096,64]{0,1:T(8,128)(2,1)}, u32[]{:S(2)}) copy-start(bf16[4096,64]{0,1:T(8,128)(2,1)} %param.11) | copy-start | bytes 1572868
  24.2 0.7 %copy-start.9 = (s32[128]{0:T(128)S(1)}, s32[128]{0:T(128)}, u32[]{:S(2)}) copy-start(s32[128]{0:T(128)} %param.9) | copy-start | bytes 1540
  24.8 32.8 %copy-start.10 = (s32[128]{0:T(128)S(1)}, s32[128]{0:T(128)}, u32[]{:S(2)}) copy-start(s32[128]{0:T(128)} %param.9) | copy-start | bytes 1540
  24.8 32.8 %copy-start.11 = (f32[2]{0:T(128)S(1)}, f32[2]{0:T(128)}, u32[]{:S(2)}) copy-start(f32[2]{0:T(128)} %weight.1) | copy-start | bytes 28
  31.6 0.6 copy-start.6
  32.2 1.3 %collective-permute-start = (f32[136,128]{1,0:T(8,128)S(1)}, f32[136,128]{1,0:T(8,128)S(1)}, u32[]{:S(2)}, u32[]{:S(2)}) collective-permute-start(f32[136,128]{1,0:T(8,128)S(1)} %get-tuple-element.10), channel_id=1, source_target_pairs={{0,1},{1,0},{2,3},{3,2},{4,5},{5,4},{6,7},{7,6},{8,9},{9,8},{10,11... | collective-permute-start | bytes 208904 | tf_op jit(solution)/shard_map/ppermute | solution.py:198
  33.5 0.6 copy-start.4
  36.0 5.0 %collective-permute-start.1 = (f32[64,128]{1,0:T(8,128)}, f32[64,128]{1,0:T(8,128)S(1)}, u32[]{:S(2)}, u32[]{:S(2)}) collective-permute-start(f32[64,128]{1,0:T(8,128)} %factor.1), channel_id=1, source_target_pairs={{0,8},{1,9},{2,10},{3,11},{4,12},{5,13},{6,14},{7,15},{8,0},{9,1},... | collective-permute-start | bytes 98312 | tf_op jit(solution)/shard_map/ppermute | solution.py:198
  41.8 3.9 %collective-permute-start.2 = (f32[64,128]{1,0:T(8,128)S(1)}, f32[64,128]{1,0:T(8,128)S(1)}, u32[]{:S(2)}, u32[]{:S(2)}) collective-permute-start(f32[64,128]{1,0:T(8,128)S(1)} %add.12), channel_id=1, source_target_pairs={{0,4},{1,5},{2,6},{3,7},{4,0},{5,1},{6,2},{7,3},{8,12},{9,13},{10,... | collective-permute-start | bytes 98312 | tf_op jit(solution)/shard_map/ppermute | solution.py:198
  45.7 3.9 %collective-permute-start.3 = (f32[64,128]{1,0:T(8,128)S(1)}, f32[64,128]{1,0:T(8,128)S(1)}, u32[]{:S(2)}, u32[]{:S(2)}) collective-permute-start(f32[64,128]{1,0:T(8,128)S(1)} %add.13), channel_id=1, source_target_pairs={{0,2},{1,3},{2,0},{3,1},{4,6},{5,7},{6,4},{7,5},{8,10},{9,11},{10,... | collective-permute-start | bytes 98312 | tf_op jit(solution)/shard_map/ppermute | solution.py:198
  57.7 0.9 %copy-start.5 = (f32[136,128]{1,0:T(8,128)S(1)}, f32[136,128]{1,0:T(8,128)}, u32[]{:S(2)}) copy-start(f32[136,128]{1,0:T(8,128)} %copy-done.4) | copy-start | bytes 208900
  58.5 0.8 %copy-start.7 = (f32[128,128]{1,0:T(8,128)S(1)}, f32[128,128]{1,0:T(8,128)}, u32[]{:S(2)}) copy-start(f32[128,128]{1,0:T(8,128)} %copy-done.6) | copy-start | bytes 196612
  59.4 0.8 %copy-start.8 = (f32[64,128]{1,0:T(8,128)S(1)}, f32[64,128]{1,0:T(8,128)}, u32[]{:S(2)}) copy-start(f32[64,128]{1,0:T(8,128)} %inverse.1.inv) | copy-start | bytes 98308
  61.9 1.2 %collective-permute-start.8 = (f32[16,64]{1,0:T(8,128)S(1)}, f32[16,64]{1,0:T(8,128)S(1)}, u32[]{:S(2)}, u32[]{:S(2)}) collective-permute-start(f32[16,64]{1,0:T(8,128)S(1)} %get-tuple-element.12), channel_id=1, source_target_pairs={{0,1},{1,0},{2,3},{3,2},{4,5},{5,4},{6,7},{7,6},{8,9},{9,8},{10,11... | collective-permute-start | bytes 12296 | tf_op jit(solution)/shard_map/ppermute | solution.py:198

commit v2 on v1

--- a/solution.py
+++ b/solution.py
@@ -12,7 +12,7 @@
 F32 = jnp.float32
 BF16 = jnp.bfloat16
 VMEM = pl.BlockSpec(memory_space=pltpu.VMEM)
-ANY = pl.BlockSpec(memory_space=pl.ANY)
+HBM = pl.BlockSpec(memory_space=pltpu.HBM)
 
 
 def nt(x, y, precision=None):
@@ -21,67 +21,84 @@
     )
 
 
-def project_kernel(chunks, act, grad, ids, pin, pout, keep, send, act_v, grad_v, pin_v, pout_v, sems):
+def project_kernel(
+    chunks, act, grad, ids, pin, pout, query, weight,
+    keep, send, q_keep, q_send,
+    act_v, grad_v, ids_v, pin_v, pout_v, query_v, weight_v, sems,
+):
     ckpts, rows, depth = act.shape
     side = pin.shape[0]
     step = depth // chunks
     copies = [
         pltpu.make_async_copy(pout, pout_v, sems.at[0]),
         pltpu.make_async_copy(grad, grad_v, sems.at[1]),
+        pltpu.make_async_copy(query, query_v, sems.at[2]),
+        pltpu.make_async_copy(ids, ids_v, sems.at[3]),
+        pltpu.make_async_copy(weight, weight_v, sems.at[4]),
     ]
     for k in range(chunks):
         span = pl.ds(k * step, step)
-        copies.append(pltpu.make_async_copy(pin.at[:, span], pin_v.at[:, span], sems.at[2 + 2 * k]))
+        copies.append(pltpu.make_async_copy(pin.at[:, span], pin_v.at[:, span], sems.at[5 + 2 * k]))
         copies.append(
-            pltpu.make_async_copy(act.at[:, :, span], act_v.at[:, :, span], sems.at[3 + 2 * k])
+            pltpu.make_async_copy(act.at[:, :, span], act_v.at[:, :, span], sems.at[6 + 2 * k])
         )
     for copy in copies:
         copy.start()
-    copies[0].wait()
-    copies[1].wait()
+    for copy in copies[:5]:
+        copy.wait()
+    odd = lax.rem(lax.axis_index("tok"), 2)
+    tail = jnp.broadcast_to(ids_v[...].astype(F32), (8, rows))
+    keep[rows : rows + 8, :] = tail
+    send[rows : rows + 8, :] = tail
+    keep[rows + 8 :, :] = jnp.full((8, 2 * side), weight_v[odd] / side, F32)
+    q_keep[...] = jnp.where(odd == 0, query_v[0], query_v[1])
+    q_send[...] = jnp.where(odd == 0, query_v[1], query_v[0])
     s = nt(grad_v[...].reshape(ckpts * rows, -1), pout_v[...])
     a = jnp.zeros((ckpts * rows, side), F32)
     for k in range(chunks):
-        copies[2 + 2 * k].wait()
-        copies[3 + 2 * k].wait()
+        copies[5 + 2 * k].wait()
+        copies[6 + 2 * k].wait()
         span = slice(k * step, (k + 1) * step)
         a = a + nt(act_v[:, :, span].reshape(ckpts * rows, step), pin_v[:, span])
     both = jnp.concatenate([a, s], axis=1)
-    odd = lax.rem(lax.axis_index("tok"), 2)
     first, second = both[:rows], both[rows:]
-    keep[...] = jnp.where(odd == 0, first, second)
+    keep[0:rows, :] = jnp.where(odd == 0, first, second)
     send[0:rows, :] = jnp.where(odd == 0, second, first)
-    send[rows : rows + 8, :] = jnp.broadcast_to(ids[...].astype(F32), (8, rows))
-
-
-def project(act, grad, ids, pin, pout):
+
+
+def project(act, grad, ids, pin, pout, query, weight):
     ckpts, rows, depth = act.shape
     side, width = pout.shape
     chunks = 8
     return pl.pallas_call(
         functools.partial(project_kernel, chunks),
         out_shape=(
-            jax.ShapeDtypeStruct((rows, 2 * side), F32),
+            jax.ShapeDtypeStruct((rows + 16, 2 * side), F32),
             jax.ShapeDtypeStruct((rows + 8, 2 * side), F32),
+            jax.ShapeDtypeStruct(query.shape[1:], BF16),
+            jax.ShapeDtypeStruct(query.shape[1:], BF16),
         ),
-        in_specs=[ANY, ANY, VMEM, ANY, ANY],
-        out_specs=(VMEM, VMEM),
+        in_specs=[HBM] * 7,
+        out_specs=(VMEM,) * 4,
         scratch_shapes=[
             pltpu.VMEM((ckpts, rows, depth), BF16),
             pltpu.VMEM((ckpts, rows, width), BF16),
+            pltpu.VMEM((1, rows), jnp.int32),
             pltpu.VMEM((side, depth), BF16),
             pltpu.VMEM((side, width), BF16),
-            pltpu.SemaphoreType.DMA((2 + 2 * chunks,)),
+            pltpu.VMEM(query.shape, BF16),
+            pltpu.SMEM(weight.shape, F32),
+            pltpu.SemaphoreType.DMA((5 + 2 * chunks,)),
         ],
-        compiler_params=pltpu.CompilerParams(vmem_limit_bytes=40 * 2**20),
+        compiler_params=pltpu.CompilerParams(vmem_limit_bytes=63 * 2**20),
         name="project",
-    )(act, grad, ids, pin, pout)
+    )(act, grad, ids, pin, pout, query, weight)
 
 
 def factor_kernel(total, mine, other, out):
-    rows, lanes = mine.shape
+    rows, lanes = other.shape[0] - 8, other.shape[1]
     side = lanes // 2
-    x = jnp.concatenate([mine[...], other[0:rows, :]], axis=0)
+    x = jnp.concatenate([mine[0:rows, :], other[0:rows, :]], axis=0)
     g = lax.dot_general(
         x, x, (((0,), (0,)), ((), ())), precision=HIGH, preferred_element_type=F32
     )
@@ -117,12 +134,12 @@
     return hi, (x - hi.astype(F32)).astype(BF16)
 
 
-def score_kernel(q_rows, masks, inv, mine, other, ids, queries, weight, keep, send):
-    rows, lanes = mine.shape
+def score_kernel(q_rows, masks, inv, mine, other, queries, keep, send):
+    rows, lanes = other.shape[0] - 8, other.shape[1]
     side = lanes // 2
     ckpt = lax.rem(lax.axis_index("tok"), 2)
     me = lax.axis_index("tok")
-    x = jnp.concatenate([mine[...], other[0:rows, :]], axis=0)
+    x = jnp.concatenate([mine[0:rows, :], other[0:rows, :]], axis=0)
     lane = lax.broadcasted_iota(jnp.int32, (side, lanes), 1)
     left = lane < side
     p = inv[...]
@@ -139,7 +156,7 @@
     s_hi, s_lo = split(st)
     s_hi, s_lo = s_hi.astype(F32), s_lo.astype(F32)
     example = lax.broadcasted_iota(jnp.int32, (EX_DEV, rows), 0)
-    own_ids = ids[...] - me * EX_DEV
+    own_ids = mine[rows : rows + 1, :].astype(jnp.int32) - me * EX_DEV
     near = me + 1 - 2 * ckpt
     far_ids = other[rows : rows + 1, :].astype(jnp.int32) - near * EX_DEV
     parts = []
@@ -181,7 +198,7 @@
         block = block ^ ((src >> (shift + bit)) & 1) * mask
     order = (block * q_rows + (src & (q_rows - 1)) == dst).astype(F32)
     scores = jnp.dot(inner, order, precision=HIGH, preferred_element_type=F32)
-    scores = scores * (weight[ckpt] / side)
+    scores = scores * mine[rows + 8 : rows + 9, 0:1]
     keep[...] = scores[:EX_DEV]
     send[...] = scores[EX_DEV:]
 
@@ -198,10 +215,9 @@
         return lax.ppermute(x, "tok", [(i, i ^ mask) for i in range(devices)])
 
     ids = example_ids.reshape(1, rows)
-    even = lax.rem(me, 2) == 0
-    q_keep = jnp.where(even, query_sketch[0], query_sketch[1])
-    q_send = jnp.where(even, query_sketch[1], query_sketch[0])
-    mine, send = project(inputs_act, out_grads, ids, proj_in.T, proj_out.T)
+    mine, send, q_keep, q_send = project(
+        inputs_act, out_grads, ids, proj_in.T, proj_out.T, query_sketch, ckpt_weight
+    )
     other = swap(send, 1)
     queries = jnp.concatenate([q_keep, swap(q_send, 1)], axis=0)
     g = pl.pallas_call(
@@ -209,12 +225,14 @@
         out_shape=jax.ShapeDtypeStruct((side, 2 * side), F32),
         in_specs=[VMEM, VMEM],
         out_specs=VMEM,
+        compiler_params=pltpu.CompilerParams(vmem_limit_bytes=4 * 2**20),
         name="factor",
     )(mine, other)
     masks = [1]
     while devices >> len(masks) > 1:
         masks.append(devices >> len(masks))
     for mask in masks[1:]:
+        queries, _ = lax.optimization_barrier((queries, g))
         g = g + swap(g, mask)
         queries = jnp.concatenate([queries, swap(queries, mask)], axis=0)
     inv = pl.pallas_call(
@@ -222,6 +240,7 @@
         out_shape=jax.ShapeDtypeStruct((side, 2 * side), F32),
         in_specs=[VMEM],
         out_specs=VMEM,
+        compiler_params=pltpu.CompilerParams(vmem_limit_bytes=4 * 2**20),
         name="inverse",
     )(g)
     keep, send = pl.pallas_call(
@@ -230,11 +249,11 @@
             jax.ShapeDtypeStruct((EX_DEV, q_rows * devices), F32),
             jax.ShapeDtypeStruct((EX_DEV, q_rows * devices), F32),
         ),
-        in_specs=[VMEM] * 5 + [pl.BlockSpec(memory_space=pltpu.SMEM)],
+        in_specs=[VMEM] * 4,
         out_specs=(VMEM, VMEM),
-        compiler_params=pltpu.CompilerParams(vmem_limit_bytes=40 * 2**20),
+        compiler_params=pltpu.CompilerParams(vmem_limit_bytes=16 * 2**20),
         name="score",
-    )(inv, mine, other, ids, queries, ckpt_weight)
+    )(inv, mine, other, queries)
     return keep + swap(send, 1)
 
 

time: 64.4 us -> 43.5 us (0.68)
  the two profiles are of different devices: /device:TPU:0 before, /device:TPU:17 now
where the time goes in v2:
time: 43.5 us; the launch traced here: 43.2 us
  Pallas kernels  15.4 us (35%)
  waiting for transfers between devices  14.5 us (33%)
  starting transfers between devices  10.8 us (25%)
  other arithmetic  1.48 us (3%)
  local copies, waits for them, and re-layouts  0.88 us (2%)
    ppermute x9, waiting for transfers between devices, swap(): return lax.ppermute(x, 'tok', [(i, i ^ mask) for i in range(devices)])  14.5 us
    ppermute x9, starting transfers between devices, swap(): return lax.ppermute(x, 'tok', [(i, i ^ mask) for i in range(devices)])  10.8 us
    pallas_call x1, Pallas kernels, project(): pl.pallas_call(functools.partial(project_kernel, chunks), out_shape=(jax....  7.99 us
    pallas_call x1, Pallas kernels, local(): pl.pallas_call(inverse_kernel, out_shape=jax.ShapeDtypeStruct((side, 2 *...  5.88 us
    pallas_call x1, Pallas kernels, local(): pl.pallas_call(functools.partial(score_kernel, q_rows, tuple(masks)), out...  1.24 us
    unnamed x4, local copies, waits for them, and re-layouts  0.88 us
  transfers between devices with their start and end apart: 9, of which 5 were waited for; matrix products, arithmetic and copies ran while one was open for 2% of the time, Pallas kernels for 14%

profile of v2, /device:TPU:17, one launch (start us, length us, event | category | flops | bytes accessed | tf_op | source)
XLA Modules:
  0.0 43.2 jit_solution(12385958710933842681)
XLA Ops:
  0.0 8.0 %project.1 = (f32[144,128]{1,0:T(8,128)}, f32[136,128]{1,0:T(8,128)}, bf16[4,4096]{1,0:T(4,128)(2,1)}, bf16[4,4096]{1,0:T(4,128)(2,1)}) custom-call(bf16[2,128,14336]{2,1,0:T(8,128)(2,1)} %act.1, bf16[2,128,4096]{2,1,0:T(8,128)(2,1)} %grad.1, s32[1,128]{1,0:T(1,128)} %bitcast.5, bf16[64,14336]{1,0:T(8,128)(2,1)} %bitcast.3, bf16[64,4096]{1,0:T(8,128)(2,1)} %bitcast.4, ...), custom_call_target="tpu_custom_call" | custom-call | tf_op jit(solution)/shard_map/project/pallas_call | solution.py:73
  8.0 0.0 copy-start.1
  8.0 0.7 %collective-permute-start.4 = (bf16[4,4096]{1,0:T(4,128)(2,1)}, bf16[4,4096]{1,0:T(4,128)(2,1)S(1)}, u32[]{:S(2)}, u32[]{:S(2)}) collective-permute-start(bf16[4,4096]{1,0:T(4,128)(2,1)} %get-tuple-element.17), channel_id=1, source_target_pairs={{0,1},{1,0},{2,3},{3,2},{4,5},{5,4},{6,7},{7,6},{8,9},{9,8},{10,11... | collective-permute-start | bytes 98312 | tf_op jit(solution)/shard_map/ppermute | solution.py:215
  8.8 0.1 collective-permute-start
  8.8 1.0 %collective-permute-done.4 = bf16[4,4096]{1,0:T(4,128)(2,1)S(1)} collective-permute-done((bf16[4,4096]{1,0:T(4,128)(2,1)}, bf16[4,4096]{1,0:T(4,128)(2,1)S(1)}, u32[]{:S(2)}, u32[]{:S(2)}) %collective-permute-start.4) | collective-permute-done | bytes 32800 | tf_op jit(solution)/shard_map/ppermute | solution.py:215
  9.8 0.8 %pad_maximum_fusion.3 = bf16[8,4096]{1,0:T(8,128)(2,1)S(1)} fusion(bf16[4,4096]{1,0:T(4,128)(2,1)S(1)} %collective-permute-done.4, bf16[4,4096]{1,0:T(4,128)(2,1)} %get-tuple-element.16), kind=kLoop, calls=%fused_computation.3 | loop fusion | flops 131072 | bytes 131072 | tf_op jit(solution)/shard_map/concatenate | solution.py:222
  10.6 0.0 collective-permute-done.other
  10.6 0.0 copy-start
  10.6 0.9 %copy-done = f32[144,128]{1,0:T(8,128)S(1)} copy-done((f32[144,128]{1,0:T(8,128)S(1)}, f32[144,128]{1,0:T(8,128)}, u32[]{:S(2)}) %copy-start) | copy-done | bytes 73752
  11.5 0.3 factor.1
  11.8 0.1 collective-permute-start.5
  11.9 2.4 %collective-permute-start.1 = (f32[64,128]{1,0:T(8,128)S(1)}, f32[64,128]{1,0:T(8,128)S(1)}, u32[]{:S(2)}, u32[]{:S(2)}) collective-permute-start(f32[64,128]{1,0:T(8,128)S(1)} %factor.1), channel_id=1, source_target_pairs={{0,8},{1,9},{2,10},{3,11},{4,12},{5,13},{6,14},{7,15},{8,0},{9,1},... | collective-permute-start | bytes 98312 | tf_op jit(solution)/shard_map/ppermute | solution.py:215
  14.3 2.6 %collective-permute-done.1 = f32[64,128]{1,0:T(8,128)S(1)} collective-permute-done((f32[64,128]{1,0:T(8,128)S(1)}, f32[64,128]{1,0:T(8,128)S(1)}, u32[]{:S(2)}, u32[]{:S(2)}) %collective-permute-start.1) | collective-permute-done | bytes 32800 | tf_op jit(solution)/shard_map/ppermute | solution.py:215
  16.8 0.0 collective-permute-done.5
  16.9 4.1 %collective-permute-start.6 = (bf16[16,4096]{1,0:T(8,128)(2,1)S(1)}, bf16[16,4096]{1,0:T(8,128)(2,1)S(1)}, u32[]{:S(2)}, u32[]{:S(2)}) collective-permute-start(bf16[16,4096]{1,0:T(8,128)(2,1)S(1)} %pad_maximum_fusion.2), channel_id=1, source_target_pairs={{0,4},{1,5},{2,6},{3,7},{4,0},{5,1},{6,2},{7,3},{8,12},{9,13},{10,... | collective-permute-start | bytes 393224 | tf_op jit(solution)/shard_map/ppermute | solution.py:215
  20.9 0.1 collective-permute-start.2
  21.0 4.1 %collective-permute-done.2 = f32[64,128]{1,0:T(8,128)S(1)} collective-permute-done((f32[64,128]{1,0:T(8,128)S(1)}, f32[64,128]{1,0:T(8,128)S(1)}, u32[]{:S(2)}, u32[]{:S(2)}) %collective-permute-start.2) | collective-permute-done | bytes 32800 | tf_op jit(solution)/shard_map/ppermute | solution.py:215
  25.1 0.0 collective-permute-done.6
  25.1 1.3 %collective-permute-start.7 = (bf16[32,4096]{1,0:T(8,128)(2,1)S(1)}, bf16[32,4096]{1,0:T(8,128)(2,1)S(1)}, u32[]{:S(2)}, u32[]{:S(2)}) collective-permute-start(bf16[32,4096]{1,0:T(8,128)(2,1)S(1)} %pad_maximum_fusion.1), channel_id=1, source_target_pairs={{0,2},{1,3},{2,0},{3,1},{4,6},{5,7},{6,4},{7,5},{8,10},{9,11},{10,... | collective-permute-start | bytes 786440 | tf_op jit(solution)/shard_map/ppermute | solution.py:215
  26.4 0.2 collective-permute-start.3
  26.7 6.0 %collective-permute-done.3 = f32[64,128]{1,0:T(8,128)S(1)} collective-permute-done((f32[64,128]{1,0:T(8,128)S(1)}, f32[64,128]{1,0:T(8,128)S(1)}, u32[]{:S(2)}, u32[]{:S(2)}) %collective-permute-start.3) | collective-permute-done | bytes 32800 | tf_op jit(solution)/shard_map/ppermute | solution.py:215
  32.7 5.9 %inverse.1.inv = f32[64,128]{1,0:T(8,128)S(1)} custom-call(f32[64,128]{1,0:T(8,128)S(1)} %add.14.g), custom_call_target="tpu_custom_call" | custom-call | tf_op jit(solution)/shard_map/inverse/pallas_call | solution.py:238
  38.6 0.0 collective-permute-done.7
  38.6 0.0 copy-done.1
  38.7 1.2 %score.1 = (f32[16,64]{1,0:T(8,128)S(1)}, f32[16,64]{1,0:T(8,128)S(1)}) custom-call(f32[64,128]{1,0:T(8,128)S(1)} %inverse.1.inv, f32[144,128]{1,0:T(8,128)S(1)} %copy-done.1, f32[136,128]{1,0:T(8,128)S(1)} %collective-permute-done.other, bf16[64,4096]{1,0:T(8,128)(2,1)S(1)} %pad_maximum_fusion.queries), custom_call_target="tpu_custom_call" | custom-call | tf_op jit(solution)/shard_map/score/pallas_call | solution.py:246
  39.9 1.9 %collective-permute-start.8 = (f32[16,64]{1,0:T(8,128)S(1)}, f32[16,64]{1,0:T(8,128)S(1)}, u32[]{:S(2)}, u32[]{:S(2)}) collective-permute-start(f32[16,64]{1,0:T(8,128)S(1)} %get-tuple-element.22), channel_id=1, source_target_pairs={{0,1},{1,0},{2,3},{3,2},{4,5},{5,4},{6,7},{7,6},{8,9},{9,8},{10,11... | collective-permute-start | bytes 12296 | tf_op jit(solution)/shard_map/ppermute | solution.py:215
  41.8 0.8 %collective-permute-done.8 = f32[16,64]{1,0:T(8,128)S(1)} collective-permute-done((f32[16,64]{1,0:T(8,128)S(1)}, f32[16,64]{1,0:T(8,128)S(1)}, u32[]{:S(2)}, u32[]{:S(2)}) %collective-permute-start.8) | collective-permute-done | bytes 4128 | tf_op jit(solution)/shard_map/ppermute | solution.py:215
  42.6 0.6 %add.15 = f32[16,64]{1,0:T(8,128)} add(f32[16,64]{1,0:T(8,128)S(1)} %get-tuple-element.21, f32[16,64]{1,0:T(8,128)S(1)} %collective-permute-done.8) | non-fusion elementwise | flops 1024 | bytes 12288 | tf_op jit(solution)/shard_map/add | solution.py:257
  (6 shorter events, 0.1 us)
Async XLA Ops:
  8.0 30.6 %copy-start.1 = (f32[144,128]{1,0:T(8,128)S(1)}, f32[144,128]{1,0:T(8,128)}, u32[]{:S(2)}) copy-start(f32[144,128]{1,0:T(8,128)} %get-tuple-element.14.mine) | copy-start | bytes 221188
  8.0 1.8 %collective-permute-start.4 = (bf16[4,4096]{1,0:T(4,128)(2,1)}, bf16[4,4096]{1,0:T(4,128)(2,1)S(1)}, u32[]{:S(2)}, u32[]{:S(2)}) collective-permute-start(bf16[4,4096]{1,0:T(4,128)(2,1)} %get-tuple-element.17), channel_id=1, source_target_pairs={{0,1},{1,0},{2,3},{3,2},{4,5},{5,4},{6,7},{7,6},{8,9},{9,8},{10,11... | collective-permute-start | bytes 98312 | tf_op jit(solution)/shard_map/ppermute | solution.py:215
  8.8 1.9 %collective-permute-start = (f32[136,128]{1,0:T(8,128)}, f32[136,128]{1,0:T(8,128)S(1)}, u32[]{:S(2)}, u32[]{:S(2)}) collective-permute-start(f32[136,128]{1,0:T(8,128)} %get-tuple-element.15), channel_id=1, source_target_pairs={{0,1},{1,0},{2,3},{3,2},{4,5},{5,4},{6,7},{7,6},{8,9},{9,8},{10,11... | collective-permute-start | bytes 208904 | tf_op jit(solution)/shard_map/ppermute | solution.py:215
  10.6 0.9 %copy-start = (f32[144,128]{1,0:T(8,128)S(1)}, f32[144,128]{1,0:T(8,128)}, u32[]{:S(2)}) copy-start(f32[144,128]{1,0:T(8,128)} %get-tuple-element.14.mine) | copy-start | bytes 221188
  11.8 5.0 %collective-permute-start.5 = (bf16[8,4096]{1,0:T(8,128)(2,1)S(1)}, bf16[8,4096]{1,0:T(8,128)(2,1)S(1)}, u32[]{:S(2)}, u32[]{:S(2)}) collective-permute-start(bf16[8,4096]{1,0:T(8,128)(2,1)S(1)} %pad_maximum_fusion.3), channel_id=1, source_target_pairs={{0,8},{1,9},{2,10},{3,11},{4,12},{5,13},{6,14},{7,15},{8,0},{9,1},... | collective-permute-start | bytes 196616 | tf_op jit(solution)/shard_map/ppermute | solution.py:215
  11.9 4.9 %collective-permute-start.1 = (f32[64,128]{1,0:T(8,128)S(1)}, f32[64,128]{1,0:T(8,128)S(1)}, u32[]{:S(2)}, u32[]{:S(2)}) collective-permute-start(f32[64,128]{1,0:T(8,128)S(1)} %factor.1), channel_id=1, source_target_pairs={{0,8},{1,9},{2,10},{3,11},{4,12},{5,13},{6,14},{7,15},{8,0},{9,1},... | collective-permute-start | bytes 98312 | tf_op jit(solution)/shard_map/ppermute | solution.py:215
  16.9 8.2 %collective-permute-start.6 = (bf16[16,4096]{1,0:T(8,128)(2,1)S(1)}, bf16[16,4096]{1,0:T(8,128)(2,1)S(1)}, u32[]{:S(2)}, u32[]{:S(2)}) collective-permute-start(bf16[16,4096]{1,0:T(8,128)(2,1)S(1)} %pad_maximum_fusion.2), channel_id=1, source_target_pairs={{0,4},{1,5},{2,6},{3,7},{4,0},{5,1},{6,2},{7,3},{8,12},{9,13},{10,... | collective-permute-start | bytes 393224 | tf_op jit(solution)/shard_map/ppermute | solution.py:215
  20.9 4.2 %collective-permute-start.2 = (f32[64,128]{1,0:T(8,128)S(1)}, f32[64,128]{1,0:T(8,128)S(1)}, u32[]{:S(2)}, u32[]{:S(2)}) collective-permute-start(f32[64,128]{1,0:T(8,128)S(1)} %add.12), channel_id=1, source_target_pairs={{0,4},{1,5},{2,6},{3,7},{4,0},{5,1},{6,2},{7,3},{8,12},{9,13},{10,... | collective-permute-start | bytes 98312 | tf_op jit(solution)/shard_map/ppermute | solution.py:215
  25.1 13.5 %collective-permute-start.7 = (bf16[32,4096]{1,0:T(8,128)(2,1)S(1)}, bf16[32,4096]{1,0:T(8,128)(2,1)S(1)}, u32[]{:S(2)}, u32[]{:S(2)}) collective-permute-start(bf16[32,4096]{1,0:T(8,128)(2,1)S(1)} %pad_maximum_fusion.1), channel_id=1, source_target_pairs={{0,2},{1,3},{2,0},{3,1},{4,6},{5,7},{6,4},{7,5},{8,10},{9,11},{10,... | collective-permute-start | bytes 786440 | tf_op jit(solution)/shard_map/ppermute | solution.py:215
  26.4 6.3 %collective-permute-start.3 = (f32[64,128]{1,0:T(8,128)S(1)}, f32[64,128]{1,0:T(8,128)S(1)}, u32[]{:S(2)}, u32[]{:S(2)}) collective-permute-start(f32[64,128]{1,0:T(8,128)S(1)} %add.13), channel_id=1, source_target_pairs={{0,2},{1,3},{2,0},{3,1},{4,6},{5,7},{6,4},{7,5},{8,10},{9,11},{10,... | collective-permute-start | bytes 98312 | tf_op jit(solution)/shard_map/ppermute | solution.py:215
  39.9 2.8 %collective-permute-start.8 = (f32[16,64]{1,0:T(8,128)S(1)}, f32[16,64]{1,0:T(8,128)S(1)}, u32[]{:S(2)}, u32[]{:S(2)}) collective-permute-start(f32[16,64]{1,0:T(8,128)S(1)} %get-tuple-element.22), channel_id=1, source_target_pairs={{0,1},{1,0},{2,3},{3,2},{4,5},{5,4},{6,7},{7,6},{8,9},{9,8},{10,11... | collective-permute-start | bytes 12296 | tf_op jit(solution)/shard_map/ppermute | solution.py:215

commit v3 on v2

--- a/solution.py
+++ b/solution.py
@@ -8,6 +8,8 @@
 from jax.sharding import PartitionSpec as P
 
 EX_DEV = 16
+BLOCK = 8
+LIGHT, HEAVY = 10**6, 2 * 10**10
 HIGH = lax.Precision.HIGHEST
 F32 = jnp.float32
 BF16 = jnp.bfloat16
@@ -22,9 +24,9 @@
 
 
 def project_kernel(
-    chunks, act, grad, ids, pin, pout, query, weight,
-    keep, send, q_keep, q_send,
-    act_v, grad_v, ids_v, pin_v, pout_v, query_v, weight_v, sems,
+    chunks, act, grad, ids, pin, pout, weight,
+    keep, send,
+    act_v, grad_v, ids_v, pin_v, pout_v, weight_v, sems,
 ):
     ckpts, rows, depth = act.shape
     side = pin.shape[0]
@@ -32,32 +34,29 @@
     copies = [
         pltpu.make_async_copy(pout, pout_v, sems.at[0]),
         pltpu.make_async_copy(grad, grad_v, sems.at[1]),
-        pltpu.make_async_copy(query, query_v, sems.at[2]),
-        pltpu.make_async_copy(ids, ids_v, sems.at[3]),
-        pltpu.make_async_copy(weight, weight_v, sems.at[4]),
+        pltpu.make_async_copy(ids, ids_v, sems.at[2]),
+        pltpu.make_async_copy(weight, weight_v, sems.at[3]),
     ]
     for k in range(chunks):
         span = pl.ds(k * step, step)
-        copies.append(pltpu.make_async_copy(pin.at[:, span], pin_v.at[:, span], sems.at[5 + 2 * k]))
+        copies.append(pltpu.make_async_copy(pin.at[:, span], pin_v.at[:, span], sems.at[4 + 2 * k]))
         copies.append(
-            pltpu.make_async_copy(act.at[:, :, span], act_v.at[:, :, span], sems.at[6 + 2 * k])
+            pltpu.make_async_copy(act.at[:, :, span], act_v.at[:, :, span], sems.at[5 + 2 * k])
         )
     for copy in copies:
         copy.start()
-    for copy in copies[:5]:
+    for copy in copies[:4]:
         copy.wait()
     odd = lax.rem(lax.axis_index("tok"), 2)
     tail = jnp.broadcast_to(ids_v[...].astype(F32), (8, rows))
     keep[rows : rows + 8, :] = tail
     send[rows : rows + 8, :] = tail
     keep[rows + 8 :, :] = jnp.full((8, 2 * side), weight_v[odd] / side, F32)
-    q_keep[...] = jnp.where(odd == 0, query_v[0], query_v[1])
-    q_send[...] = jnp.where(odd == 0, query_v[1], query_v[0])
     s = nt(grad_v[...].reshape(ckpts * rows, -1), pout_v[...])
     a = jnp.zeros((ckpts * rows, side), F32)
     for k in range(chunks):
+        copies[4 + 2 * k].wait()
         copies[5 + 2 * k].wait()
-        copies[6 + 2 * k].wait()
         span = slice(k * step, (k + 1) * step)
         a = a + nt(act_v[:, :, span].reshape(ckpts * rows, step), pin_v[:, span])
     both = jnp.concatenate([a, s], axis=1)
@@ -66,7 +65,7 @@
     send[0:rows, :] = jnp.where(odd == 0, second, first)
 
 
-def project(act, grad, ids, pin, pout, query, weight):
+def project(act, grad, ids, pin, pout, weight):
     ckpts, rows, depth = act.shape
     side, width = pout.shape
     chunks = 8
@@ -75,35 +74,70 @@
         out_shape=(
             jax.ShapeDtypeStruct((rows + 16, 2 * side), F32),
             jax.ShapeDtypeStruct((rows + 8, 2 * side), F32),
-            jax.ShapeDtypeStruct(query.shape[1:], BF16),
-            jax.ShapeDtypeStruct(query.shape[1:], BF16),
         ),
-        in_specs=[HBM] * 7,
-        out_specs=(VMEM,) * 4,
+        in_specs=[HBM] * 6,
+        out_specs=(VMEM, VMEM),
         scratch_shapes=[
             pltpu.VMEM((ckpts, rows, depth), BF16),
             pltpu.VMEM((ckpts, rows, width), BF16),
             pltpu.VMEM((1, rows), jnp.int32),
             pltpu.VMEM((side, depth), BF16),
             pltpu.VMEM((side, width), BF16),
-            pltpu.VMEM(query.shape, BF16),
             pltpu.SMEM(weight.shape, F32),
-            pltpu.SemaphoreType.DMA((5 + 2 * chunks,)),
+            pltpu.SemaphoreType.DMA((4 + 2 * chunks,)),
         ],
         compiler_params=pltpu.CompilerParams(vmem_limit_bytes=63 * 2**20),
+        cost_estimate=pl.CostEstimate(flops=HEAVY, bytes_accessed=2 * 10**7, transcendentals=0),
         name="project",
-    )(act, grad, ids, pin, pout, query, weight)
-
-
-def factor_kernel(total, mine, other, out):
-    rows, lanes = other.shape[0] - 8, other.shape[1]
+    )(act, grad, ids, pin, pout, weight)
+
+
+def gram_kernel(total, rows, x, *rest):
+    lanes = x.shape[1]
     side = lanes // 2
-    x = jnp.concatenate([mine[0:rows, :], other[0:rows, :]], axis=0)
+    x = x[0:rows, :]
     g = lax.dot_general(
         x, x, (((0,), (0,)), ((), ())), precision=HIGH, preferred_element_type=F32
     )
     lane = lax.broadcasted_iota(jnp.int32, (side, lanes), 1)
-    out[...] = jnp.where(lane < side, g[:side], g[side:]) * (1.0 / total)
+    g = jnp.where(lane < side, g[:side], g[side:]) * (1.0 / total)
+    for more in rest[:-1]:
+        g = g + more[...]
+    rest[-1][...] = g
+
+
+def gram(total, rows, cost, x, *more):
+    lanes = x.shape[1]
+    return pl.pallas_call(
+        functools.partial(gram_kernel, total, rows),
+        out_shape=jax.ShapeDtypeStruct((lanes // 2, lanes), F32),
+        in_specs=[VMEM] * (1 + len(more)),
+        out_specs=VMEM,
+        compiler_params=pltpu.CompilerParams(vmem_limit_bytes=4 * 2**20),
+        cost_estimate=pl.CostEstimate(flops=cost, bytes_accessed=cost // 1000, transcendentals=0),
+        name="gram",
+    )(x, *more)
+
+
+def tick_kernel(*refs):
+    total = refs[0][...]
+    for ref in refs[1:-1]:
+        total = total + ref[...]
+    refs[-1][...] = total
+
+
+def tick(weight, *terms):
+    return pl.pallas_call(
+        tick_kernel,
+        out_shape=jax.ShapeDtypeStruct(terms[0].shape, F32),
+        in_specs=[VMEM] * len(terms),
+        out_specs=VMEM,
+        compiler_params=pltpu.CompilerParams(vmem_limit_bytes=2**20),
+        cost_estimate=pl.CostEstimate(
+            flops=weight, bytes_accessed=weight // 1000, transcendentals=0
+        ),
+        name="tick",
+    )(*terms)
 
 
 def inverse_kernel(g, out):
@@ -114,18 +148,37 @@
     local = jnp.where(left, lane, lane - side)
     m = g[...]
     diag = jnp.sum(jnp.where(local == row, m, 0.0), axis=0, keepdims=True)
-    lead = left[:1]
-    tr_a = jnp.sum(jnp.where(lead, diag, 0.0), axis=1, keepdims=True)
-    tr_s = jnp.sum(jnp.where(lead, 0.0, diag), axis=1, keepdims=True)
-    damp = 0.05 * (jnp.where(lead, tr_a, tr_s) / side)
+    first = left[:1]
+    tr_a = jnp.sum(jnp.where(first, diag, 0.0), axis=1, keepdims=True)
+    tr_s = jnp.sum(jnp.where(first, 0.0, diag), axis=1, keepdims=True)
+    damp = 0.05 * (jnp.where(first, tr_a, tr_s) / side)
     m = m + jnp.where(local == row, damp, 0.0)
-    for k in range(side):
-        col = jnp.where(left, m[:, k : k + 1], m[:, side + k : side + k + 1])
-        pivot = 1.0 / col[k : k + 1]
-        mark = local[:1] == k
-        line = jnp.where(mark, 1.0, m[k : k + 1]) * pivot
-        here = row == k
-        m = jnp.where(here, 0.0, jnp.where(local == k, 0.0, m)) - jnp.where(here, -1.0, col) * line
+    lead = local[:1]
+    for k in range(0, side, BLOCK):
+        at = jnp.where(left, k, side + k)
+        cols = [jnp.take_along_axis(m, at + j, axis=1) for j in range(BLOCK)]
+        small = [[col[k + i : k + i + 1] for col in cols] for i in range(BLOCK)]
+        lines = []
+        for i in range(BLOCK):
+            line = m[k + i : k + i + 1]
+            for j in range(BLOCK):
+                line = jnp.where(lead == k + j, float(i == j), line)
+            lines.append(line)
+        for p in range(BLOCK):
+            scale = 1.0 / small[p][p]
+            for j in range(p + 1, BLOCK):
+                small[p][j] = small[p][j] * scale
+            lines[p] = lines[p] * scale
+            for i in range(BLOCK):
+                if i != p:
+                    factor = small[i][p]
+                    for j in range(p + 1, BLOCK):
+                        small[i][j] = small[i][j] - factor * small[p][j]
+                    lines[i] = lines[i] - factor * lines[p]
+        inside = (row >= k) & (row < k + BLOCK)
+        m = jnp.where(inside | ((local >= k) & (local < k + BLOCK)), 0.0, m)
+        for j in range(BLOCK):
+            m = m - jnp.where(row == k + j, -1.0, jnp.where(inside, 0.0, cols[j])) * lines[j]
     out[...] = m
 
 
@@ -215,26 +268,28 @@
         return lax.ppermute(x, "tok", [(i, i ^ mask) for i in range(devices)])
 
     ids = example_ids.reshape(1, rows)
-    mine, send, q_keep, q_send = project(
-        inputs_act, out_grads, ids, proj_in.T, proj_out.T, query_sketch, ckpt_weight
-    )
+    first = devices // 2
+    arrived = swap(query_sketch, first)
+    mine, send = project(inputs_act, out_grads, ids, proj_in.T, proj_out.T, ckpt_weight)
     other = swap(send, 1)
-    queries = jnp.concatenate([q_keep, swap(q_send, 1)], axis=0)
-    g = pl.pallas_call(
-        functools.partial(factor_kernel, total),
-        out_shape=jax.ShapeDtypeStruct((side, 2 * side), F32),
-        in_specs=[VMEM, VMEM],
-        out_specs=VMEM,
-        compiler_params=pltpu.CompilerParams(vmem_limit_bytes=4 * 2**20),
-        name="factor",
-    )(mine, other)
-    masks = [1]
-    while devices >> len(masks) > 1:
-        masks.append(devices >> len(masks))
-    for mask in masks[1:]:
-        queries, _ = lax.optimization_barrier((queries, g))
-        g = g + swap(g, mask)
-        queries = jnp.concatenate([queries, swap(queries, mask)], axis=0)
+    arrived, mine = lax.optimization_barrier((arrived, mine))
+    both = jnp.concatenate([query_sketch, arrived], axis=1)
+    even = lax.rem(me, 2) == 0
+    queries = jnp.where(even, both[0], both[1])
+    queries = jnp.concatenate([queries, swap(jnp.where(even, both[1], both[0]), 1)], axis=0)
+    g = gram(total, rows, LIGHT, other, gram(total, rows, HEAVY, mine))
+    sums = [first]
+    while sums[-1] > 2:
+        sums.append(sums[-1] // 2)
+    late = sums[:0:-1]
+    masks = (first, 1, *late)
+    for step, mask in enumerate(sums):
+        last = step == len(sums) - 1
+        held = g
+        if late:
+            queries, held = lax.optimization_barrier((queries, tick(HEAVY, g)))
+            queries = jnp.concatenate([queries, swap(queries, late.pop(0))], axis=0)
+        g = tick(HEAVY if held is not g else LIGHT, held, swap(g, mask))
     inv = pl.pallas_call(
         inverse_kernel,
         out_shape=jax.ShapeDtypeStruct((side, 2 * side), F32),
@@ -244,7 +299,7 @@
         name="inverse",
     )(g)
     keep, send = pl.pallas_call(
-        functools.partial(score_kernel, q_rows, tuple(masks)),
+        functools.partial(score_kernel, q_rows, masks),
         out_shape=(
             jax.ShapeDtypeStruct((EX_DEV, q_rows * devices), F32),
             jax.ShapeDtypeStruct((EX_DEV, q_rows * devices), F32),

time: 43.5 us -> 33.4 us (0.77)
  the two profiles are of different devices: /device:TPU:17 before, /device:TPU:0 now
where the time goes in v3:
time: 33.4 us; the launch traced here: 33.2 us
  Pallas kernels  11.6 us (35%)
  starting transfers between devices  10.7 us (32%)
  waiting for transfers between devices  8.58 us (26%)
  local copies, waits for them, and re-layouts  1.46 us (4%)
  other arithmetic  0.74 us (2%)
    ppermute x9, starting transfers between devices, swap(): return lax.ppermute(x, 'tok', [(i, i ^ mask) for i in range(devices)])  10.7 us
    ppermute x9, waiting for transfers between devices, swap(): return lax.ppermute(x, 'tok', [(i, i ^ mask) for i in range(devices)])  8.58 us
    pallas_call x1, Pallas kernels, project(): pl.pallas_call(functools.partial(project_kernel, chunks), out_shape=(jax....  7.98 us
    pallas_call x1, Pallas kernels, local(): pl.pallas_call(inverse_kernel, out_shape=jax.ShapeDtypeStruct((side, 2 *...  1.83 us
    unnamed x6, local copies, waits for them, and re-layouts  1.46 us
    pallas_call x1, Pallas kernels, local(): pl.pallas_call(functools.partial(score_kernel, q_rows, masks), out_shape=...  1.23 us
  transfers between devices with their start and end apart: 9, of which 5 were waited for; matrix products, arithmetic and copies ran while one was open for 0% of the time, Pallas kernels for 31%

profile of v3, /device:TPU:0, one launch (start us, length us, event | category | flops | bytes accessed | tf_op | source)
XLA Modules:
  0.0 33.2 jit_solution(927225401076773725)
XLA Ops:
  0.0 4.0 %collective-permute-start = (bf16[2,4,4096]{2,1,0:T(4,128)(2,1)}, bf16[2,4,4096]{2,1,0:T(4,128)(2,1)S(1)}, u32[]{:S(2)}, u32[]{:S(2)}) collective-permute-start(bf16[2,4,4096]{2,1,0:T(4,128)(2,1)} %param.12), channel_id=1, source_target_pairs={{0,8},{1,9},{2,10},{3,11},{4,12},{5,13},{6,14},{7,15},{8,0},{9,1},... | collective-permute-start | bytes 196616 | tf_op jit(solution)/shard_map/ppermute | solution.py:268
  4.0 8.0 %project.1 = (f32[144,128]{1,0:T(8,128)}, f32[136,128]{1,0:T(8,128)}) custom-call(bf16[2,128,14336]{2,1,0:T(8,128)(2,1)} %act.1, bf16[2,128,4096]{2,1,0:T(8,128)(2,1)} %grad.1, s32[1,128]{1,0:T(1,128)} %bitcast.9, bf16[64,14336]{1,0:T(8,128)(2,1)} %bitcast.7, bf16[64,4096]{1,0:T(8,128)(2,1)} %bitcast.8, f32[2]{0:T(128)} %weight.1), custom_call_target="tpu_custom_call" | custom-call | flops 20000000000 | bytes 20000000 | tf_op jit(solution)/shard_map/project/pallas_call | solution.py:72
  12.0 0.1 collective-permute-start.2
  12.1 0.0 collective-permute-done
  12.1 0.0 copy-start
  12.1 0.9 %copy-done = f32[144,128]{1,0:T(8,128)S(1)} copy-done((f32[144,128]{1,0:T(8,128)S(1)}, f32[144,128]{1,0:T(8,128)}, u32[]{:S(2)}) %copy-start) | copy-done | bytes 73752
  13.0 0.0 copy-start.2
  13.0 0.3 gram.2.rest_0_
  13.3 0.6 %copy-done.2 = bf16[2,4,4096]{2,1,0:T(4,128)(2,1)S(1)} copy-done((bf16[2,4,4096]{2,1,0:T(4,128)(2,1)S(1)}, bf16[2,4,4096]{2,1,0:T(4,128)(2,1)}, u32[]{:S(2)}) %copy-start.2) | copy-done | bytes 65560
  13.8 0.1 select_bitcast_fusion.1
  13.9 0.5 %collective-permute-start.1 = (bf16[8,4096]{1,0:T(8,128)(2,1)S(1)}, bf16[8,4096]{1,0:T(8,128)(2,1)S(1)}, u32[]{:S(2)}, u32[]{:S(2)}) collective-permute-start(bf16[8,4096]{1,0:T(8,128)(2,1)S(1)} %get-tuple-element.26), channel_id=1, source_target_pairs={{0,1},{1,0},{2,3},{3,2},{4,5},{5,4},{6,7},{7,6},{8,9},{9,8},{10,11... | collective-permute-start | bytes 196616 | tf_op jit(solution)/shard_map/ppermute | solution.py:268
  14.5 0.0 collective-permute-done.2.x.other
  14.5 0.3 gram.3.refs_0_
  14.8 0.1 collective-permute-start.4
  14.8 0.5 %collective-permute-done.1 = bf16[8,4096]{1,0:T(8,128)(2,1)S(1)} collective-permute-done((bf16[8,4096]{1,0:T(8,128)(2,1)S(1)}, bf16[8,4096]{1,0:T(8,128)(2,1)S(1)}, u32[]{:S(2)}, u32[]{:S(2)}) %collective-permute-start.1) | collective-permute-done | bytes 65568 | tf_op jit(solution)/shard_map/ppermute | solution.py:268
  15.4 1.6 %collective-permute-start.3 = (bf16[16,4096]{1,0:T(8,128)(2,1)S(1)}, bf16[16,4096]{1,0:T(8,128)(2,1)S(1)}, u32[]{:S(2)}, u32[]{:S(2)}) collective-permute-start(bf16[16,4096]{1,0:T(8,128)(2,1)S(1)} %pad_maximum_fusion.2), channel_id=1, source_target_pairs={{0,2},{1,3},{2,0},{3,1},{4,6},{5,7},{6,4},{7,5},{8,10},{9,11},{10,... | collective-permute-start | bytes 393224 | tf_op jit(solution)/shard_map/ppermute | solution.py:268
  17.0 3.0 %collective-permute-done.4.refs_1_ = f32[64,128]{1,0:T(8,128)S(1)} collective-permute-done((f32[64,128]{1,0:T(8,128)S(1)}, f32[64,128]{1,0:T(8,128)S(1)}, u32[]{:S(2)}, u32[]{:S(2)}) %collective-permute-start.4) | collective-permute-done | bytes 32800 | tf_op jit(solution)/shard_map/ppermute | solution.py:268
  20.0 1.3 %collective-permute-start.5 = (f32[64,128]{1,0:T(8,128)S(1)}, f32[64,128]{1,0:T(8,128)S(1)}, u32[]{:S(2)}, u32[]{:S(2)}) collective-permute-start(f32[64,128]{1,0:T(8,128)S(1)} %tick.6.refs_0_), channel_id=1, source_target_pairs={{0,4},{1,5},{2,6},{3,7},{4,0},{5,1},{6,2},{7,3},{8,12},{9,13},{10,... | collective-permute-start | bytes 98312 | tf_op jit(solution)/shard_map/ppermute | solution.py:268
  21.3 0.0 collective-permute-done.3
  21.3 0.0 copy-start.1
  21.3 1.6 %collective-permute-start.7 = (bf16[32,4096]{1,0:T(8,128)(2,1)S(1)}, bf16[32,4096]{1,0:T(8,128)(2,1)S(1)}, u32[]{:S(2)}, u32[]{:S(2)}) collective-permute-start(bf16[32,4096]{1,0:T(8,128)(2,1)S(1)} %pad_maximum_fusion.1), channel_id=1, source_target_pairs={{0,4},{1,5},{2,6},{3,7},{4,0},{5,1},{6,2},{7,3},{8,12},{9,13},{10,... | collective-permute-start | bytes 786440 | tf_op jit(solution)/shard_map/ppermute | solution.py:268
  22.9 1.4 %collective-permute-done.5.refs_1_ = f32[64,128]{1,0:T(8,128)S(1)} collective-permute-done((f32[64,128]{1,0:T(8,128)S(1)}, f32[64,128]{1,0:T(8,128)S(1)}, u32[]{:S(2)}, u32[]{:S(2)}) %collective-permute-start.5) | collective-permute-done | bytes 32800 | tf_op jit(solution)/shard_map/ppermute | solution.py:268
  24.3 1.5 %collective-permute-start.6 = (f32[64,128]{1,0:T(8,128)S(1)}, f32[64,128]{1,0:T(8,128)S(1)}, u32[]{:S(2)}, u32[]{:S(2)}) collective-permute-start(f32[64,128]{1,0:T(8,128)S(1)} %tick.8.refs_0_), channel_id=1, source_target_pairs={{0,2},{1,3},{2,0},{3,1},{4,6},{5,7},{6,4},{7,5},{8,10},{9,11},{10,... | collective-permute-start | bytes 98312 | tf_op jit(solution)/shard_map/ppermute | solution.py:268
  25.9 2.4 %collective-permute-done.6.refs_1_ = f32[64,128]{1,0:T(8,128)S(1)} collective-permute-done((f32[64,128]{1,0:T(8,128)S(1)}, f32[64,128]{1,0:T(8,128)S(1)}, u32[]{:S(2)}, u32[]{:S(2)}) %collective-permute-start.6) | collective-permute-done | bytes 32800 | tf_op jit(solution)/shard_map/ppermute | solution.py:268
  28.3 1.8 %inverse.1.inv = f32[64,128]{1,0:T(8,128)S(1)} custom-call(f32[64,128]{1,0:T(8,128)S(1)} %tick.9.g), custom_call_target="tpu_custom_call" | custom-call | tf_op jit(solution)/shard_map/inverse/pallas_call | solution.py:293
  30.1 0.0 collective-permute-done.7
  30.1 0.0 copy-done.1
  30.1 1.2 %score.1 = (f32[16,64]{1,0:T(8,128)S(1)}, f32[16,64]{1,0:T(8,128)S(1)}) custom-call(f32[64,128]{1,0:T(8,128)S(1)} %inverse.1.inv, f32[144,128]{1,0:T(8,128)S(1)} %copy-done.1, f32[136,128]{1,0:T(8,128)S(1)} %collective-permute-done.2.x.other, bf16[64,4096]{1,0:T(8,128)(2,1)S(1)} %pad_maximum_fusion.queries), custom_call_target="tpu_custom_call" | custom-call | tf_op jit(solution)/shard_map/score/pallas_call | solution.py:301
  31.4 0.0 collective-permute-start.8
  31.4 1.2 %collective-permute-done.8 = f32[16,64]{1,0:T(8,128)S(1)} collective-permute-done((f32[16,64]{1,0:T(8,128)S(1)}, f32[16,64]{1,0:T(8,128)S(1)}, u32[]{:S(2)}, u32[]{:S(2)}) %collective-permute-start.8) | collective-permute-done | bytes 4128 | tf_op jit(solution)/shard_map/ppermute | solution.py:268
  32.6 0.6 %add.3 = f32[16,64]{1,0:T(8,128)} add(f32[16,64]{1,0:T(8,128)S(1)} %get-tuple-element.23, f32[16,64]{1,0:T(8,128)S(1)} %collective-permute-done.8) | non-fusion elementwise | flops 1024 | bytes 12288 | tf_op jit(solution)/shard_map/add | solution.py:312
  (8 shorter events, 0.1 us)
Async XLA Ops:
  0.0 12.1 %collective-permute-start = (bf16[2,4,4096]{2,1,0:T(4,128)(2,1)}, bf16[2,4,4096]{2,1,0:T(4,128)(2,1)S(1)}, u32[]{:S(2)}, u32[]{:S(2)}) collective-permute-start(bf16[2,4,4096]{2,1,0:T(4,128)(2,1)} %param.12), channel_id=1, source_target_pairs={{0,8},{1,9},{2,10},{3,11},{4,12},{5,13},{6,14},{7,15},{8,0},{9,1},... | collective-permute-start | bytes 196616 | tf_op jit(solution)/shard_map/ppermute | solution.py:268
  12.0 2.5 %collective-permute-start.2 = (f32[136,128]{1,0:T(8,128)}, f32[136,128]{1,0:T(8,128)S(1)}, u32[]{:S(2)}, u32[]{:S(2)}) collective-permute-start(f32[136,128]{1,0:T(8,128)} %get-tuple-element.17), channel_id=1, source_target_pairs={{0,1},{1,0},{2,3},{3,2},{4,5},{5,4},{6,7},{7,6},{8,9},{9,8},{10,11... | collective-permute-start | bytes 208904 | tf_op jit(solution)/shard_map/ppermute | solution.py:268
  12.1 0.9 %copy-start = (f32[144,128]{1,0:T(8,128)S(1)}, f32[144,128]{1,0:T(8,128)}, u32[]{:S(2)}) copy-start(f32[144,128]{1,0:T(8,128)} %get-tuple-element.18.x.mine) | copy-start | bytes 221188
  13.0 0.8 %copy-start.2 = (bf16[2,4,4096]{2,1,0:T(4,128)(2,1)S(1)}, bf16[2,4,4096]{2,1,0:T(4,128)(2,1)}, u32[]{:S(2)}) copy-start(bf16[2,4,4096]{2,1,0:T(4,128)(2,1)} %param.12) | copy-start | bytes 196612
  13.9 1.5 %collective-permute-start.1 = (bf16[8,4096]{1,0:T(8,128)(2,1)S(1)}, bf16[8,4096]{1,0:T(8,128)(2,1)S(1)}, u32[]{:S(2)}, u32[]{:S(2)}) collective-permute-start(bf16[8,4096]{1,0:T(8,128)(2,1)S(1)} %get-tuple-element.26), channel_id=1, source_target_pairs={{0,1},{1,0},{2,3},{3,2},{4,5},{5,4},{6,7},{7,6},{8,9},{9,8},{10,11... | collective-permute-start | bytes 196616 | tf_op jit(solution)/shard_map/ppermute | solution.py:268
  14.8 5.2 %collective-permute-start.4 = (f32[64,128]{1,0:T(8,128)S(1)}, f32[64,128]{1,0:T(8,128)S(1)}, u32[]{:S(2)}, u32[]{:S(2)}) collective-permute-start(f32[64,128]{1,0:T(8,128)S(1)} %gram.3.refs_0_), channel_id=1, source_target_pairs={{0,8},{1,9},{2,10},{3,11},{4,12},{5,13},{6,14},{7,15},{8,0},{9,1},... | collective-permute-start | bytes 98312 | tf_op jit(solution)/shard_map/ppermute | solution.py:268
  15.4 5.9 %collective-permute-start.3 = (bf16[16,4096]{1,0:T(8,128)(2,1)S(1)}, bf16[16,4096]{1,0:T(8,128)(2,1)S(1)}, u32[]{:S(2)}, u32[]{:S(2)}) collective-permute-start(bf16[16,4096]{1,0:T(8,128)(2,1)S(1)} %pad_maximum_fusion.2), channel_id=1, source_target_pairs={{0,2},{1,3},{2,0},{3,1},{4,6},{5,7},{6,4},{7,5},{8,10},{9,11},{10,... | collective-permute-start | bytes 393224 | tf_op jit(solution)/shard_map/ppermute | solution.py:268
  20.0 4.3 %collective-permute-start.5 = (f32[64,128]{1,0:T(8,128)S(1)}, f32[64,128]{1,0:T(8,128)S(1)}, u32[]{:S(2)}, u32[]{:S(2)}) collective-permute-start(f32[64,128]{1,0:T(8,128)S(1)} %tick.6.refs_0_), channel_id=1, source_target_pairs={{0,4},{1,5},{2,6},{3,7},{4,0},{5,1},{6,2},{7,3},{8,12},{9,13},{10,... | collective-permute-start | bytes 98312 | tf_op jit(solution)/shard_map/ppermute | solution.py:268
  21.3 8.8 %copy-start.1 = (f32[144,128]{1,0:T(8,128)S(1)}, f32[144,128]{1,0:T(8,128)}, u32[]{:S(2)}) copy-start(f32[144,128]{1,0:T(8,128)} %get-tuple-element.18.x.mine) | copy-start | bytes 221188
  21.3 8.8 %collective-permute-start.7 = (bf16[32,4096]{1,0:T(8,128)(2,1)S(1)}, bf16[32,4096]{1,0:T(8,128)(2,1)S(1)}, u32[]{:S(2)}, u32[]{:S(2)}) collective-permute-start(bf16[32,4096]{1,0:T(8,128)(2,1)S(1)} %pad_maximum_fusion.1), channel_id=1, source_target_pairs={{0,4},{1,5},{2,6},{3,7},{4,0},{5,1},{6,2},{7,3},{8,12},{9,13},{10,... | collective-permute-start | bytes 786440 | tf_op jit(solution)/shard_map/ppermute | solution.py:268
  24.3 3.9 %collective-permute-start.6 = (f32[64,128]{1,0:T(8,128)S(1)}, f32[64,128]{1,0:T(8,128)S(1)}, u32[]{:S(2)}, u32[]{:S(2)}) collective-permute-start(f32[64,128]{1,0:T(8,128)S(1)} %tick.8.refs_0_), channel_id=1, source_target_pairs={{0,2},{1,3},{2,0},{3,1},{4,6},{5,7},{6,4},{7,5},{8,10},{9,11},{10,... | collective-permute-start | bytes 98312 | tf_op jit(solution)/shard_map/ppermute | solution.py:268
  31.4 1.2 %collective-permute-start.8 = (f32[16,64]{1,0:T(8,128)S(1)}, f32[16,64]{1,0:T(8,128)S(1)}, u32[]{:S(2)}, u32[]{:S(2)}) collective-permute-start(f32[16,64]{1,0:T(8,128)S(1)} %get-tuple-element.24), channel_id=1, source_target_pairs={{0,1},{1,0},{2,3},{3,2},{4,5},{5,4},{6,7},{7,6},{8,9},{9,8},{10,11... | collective-permute-start | bytes 12296 | tf_op jit(solution)/shard_map/ppermute | solution.py:268

commit v4 on v3

--- a/solution.py
+++ b/solution.py
@@ -17,106 +17,91 @@
 HBM = pl.BlockSpec(memory_space=pltpu.HBM)
 
 
+def role(me, devices):
+    return me & 1
+
+
 def nt(x, y, precision=None):
     return lax.dot_general(
         x, y, (((1,), (1,)), ((), ())), precision=precision, preferred_element_type=F32
     )
 
 
-def project_kernel(
-    chunks, act, grad, ids, pin, pout, weight,
-    keep, send,
-    act_v, grad_v, ids_v, pin_v, pout_v, weight_v, sems,
-):
-    ckpts, rows, depth = act.shape
+def project_kernel(devices, act, grad, ids, pin, pout, weight, zero, keep, send, own):
+    ckpts, rows, _ = act.shape
     side = pin.shape[0]
-    step = depth // chunks
-    copies = [
-        pltpu.make_async_copy(pout, pout_v, sems.at[0]),
-        pltpu.make_async_copy(grad, grad_v, sems.at[1]),
-        pltpu.make_async_copy(ids, ids_v, sems.at[2]),
-        pltpu.make_async_copy(weight, weight_v, sems.at[3]),
-    ]
-    for k in range(chunks):
-        span = pl.ds(k * step, step)
-        copies.append(pltpu.make_async_copy(pin.at[:, span], pin_v.at[:, span], sems.at[4 + 2 * k]))
-        copies.append(
-            pltpu.make_async_copy(act.at[:, :, span], act_v.at[:, :, span], sems.at[5 + 2 * k])
+    half = rows // 2
+
+    def dots(x, w):
+        return [
+            nt(x[c, h * half : (h + 1) * half, :], w[...]) for c in range(ckpts) for h in range(2)
+        ]
+
+    s = dots(grad, pout)
+    a = dots(act, pin)
+    first, second = (
+        jnp.concatenate(
+            [jnp.concatenate([a[j], s[j]], axis=1) for j in (2 * c, 2 * c + 1)], axis=0
         )
-    for copy in copies:
-        copy.start()
-    for copy in copies[:4]:
-        copy.wait()
-    odd = lax.rem(lax.axis_index("tok"), 2)
-    tail = jnp.broadcast_to(ids_v[...].astype(F32), (8, rows))
+        for c in range(2)
+    )
+    odd = role(lax.axis_index("tok"), devices)
+    mine = jnp.where(odd == 0, first, second)
+    tail = jnp.broadcast_to(ids[...].astype(F32), (8, rows))
+    scale = jnp.where(odd == 0, weight[:, 0:1], weight[:, 1:2]) / side + zero[0:1, 0:1]
+    keep[0:rows, :] = mine
     keep[rows : rows + 8, :] = tail
+    keep[rows + 8 :, :] = jnp.broadcast_to(scale, (8, 2 * side))
+    send[0:rows, :] = jnp.where(odd == 0, second, first)
     send[rows : rows + 8, :] = tail
-    keep[rows + 8 :, :] = jnp.full((8, 2 * side), weight_v[odd] / side, F32)
-    s = nt(grad_v[...].reshape(ckpts * rows, -1), pout_v[...])
-    a = jnp.zeros((ckpts * rows, side), F32)
-    for k in range(chunks):
-        copies[4 + 2 * k].wait()
-        copies[5 + 2 * k].wait()
-        span = slice(k * step, (k + 1) * step)
-        a = a + nt(act_v[:, :, span].reshape(ckpts * rows, step), pin_v[:, span])
-    both = jnp.concatenate([a, s], axis=1)
-    first, second = both[:rows], both[rows:]
-    keep[0:rows, :] = jnp.where(odd == 0, first, second)
-    send[0:rows, :] = jnp.where(odd == 0, second, first)
-
-
-def project(act, grad, ids, pin, pout, weight):
-    ckpts, rows, depth = act.shape
-    side, width = pout.shape
-    chunks = 8
+    own[...] = factors(mine, rows * devices)
+
+
+def project(devices, act, grad, ids, pin, pout, weight, zero):
+    rows = act.shape[1]
+    side = pout.shape[0]
     return pl.pallas_call(
-        functools.partial(project_kernel, chunks),
+        functools.partial(project_kernel, devices),
         out_shape=(
             jax.ShapeDtypeStruct((rows + 16, 2 * side), F32),
             jax.ShapeDtypeStruct((rows + 8, 2 * side), F32),
+            jax.ShapeDtypeStruct((side, 2 * side), F32),
         ),
-        in_specs=[HBM] * 6,
-        out_specs=(VMEM, VMEM),
-        scratch_shapes=[
-            pltpu.VMEM((ckpts, rows, depth), BF16),
-            pltpu.VMEM((ckpts, rows, width), BF16),
-            pltpu.VMEM((1, rows), jnp.int32),
-            pltpu.VMEM((side, depth), BF16),
-            pltpu.VMEM((side, width), BF16),
-            pltpu.SMEM(weight.shape, F32),
-            pltpu.SemaphoreType.DMA((4 + 2 * chunks,)),
-        ],
-        compiler_params=pltpu.CompilerParams(vmem_limit_bytes=63 * 2**20),
+        in_specs=[VMEM] * 7,
+        out_specs=(VMEM, VMEM, VMEM),
+        compiler_params=pltpu.CompilerParams(vmem_limit_bytes=24 * 2**20),
         cost_estimate=pl.CostEstimate(flops=HEAVY, bytes_accessed=2 * 10**7, transcendentals=0),
         name="project",
-    )(act, grad, ids, pin, pout, weight)
-
-
-def gram_kernel(total, rows, x, *rest):
-    lanes = x.shape[1]
-    side = lanes // 2
-    x = x[0:rows, :]
+    )(act, grad, ids, pin, pout, weight, zero)
+
+
+def factors(x, total):
+    side = x.shape[1] // 2
     g = lax.dot_general(
         x, x, (((0,), (0,)), ((), ())), precision=HIGH, preferred_element_type=F32
     )
-    lane = lax.broadcasted_iota(jnp.int32, (side, lanes), 1)
-    g = jnp.where(lane < side, g[:side], g[side:]) * (1.0 / total)
-    for more in rest[:-1]:
-        g = g + more[...]
-    rest[-1][...] = g
-
-
-def gram(total, rows, cost, x, *more):
-    lanes = x.shape[1]
+    lane = lax.broadcasted_iota(jnp.int32, (side, 2 * side), 1)
+    return jnp.where(lane < side, g[:side], g[side:]) * (1.0 / total)
+
+
+def gram_kernel(total, x, own, out):
+    rows = x.shape[0] - 8
+    out[...] = own[...] + factors(x[0:rows, :], total)
+
+
+def lead_kernel(out):
+    out[...] = jnp.zeros(out.shape, F32)
+
+
+def lead():
     return pl.pallas_call(
-        functools.partial(gram_kernel, total, rows),
-        out_shape=jax.ShapeDtypeStruct((lanes // 2, lanes), F32),
-        in_specs=[VMEM] * (1 + len(more)),
+        lead_kernel,
+        out_shape=jax.ShapeDtypeStruct((8, 128), F32),
         out_specs=VMEM,
-        compiler_params=pltpu.CompilerParams(vmem_limit_bytes=4 * 2**20),
-        cost_estimate=pl.CostEstimate(flops=cost, bytes_accessed=cost // 1000, transcendentals=0),
-        name="gram",
-    )(x, *more)
+        compiler_params=pltpu.CompilerParams(vmem_limit_bytes=2**20),
+        cost_estimate=pl.CostEstimate(flops=HEAVY, bytes_accessed=2 * 10**7, transcendentals=0),
+        name="lead",
+    )()
 
 
 def tick_kernel(*refs):
@@ -190,7 +175,6 @@
 def score_kernel(q_rows, masks, inv, mine, other, queries, keep, send):
     rows, lanes = other.shape[0] - 8, other.shape[1]
     side = lanes // 2
-    ckpt = lax.rem(lax.axis_index("tok"), 2)
     me = lax.axis_index("tok")
     x = jnp.concatenate([mine[0:rows, :], other[0:rows, :]], axis=0)
     lane = lax.broadcasted_iota(jnp.int32, (side, lanes), 1)
@@ -210,7 +194,7 @@
     s_hi, s_lo = s_hi.astype(F32), s_lo.astype(F32)
     example = lax.broadcasted_iota(jnp.int32, (EX_DEV, rows), 0)
     own_ids = mine[rows : rows + 1, :].astype(jnp.int32) - me * EX_DEV
-    near = me + 1 - 2 * ckpt
+    near = me ^ 1
     far_ids = other[rows : rows + 1, :].astype(jnp.int32) - near * EX_DEV
     parts = []
     for block, which in enumerate((own_ids, far_ids)):
@@ -269,19 +253,26 @@
 
     ids = example_ids.reshape(1, rows)
     first = devices // 2
-    arrived = swap(query_sketch, first)
-    mine, send = project(inputs_act, out_grads, ids, proj_in.T, proj_out.T, ckpt_weight)
+    raw, zero = lax.optimization_barrier((query_sketch, lead()))
+    arrived = swap(raw, first)
+    mine, send, own = project(devices, inputs_act, out_grads, ids, proj_in.T, proj_out.T, ckpt_weight[None], zero)
     other = swap(send, 1)
     arrived, mine = lax.optimization_barrier((arrived, mine))
     both = jnp.concatenate([query_sketch, arrived], axis=1)
-    even = lax.rem(me, 2) == 0
+    even = role(me, devices) == 0
     queries = jnp.where(even, both[0], both[1])
     queries = jnp.concatenate([queries, swap(jnp.where(even, both[1], both[0]), 1)], axis=0)
-    g = gram(total, rows, LIGHT, other, gram(total, rows, HEAVY, mine))
-    sums = [first]
-    while sums[-1] > 2:
-        sums.append(sums[-1] // 2)
-    late = sums[:0:-1]
+    g = pl.pallas_call(
+        functools.partial(gram_kernel, total),
+        out_shape=jax.ShapeDtypeStruct((side, 2 * side), F32),
+        in_specs=[VMEM, VMEM],
+        out_specs=VMEM,
+        compiler_params=pltpu.CompilerParams(vmem_limit_bytes=4 * 2**20),
+        name="gram",
+    )(other, tick(HEAVY, own))
+    far = [devices >> k for k in range(1, devices.bit_length() - 2)]
+    sums = [2, *far]
+    late = [*far[:0:-1], 2]
     masks = (first, 1, *late)
     for step, mask in enumerate(sums):
         last = step == len(sums) - 1

time: 33.4 us -> 28.2 us (0.84)
  Pallas kernels: 11.6 us -> 6.27 us
  starting transfers between devices: 10.7 us -> 14.3 us
  waiting for transfers between devices: 8.58 us -> 5.77 us
  local copies, waits for them, and re-layouts: 1.46 us -> 0.82 us
    pallas_call x3, Pallas kernels: 8.49 us -> 3.18 us  [the longest x1 2.92 us: project(): pl.pallas_call(functools.partial(project_kernel, devices), out_shape=(jax...]
    ppermute x9, starting transfers between devices: 10.7 us -> 14.3 us  [swap(): return lax.ppermute(x, 'tok', [(i, i ^ mask) for i in range(devices)])]
    ppermute x9, waiting for transfers between devices: 8.58 us -> 5.77 us  [swap(): return lax.ppermute(x, 'tok', [(i, i ^ mask) for i in range(devices)])]
    unnamed x6 -> x14, local copies, waits for them, and re-layouts: 1.46 us -> 0.82 us
  transfers between devices with their start and end apart: 9 -> 9, of which waited for: 5 -> 7; matrix products, arithmetic and copies ran while one was open for 0% -> 0% of each run, Pallas kernels for 31% -> 18%
where the time goes in v4:
time: 28.2 us; the launch traced here: 28.1 us
  starting transfers between devices  14.3 us (51%)
  Pallas kernels  6.27 us (22%)
  waiting for transfers between devices  5.77 us (20%)
  local copies, waits for them, and re-layouts  0.82 us (3%)
  other arithmetic  0.74 us (3%)
    ppermute x9, starting transfers between devices, swap(): return lax.ppermute(x, 'tok', [(i, i ^ mask) for i in range(devices)])  14.3 us
    ppermute x9, waiting for transfers between devices, swap(): return lax.ppermute(x, 'tok', [(i, i ^ mask) for i in range(devices)])  5.77 us
    pallas_call x1, Pallas kernels, project(): pl.pallas_call(functools.partial(project_kernel, devices), out_shape=(jax...  2.92 us
    pallas_call x1, Pallas kernels, local(): pl.pallas_call(inverse_kernel, out_shape=jax.ShapeDtypeStruct((side, 2 *...  1.83 us
    pallas_call x1, Pallas kernels, local(): pl.pallas_call(functools.partial(score_kernel, q_rows, masks), out_shape=...  1.23 us
    unnamed x14, local copies, waits for them, and re-layouts  0.82 us
    add x1, other arithmetic, local(): return keep + swap(send, 1)  0.6 us
  transfers between devices with their start and end apart: 9, of which 7 were waited for; matrix products, arithmetic and copies ran while one was open for 0% of the time, Pallas kernels for 18%

profile of v4, /device:TPU:0, one launch (start us, length us, event | category | flops | bytes accessed | tf_op | source)
XLA Modules:
  0.0 28.1 jit_solution(9271643195564314334)
XLA Ops:
  0.0 0.0 copy-start.1
  0.0 0.0 copy-start
  0.0 0.8 %copy-done.6 = bf16[2,4,4096]{2,1,0:T(4,128)(2,1)S(1)} copy-done((bf16[2,4,4096]{2,1,0:T(4,128)(2,1)S(1)}, bf16[2,4,4096]{2,1,0:T(4,128)(2,1)}, u32[]{:S(2)}) %copy-start.6) | copy-done | bytes 65560
  0.8 4.0 %collective-permute-start = (bf16[2,4,4096]{2,1,0:T(4,128)(2,1)S(1)}, bf16[2,4,4096]{2,1,0:T(4,128)(2,1)S(1)}, u32[]{:S(2)}, u32[]{:S(2)}) collective-permute-start(bf16[2,4,4096]{2,1,0:T(4,128)(2,1)S(1)} %copy-done.6), channel_id=1, source_target_pairs={{0,8},{1,9},{2,10},{3,11},{4,12},{5,13},{6,14},{7,15},{8,0},{9,1},... | collective-permute-start | bytes 196616 | tf_op jit(solution)/shard_map/ppermute | solution.py:252
  4.9 0.0 copy-done.5
  4.9 0.0 copy-done.3
  4.9 0.0 copy-done.2
  4.9 0.0 copy-done.4
  4.9 0.0 copy-done.1
  4.9 2.9 %project.1 = (f32[144,128]{1,0:T(8,128)S(1)}, f32[136,128]{1,0:T(8,128)S(1)}, f32[64,128]{1,0:T(8,128)S(1)}) custom-call(bf16[2,128,14336]{2,1,0:T(8,128)(2,1)S(1)} %copy-done, bf16[2,128,4096]{2,1,0:T(8,128)(2,1)S(1)} %copy-done.1, s32[1,128]{1,0:T(1,128)S(1)} %bitcast.10, bf16[64,14336]{1,0:T(8,128)(2,1)S(1)} %bitcast.8, bf16[64,4096]{1,0:T(8,128)(2,1)S(1)} %bitcast.9, ...), custom_call_target="tpu_custom_call" | custom-call | flops 20000000000 | bytes 20000000 | tf_op jit(solution)/shard_map/project/pallas_call | solution.py:63
  7.8 0.1 collective-permute-start.2
  8.0 0.6 %collective-permute-done = bf16[2,4,4096]{2,1,0:T(4,128)(2,1)S(1)} collective-permute-done((bf16[2,4,4096]{2,1,0:T(4,128)(2,1)S(1)}, bf16[2,4,4096]{2,1,0:T(4,128)(2,1)S(1)}, u32[]{:S(2)}, u32[]{:S(2)}) %collective-permute-start) | collective-permute-done | bytes 65568 | tf_op jit(solution)/shard_map/ppermute | solution.py:252
  8.5 0.1 select_bitcast_fusion.1
  8.6 0.1 collective-permute-start.1
  8.7 0.5 %collective-permute-done.2.x.other = f32[136,128]{1,0:T(8,128)S(1)} collective-permute-done((f32[136,128]{1,0:T(8,128)S(1)}, f32[136,128]{1,0:T(8,128)S(1)}, u32[]{:S(2)}, u32[]{:S(2)}) %collective-permute-start.2) | collective-permute-done | bytes 69664 | tf_op jit(solution)/shard_map/ppermute | solution.py:252
  9.2 0.3 gram.1.refs_0_
  9.4 2.6 %collective-permute-start.4 = (f32[64,128]{1,0:T(8,128)S(1)}, f32[64,128]{1,0:T(8,128)S(1)}, u32[]{:S(2)}, u32[]{:S(2)}) collective-permute-start(f32[64,128]{1,0:T(8,128)S(1)} %gram.1.refs_0_), channel_id=1, source_target_pairs={{0,2},{1,3},{2,0},{3,1},{4,6},{5,7},{6,4},{7,5},{8,10},{9,11},{10,... | collective-permute-start | bytes 98312 | tf_op jit(solution)/shard_map/ppermute | solution.py:252
  12.1 0.0 collective-permute-done.1
  12.1 1.6 %collective-permute-start.3 = (bf16[16,4096]{1,0:T(8,128)(2,1)S(1)}, bf16[16,4096]{1,0:T(8,128)(2,1)S(1)}, u32[]{:S(2)}, u32[]{:S(2)}) collective-permute-start(bf16[16,4096]{1,0:T(8,128)(2,1)S(1)} %pad_maximum_fusion.2), channel_id=1, source_target_pairs={{0,4},{1,5},{2,6},{3,7},{4,0},{5,1},{6,2},{7,3},{8,12},{9,13},{10,... | collective-permute-start | bytes 393224 | tf_op jit(solution)/shard_map/ppermute | solution.py:252
  13.7 0.2 collective-permute-done.4.refs_1_
  14.0 3.2 %collective-permute-start.5 = (f32[64,128]{1,0:T(8,128)S(1)}, f32[64,128]{1,0:T(8,128)S(1)}, u32[]{:S(2)}, u32[]{:S(2)}) collective-permute-start(f32[64,128]{1,0:T(8,128)S(1)} %tick.8.refs_0_), channel_id=1, source_target_pairs={{0,8},{1,9},{2,10},{3,11},{4,12},{5,13},{6,14},{7,15},{8,0},{9,1},... | collective-permute-start | bytes 98312 | tf_op jit(solution)/shard_map/ppermute | solution.py:252
  17.1 0.6 %collective-permute-done.3 = bf16[16,4096]{1,0:T(8,128)(2,1)S(1)} collective-permute-done((bf16[16,4096]{1,0:T(8,128)(2,1)S(1)}, bf16[16,4096]{1,0:T(8,128)(2,1)S(1)}, u32[]{:S(2)}, u32[]{:S(2)}) %collective-permute-start.3) | collective-permute-done | bytes 131104 | tf_op jit(solution)/shard_map/ppermute | solution.py:252
  17.8 0.9 %collective-permute-start.7 = (bf16[32,4096]{1,0:T(8,128)(2,1)S(1)}, bf16[32,4096]{1,0:T(8,128)(2,1)S(1)}, u32[]{:S(2)}, u32[]{:S(2)}) collective-permute-start(bf16[32,4096]{1,0:T(8,128)(2,1)S(1)} %pad_maximum_fusion.1), channel_id=1, source_target_pairs={{0,2},{1,3},{2,0},{3,1},{4,6},{5,7},{6,4},{7,5},{8,10},{9,11},{10,... | collective-permute-start | bytes 786440 | tf_op jit(solution)/shard_map/ppermute | solution.py:252
  18.8 0.5 %collective-permute-done.5.refs_1_ = f32[64,128]{1,0:T(8,128)S(1)} collective-permute-done((f32[64,128]{1,0:T(8,128)S(1)}, f32[64,128]{1,0:T(8,128)S(1)}, u32[]{:S(2)}, u32[]{:S(2)}) %collective-permute-start.5) | collective-permute-done | bytes 32800 | tf_op jit(solution)/shard_map/ppermute | solution.py:252
  19.2 1.7 %collective-permute-start.6 = (f32[64,128]{1,0:T(8,128)S(1)}, f32[64,128]{1,0:T(8,128)S(1)}, u32[]{:S(2)}, u32[]{:S(2)}) collective-permute-start(f32[64,128]{1,0:T(8,128)S(1)} %tick.10.refs_0_), channel_id=1, source_target_pairs={{0,4},{1,5},{2,6},{3,7},{4,0},{5,1},{6,2},{7,3},{8,12},{9,13},{10,... | collective-permute-start | bytes 98312 | tf_op jit(solution)/shard_map/ppermute | solution.py:252
  21.0 2.2 %collective-permute-done.6.refs_1_ = f32[64,128]{1,0:T(8,128)S(1)} collective-permute-done((f32[64,128]{1,0:T(8,128)S(1)}, f32[64,128]{1,0:T(8,128)S(1)}, u32[]{:S(2)}, u32[]{:S(2)}) %collective-permute-start.6) | collective-permute-done | bytes 32800 | tf_op jit(solution)/shard_map/ppermute | solution.py:252
  23.2 1.8 %inverse.1.inv = f32[64,128]{1,0:T(8,128)S(1)} custom-call(f32[64,128]{1,0:T(8,128)S(1)} %tick.11.g), custom_call_target="tpu_custom_call" | custom-call | tf_op jit(solution)/shard_map/inverse/pallas_call | solution.py:284
  25.0 0.0 collective-permute-done.7
  25.0 1.2 %score.1 = (f32[16,64]{1,0:T(8,128)S(1)}, f32[16,64]{1,0:T(8,128)S(1)}) custom-call(f32[64,128]{1,0:T(8,128)S(1)} %inverse.1.inv, f32[144,128]{1,0:T(8,128)S(1)} %get-tuple-element.27.mine, f32[136,128]{1,0:T(8,128)S(1)} %collective-permute-done.2.x.other, bf16[64,4096]{1,0:T(8,128)(2,1)S(1)} %pad_maximum_fusion.queries), custom_call_target="tpu_custom_call" | custom-call | tf_op jit(solution)/shard_map/score/pallas_call | solution.py:292
  26.3 0.0 collective-permute-start.8
  26.3 1.2 %collective-permute-done.8 = f32[16,64]{1,0:T(8,128)S(1)} collective-permute-done((f32[16,64]{1,0:T(8,128)S(1)}, f32[16,64]{1,0:T(8,128)S(1)}, u32[]{:S(2)}, u32[]{:S(2)}) %collective-permute-start.8) | collective-permute-done | bytes 4128 | tf_op jit(solution)/shard_map/ppermute | solution.py:252
  27.5 0.6 %add.3 = f32[16,64]{1,0:T(8,128)} add(f32[16,64]{1,0:T(8,128)S(1)} %get-tuple-element.29, f32[16,64]{1,0:T(8,128)S(1)} %collective-permute-done.8) | non-fusion elementwise | flops 1024 | bytes 12288 | tf_op jit(solution)/shard_map/add | solution.py:303
  (16 shorter events, 0.1 us)
Async XLA Ops:
  0.0 0.8 %copy-start.6 = (bf16[2,4,4096]{2,1,0:T(4,128)(2,1)S(1)}, bf16[2,4,4096]{2,1,0:T(4,128)(2,1)}, u32[]{:S(2)}) copy-start(bf16[2,4,4096]{2,1,0:T(4,128)(2,1)} %param.12) | copy-start | bytes 196612
  0.0 4.9 %copy-start.5 = (f32[2]{0:T(128)S(1)}, f32[2]{0:T(128)}, u32[]{:S(2)}) copy-start(f32[2]{0:T(128)} %param.13) | copy-start | bytes 28
  0.0 4.9 %copy-start.3 = (bf16[4096,64]{0,1:T(8,128)(2,1)S(1)}, bf16[4096,64]{0,1:T(8,128)(2,1)}, u32[]{:S(2)}) copy-start(bf16[4096,64]{0,1:T(8,128)(2,1)} %param.11) | copy-start | bytes 1572868
  0.0 4.9 %copy-start.2 = (bf16[14336,64]{0,1:T(8,128)(2,1)S(1)}, bf16[14336,64]{0,1:T(8,128)(2,1)}, u32[]{:S(2)}) copy-start(bf16[14336,64]{0,1:T(8,128)(2,1)} %param.10) | copy-start | bytes 5505028
  0.0 4.9 %copy-start.4 = (s32[128]{0:T(128)S(1)}, s32[128]{0:T(128)}, u32[]{:S(2)}) copy-start(s32[128]{0:T(128)} %param.9) | copy-start | bytes 1540
  0.0 4.9 %copy-start.1 = (bf16[2,128,4096]{2,1,0:T(8,128)(2,1)S(1)}, bf16[2,128,4096]{2,1,0:T(8,128)(2,1)}, u32[]{:S(2)}) copy-start(bf16[2,128,4096]{2,1,0:T(8,128)(2,1)} %grad.1) | copy-start | bytes 6291460
  0.0 4.9 %copy-start = (bf16[2,128,14336]{2,1,0:T(8,128)(2,1)S(1)}, bf16[2,128,14336]{2,1,0:T(8,128)(2,1)}, u32[]{:S(2)}) copy-start(bf16[2,128,14336]{2,1,0:T(8,128)(2,1)} %act.1) | copy-start | bytes 22020100
  0.8 7.7 %collective-permute-start = (bf16[2,4,4096]{2,1,0:T(4,128)(2,1)S(1)}, bf16[2,4,4096]{2,1,0:T(4,128)(2,1)S(1)}, u32[]{:S(2)}, u32[]{:S(2)}) collective-permute-start(bf16[2,4,4096]{2,1,0:T(4,128)(2,1)S(1)} %copy-done.6), channel_id=1, source_target_pairs={{0,8},{1,9},{2,10},{3,11},{4,12},{5,13},{6,14},{7,15},{8,0},{9,1},... | collective-permute-start | bytes 196616 | tf_op jit(solution)/shard_map/ppermute | solution.py:252
  7.8 1.3 %collective-permute-start.2 = (f32[136,128]{1,0:T(8,128)S(1)}, f32[136,128]{1,0:T(8,128)S(1)}, u32[]{:S(2)}, u32[]{:S(2)}) collective-permute-start(f32[136,128]{1,0:T(8,128)S(1)} %get-tuple-element.22), channel_id=1, source_target_pairs={{0,1},{1,0},{2,3},{3,2},{4,5},{5,4},{6,7},{7,6},{8,9},{9,8},{10,11... | collective-permute-start | bytes 208904 | tf_op jit(solution)/shard_map/ppermute | solution.py:252
  8.6 3.5 %collective-permute-start.1 = (bf16[8,4096]{1,0:T(8,128)(2,1)S(1)}, bf16[8,4096]{1,0:T(8,128)(2,1)S(1)}, u32[]{:S(2)}, u32[]{:S(2)}) collective-permute-start(bf16[8,4096]{1,0:T(8,128)(2,1)S(1)} %get-tuple-element.32), channel_id=1, source_target_pairs={{0,1},{1,0},{2,3},{3,2},{4,5},{5,4},{6,7},{7,6},{8,9},{9,8},{10,11... | collective-permute-start | bytes 196616 | tf_op jit(solution)/shard_map/ppermute | solution.py:252
  9.4 4.5 %collective-permute-start.4 = (f32[64,128]{1,0:T(8,128)S(1)}, f32[64,128]{1,0:T(8,128)S(1)}, u32[]{:S(2)}, u32[]{:S(2)}) collective-permute-start(f32[64,128]{1,0:T(8,128)S(1)} %gram.1.refs_0_), channel_id=1, source_target_pairs={{0,2},{1,3},{2,0},{3,1},{4,6},{5,7},{6,4},{7,5},{8,10},{9,11},{10,... | collective-permute-start | bytes 98312 | tf_op jit(solution)/shard_map/ppermute | solution.py:252
  12.1 5.7 %collective-permute-start.3 = (bf16[16,4096]{1,0:T(8,128)(2,1)S(1)}, bf16[16,4096]{1,0:T(8,128)(2,1)S(1)}, u32[]{:S(2)}, u32[]{:S(2)}) collective-permute-start(bf16[16,4096]{1,0:T(8,128)(2,1)S(1)} %pad_maximum_fusion.2), channel_id=1, source_target_pairs={{0,4},{1,5},{2,6},{3,7},{4,0},{5,1},{6,2},{7,3},{8,12},{9,13},{10,... | collective-permute-start | bytes 393224 | tf_op jit(solution)/shard_map/ppermute | solution.py:252
  14.0 5.2 %collective-permute-start.5 = (f32[64,128]{1,0:T(8,128)S(1)}, f32[64,128]{1,0:T(8,128)S(1)}, u32[]{:S(2)}, u32[]{:S(2)}) collective-permute-start(f32[64,128]{1,0:T(8,128)S(1)} %tick.8.refs_0_), channel_id=1, source_target_pairs={{0,8},{1,9},{2,10},{3,11},{4,12},{5,13},{6,14},{7,15},{8,0},{9,1},... | collective-permute-start | bytes 98312 | tf_op jit(solution)/shard_map/ppermute | solution.py:252
  17.8 7.2 %collective-permute-start.7 = (bf16[32,4096]{1,0:T(8,128)(2,1)S(1)}, bf16[32,4096]{1,0:T(8,128)(2,1)S(1)}, u32[]{:S(2)}, u32[]{:S(2)}) collective-permute-start(bf16[32,4096]{1,0:T(8,128)(2,1)S(1)} %pad_maximum_fusion.1), channel_id=1, source_target_pairs={{0,2},{1,3},{2,0},{3,1},{4,6},{5,7},{6,4},{7,5},{8,10},{9,11},{10,... | collective-permute-start | bytes 786440 | tf_op jit(solution)/shard_map/ppermute | solution.py:252
  19.2 3.9 %collective-permute-start.6 = (f32[64,128]{1,0:T(8,128)S(1)}, f32[64,128]{1,0:T(8,128)S(1)}, u32[]{:S(2)}, u32[]{:S(2)}) collective-permute-start(f32[64,128]{1,0:T(8,128)S(1)} %tick.10.refs_0_), channel_id=1, source_target_pairs={{0,4},{1,5},{2,6},{3,7},{4,0},{5,1},{6,2},{7,3},{8,12},{9,13},{10,... | collective-permute-start | bytes 98312 | tf_op jit(solution)/shard_map/ppermute | solution.py:252
  26.3 1.2 %collective-permute-start.8 = (f32[16,64]{1,0:T(8,128)S(1)}, f32[16,64]{1,0:T(8,128)S(1)}, u32[]{:S(2)}, u32[]{:S(2)}) collective-permute-start(f32[16,64]{1,0:T(8,128)S(1)} %get-tuple-element.30), channel_id=1, source_target_pairs={{0,1},{1,0},{2,3},{3,2},{4,5},{5,4},{6,7},{7,6},{8,9},{9,8},{10,11... | collective-permute-start | bytes 12296 | tf_op jit(solution)/shard_map/ppermute | solution.py:252

commit v5 on v4

--- a/solution.py
+++ b/solution.py
@@ -27,7 +27,27 @@
     )
 
 
-def project_kernel(devices, act, grad, ids, pin, pout, weight, zero, keep, send, own):
+def side_kernel(grad, pout, out):
+    ckpts, rows, _ = grad.shape
+    half = rows // 2
+    for j in range(2 * ckpts):
+        piece = grad[j // 2, (j % 2) * half : (j % 2 + 1) * half, :]
+        out[j * half : (j + 1) * half, :] = nt(piece, pout[...])
+
+
+def grad_side(grad, pout):
+    return pl.pallas_call(
+        side_kernel,
+        out_shape=jax.ShapeDtypeStruct((grad.shape[0] * grad.shape[1], pout.shape[0]), F32),
+        in_specs=[VMEM, VMEM],
+        out_specs=VMEM,
+        compiler_params=pltpu.CompilerParams(vmem_limit_bytes=8 * 2**20),
+        cost_estimate=pl.CostEstimate(flops=LIGHT, bytes_accessed=1000, transcendentals=0),
+        name="grad_side",
+    )(grad, pout)
+
+
+def project_kernel(devices, act, ids, pin, s_all, weight, zero, keep, send, own):
     ckpts, rows, _ = act.shape
     side = pin.shape[0]
     half = rows // 2
@@ -37,7 +57,7 @@
             nt(x[c, h * half : (h + 1) * half, :], w[...]) for c in range(ckpts) for h in range(2)
         ]
 
-    s = dots(grad, pout)
+    s = [s_all[j * half : (j + 1) * half, :] for j in range(2 * ckpts)]
     a = dots(act, pin)
     first, second = (
         jnp.concatenate(
@@ -60,6 +80,7 @@
 def project(devices, act, grad, ids, pin, pout, weight, zero):
     rows = act.shape[1]
     side = pout.shape[0]
+    s_all = grad_side(grad, pout)
     return pl.pallas_call(
         functools.partial(project_kernel, devices),
         out_shape=(
@@ -67,12 +88,12 @@
             jax.ShapeDtypeStruct((rows + 8, 2 * side), F32),
             jax.ShapeDtypeStruct((side, 2 * side), F32),
         ),
-        in_specs=[VMEM] * 7,
+        in_specs=[VMEM] * 6,
         out_specs=(VMEM, VMEM, VMEM),
         compiler_params=pltpu.CompilerParams(vmem_limit_bytes=24 * 2**20),
         cost_estimate=pl.CostEstimate(flops=HEAVY, bytes_accessed=2 * 10**7, transcendentals=0),
         name="project",
-    )(act, grad, ids, pin, pout, weight, zero)
+    )(act, ids, pin, s_all, weight, zero)
 
 
 def factors(x, total):

time: 28.2 us -> 27.8 us (0.986)
  starting transfers between devices: 14.3 us -> 13.7 us
    ppermute x9, starting transfers between devices: 14.3 us -> 13.7 us  [swap(): return lax.ppermute(x, 'tok', [(i, i ^ mask) for i in range(devices)])]
    pallas_call x0 -> x1, Pallas kernels: none -> 0.67 us  [grad_side(): pl.pallas_call(side_kernel, out_shape=jax.ShapeDtypeStruct((grad.shape[0]...]
    pallas_call x1, Pallas kernels: 2.92 us -> 2.37 us  [project(): pl.pallas_call(functools.partial(project_kernel, devices), out_shape=(jax...]
  transfers between devices with their start and end apart: 9 -> 9, of which waited for: 7 -> 7; matrix products, arithmetic and copies ran while one was open for 0% -> 0% of each run, Pallas kernels for 18% -> 19%
where the time goes in v5:
time: 27.8 us; the launch traced here: 27.6 us
  starting transfers between devices  13.7 us (49%)
  Pallas kernels  6.39 us (23%)
  waiting for transfers between devices  5.83 us (21%)
  local copies, waits for them, and re-layouts  0.87 us (3%)
  other arithmetic  0.74 us (3%)
    ppermute x9, starting transfers between devices, swap(): return lax.ppermute(x, 'tok', [(i, i ^ mask) for i in range(devices)])  13.7 us
    ppermute x9, waiting for transfers between devices, swap(): return lax.ppermute(x, 'tok', [(i, i ^ mask) for i in range(devices)])  5.83 us
    pallas_call x1, Pallas kernels, project(): pl.pallas_call(functools.partial(project_kernel, devices), out_shape=(jax...  2.37 us
    pallas_call x1, Pallas kernels, local(): pl.pallas_call(inverse_kernel, out_shape=jax.ShapeDtypeStruct((side, 2 *...  1.83 us
    pallas_call x1, Pallas kernels, local(): pl.pallas_call(functools.partial(score_kernel, q_rows, masks), out_shape=...  1.24 us
    unnamed x14, local copies, waits for them, and re-layouts  0.87 us
    pallas_call x1, Pallas kernels, grad_side(): pl.pallas_call(side_kernel, out_shape=jax.ShapeDtypeStruct((grad.shape[0]...  0.67 us
    add x1, other arithmetic, local(): return keep + swap(send, 1)  0.6 us
  transfers between devices with their start and end apart: 9, of which 7 were waited for; matrix products, arithmetic and copies ran while one was open for 0% of the time, Pallas kernels for 19%

profile of v5, /device:TPU:0, one launch (start us, length us, event | category | flops | bytes accessed | tf_op | source)
XLA Modules:
  0.0 27.6 jit_solution(4397991159068470230)
XLA Ops:
  0.0 0.8 %copy-done.6 = bf16[2,4,4096]{2,1,0:T(4,128)(2,1)S(1)} copy-done((bf16[2,4,4096]{2,1,0:T(4,128)(2,1)S(1)}, bf16[2,4,4096]{2,1,0:T(4,128)(2,1)}, u32[]{:S(2)}) %copy-start.6) | copy-done | bytes 65560
  0.8 4.0 %collective-permute-start = (bf16[2,4,4096]{2,1,0:T(4,128)(2,1)S(1)}, bf16[2,4,4096]{2,1,0:T(4,128)(2,1)S(1)}, u32[]{:S(2)}, u32[]{:S(2)}) collective-permute-start(bf16[2,4,4096]{2,1,0:T(4,128)(2,1)S(1)} %copy-done.6), channel_id=1, source_target_pairs={{0,8},{1,9},{2,10},{3,11},{4,12},{5,13},{6,14},{7,15},{8,0},{9,1},... | collective-permute-start | bytes 196616 | tf_op jit(solution)/shard_map/ppermute | solution.py:273
  4.9 0.0 copy-done.1
  4.9 0.0 copy-done
  4.9 0.7 %grad_side.1.s_all = f32[256,64]{1,0:T(8,128)S(1)} custom-call(bf16[2,128,4096]{2,1,0:T(8,128)(2,1)S(1)} %copy-done, bf16[64,4096]{1,0:T(8,128)(2,1)S(1)} %bitcast.8), custom_call_target="tpu_custom_call" | custom-call | flops 1000000 | bytes 1000 | tf_op jit(solution)/shard_map/grad_side/pallas_call | solution.py:39
  5.6 0.0 copy-done.2
  5.6 0.0 copy-done.3
  5.6 0.0 copy-done.4
  5.6 0.0 copy-done.5
  5.6 2.4 %project.1 = (f32[144,128]{1,0:T(8,128)S(1)}, f32[136,128]{1,0:T(8,128)S(1)}, f32[64,128]{1,0:T(8,128)S(1)}) custom-call(bf16[2,128,14336]{2,1,0:T(8,128)(2,1)S(1)} %copy-done.2, s32[1,128]{1,0:T(1,128)S(1)} %bitcast.10, bf16[64,14336]{1,0:T(8,128)(2,1)S(1)} %bitcast.9, f32[256,64]{1,0:T(8,128)S(1)} %grad_side.1.s_all, f32[1,2]{1,0:T(1,128)S(1)} %bitcast.11, ...), custom_call_target="tpu_custom_call" | custom-call | flops 20000000000 | bytes 20000000 | tf_op jit(solution)/shard_map/project/pallas_call | solution.py:84
  8.0 0.1 collective-permute-start.2
  8.1 0.4 %collective-permute-done = bf16[2,4,4096]{2,1,0:T(4,128)(2,1)S(1)} collective-permute-done((bf16[2,4,4096]{2,1,0:T(4,128)(2,1)S(1)}, bf16[2,4,4096]{2,1,0:T(4,128)(2,1)S(1)}, u32[]{:S(2)}, u32[]{:S(2)}) %collective-permute-start) | collective-permute-done | bytes 65568 | tf_op jit(solution)/shard_map/ppermute | solution.py:273
  8.5 0.1 select_bitcast_fusion.1
  8.6 0.1 collective-permute-start.1
  8.7 0.6 %collective-permute-done.2.x.other = f32[136,128]{1,0:T(8,128)S(1)} collective-permute-done((f32[136,128]{1,0:T(8,128)S(1)}, f32[136,128]{1,0:T(8,128)S(1)}, u32[]{:S(2)}, u32[]{:S(2)}) %collective-permute-start.2) | collective-permute-done | bytes 69664 | tf_op jit(solution)/shard_map/ppermute | solution.py:273
  9.3 0.3 gram.1.refs_0_
  9.6 2.0 %collective-permute-start.4 = (f32[64,128]{1,0:T(8,128)S(1)}, f32[64,128]{1,0:T(8,128)S(1)}, u32[]{:S(2)}, u32[]{:S(2)}) collective-permute-start(f32[64,128]{1,0:T(8,128)S(1)} %gram.1.refs_0_), channel_id=1, source_target_pairs={{0,2},{1,3},{2,0},{3,1},{4,6},{5,7},{6,4},{7,5},{8,10},{9,11},{10,... | collective-permute-start | bytes 98312 | tf_op jit(solution)/shard_map/ppermute | solution.py:273
  11.6 0.0 collective-permute-done.1
  11.6 1.6 %collective-permute-start.3 = (bf16[16,4096]{1,0:T(8,128)(2,1)S(1)}, bf16[16,4096]{1,0:T(8,128)(2,1)S(1)}, u32[]{:S(2)}, u32[]{:S(2)}) collective-permute-start(bf16[16,4096]{1,0:T(8,128)(2,1)S(1)} %pad_maximum_fusion.2), channel_id=1, source_target_pairs={{0,4},{1,5},{2,6},{3,7},{4,0},{5,1},{6,2},{7,3},{8,12},{9,13},{10,... | collective-permute-start | bytes 393224 | tf_op jit(solution)/shard_map/ppermute | solution.py:273
  13.3 0.3 %collective-permute-done.4.refs_1_ = f32[64,128]{1,0:T(8,128)S(1)} collective-permute-done((f32[64,128]{1,0:T(8,128)S(1)}, f32[64,128]{1,0:T(8,128)S(1)}, u32[]{:S(2)}, u32[]{:S(2)}) %collective-permute-start.4) | collective-permute-done | bytes 32800 | tf_op jit(solution)/shard_map/ppermute | solution.py:273
  13.6 3.1 %collective-permute-start.5 = (f32[64,128]{1,0:T(8,128)S(1)}, f32[64,128]{1,0:T(8,128)S(1)}, u32[]{:S(2)}, u32[]{:S(2)}) collective-permute-start(f32[64,128]{1,0:T(8,128)S(1)} %tick.8.refs_0_), channel_id=1, source_target_pairs={{0,8},{1,9},{2,10},{3,11},{4,12},{5,13},{6,14},{7,15},{8,0},{9,1},... | collective-permute-start | bytes 98312 | tf_op jit(solution)/shard_map/ppermute | solution.py:273
  16.7 0.6 %collective-permute-done.3 = bf16[16,4096]{1,0:T(8,128)(2,1)S(1)} collective-permute-done((bf16[16,4096]{1,0:T(8,128)(2,1)S(1)}, bf16[16,4096]{1,0:T(8,128)(2,1)S(1)}, u32[]{:S(2)}, u32[]{:S(2)}) %collective-permute-start.3) | collective-permute-done | bytes 131104 | tf_op jit(solution)/shard_map/ppermute | solution.py:273
  17.4 0.9 %collective-permute-start.7 = (bf16[32,4096]{1,0:T(8,128)(2,1)S(1)}, bf16[32,4096]{1,0:T(8,128)(2,1)S(1)}, u32[]{:S(2)}, u32[]{:S(2)}) collective-permute-start(bf16[32,4096]{1,0:T(8,128)(2,1)S(1)} %pad_maximum_fusion.1), channel_id=1, source_target_pairs={{0,2},{1,3},{2,0},{3,1},{4,6},{5,7},{6,4},{7,5},{8,10},{9,11},{10,... | collective-permute-start | bytes 786440 | tf_op jit(solution)/shard_map/ppermute | solution.py:273
  18.3 0.5 %collective-permute-done.5.refs_1_ = f32[64,128]{1,0:T(8,128)S(1)} collective-permute-done((f32[64,128]{1,0:T(8,128)S(1)}, f32[64,128]{1,0:T(8,128)S(1)}, u32[]{:S(2)}, u32[]{:S(2)}) %collective-permute-start.5) | collective-permute-done | bytes 32800 | tf_op jit(solution)/shard_map/ppermute | solution.py:273
  18.8 1.7 %collective-permute-start.6 = (f32[64,128]{1,0:T(8,128)S(1)}, f32[64,128]{1,0:T(8,128)S(1)}, u32[]{:S(2)}, u32[]{:S(2)}) collective-permute-start(f32[64,128]{1,0:T(8,128)S(1)} %tick.10.refs_0_), channel_id=1, source_target_pairs={{0,4},{1,5},{2,6},{3,7},{4,0},{5,1},{6,2},{7,3},{8,12},{9,13},{10,... | collective-permute-start | bytes 98312 | tf_op jit(solution)/shard_map/ppermute | solution.py:273
  20.5 2.2 %collective-permute-done.6.refs_1_ = f32[64,128]{1,0:T(8,128)S(1)} collective-permute-done((f32[64,128]{1,0:T(8,128)S(1)}, f32[64,128]{1,0:T(8,128)S(1)}, u32[]{:S(2)}, u32[]{:S(2)}) %collective-permute-start.6) | collective-permute-done | bytes 32800 | tf_op jit(solution)/shard_map/ppermute | solution.py:273
  22.7 1.8 %inverse.1.inv = f32[64,128]{1,0:T(8,128)S(1)} custom-call(f32[64,128]{1,0:T(8,128)S(1)} %tick.11.g), custom_call_target="tpu_custom_call" | custom-call | tf_op jit(solution)/shard_map/inverse/pallas_call | solution.py:305
  24.5 0.0 collective-permute-done.7
  24.6 1.2 %score.1 = (f32[16,64]{1,0:T(8,128)S(1)}, f32[16,64]{1,0:T(8,128)S(1)}) custom-call(f32[64,128]{1,0:T(8,128)S(1)} %inverse.1.inv, f32[144,128]{1,0:T(8,128)S(1)} %get-tuple-element.27.mine, f32[136,128]{1,0:T(8,128)S(1)} %collective-permute-done.2.x.other, bf16[64,4096]{1,0:T(8,128)(2,1)S(1)} %pad_maximum_fusion.queries), custom_call_target="tpu_custom_call" | custom-call | tf_op jit(solution)/shard_map/score/pallas_call | solution.py:313
  25.8 0.0 collective-permute-start.8
  25.8 1.2 %collective-permute-done.8 = f32[16,64]{1,0:T(8,128)S(1)} collective-permute-done((f32[16,64]{1,0:T(8,128)S(1)}, f32[16,64]{1,0:T(8,128)S(1)}, u32[]{:S(2)}, u32[]{:S(2)}) %collective-permute-start.8) | collective-permute-done | bytes 4128 | tf_op jit(solution)/shard_map/ppermute | solution.py:273
  27.0 0.6 %add.3 = f32[16,64]{1,0:T(8,128)} add(f32[16,64]{1,0:T(8,128)S(1)} %get-tuple-element.29, f32[16,64]{1,0:T(8,128)S(1)} %collective-permute-done.8) | non-fusion elementwise | flops 1024 | bytes 12288 | tf_op jit(solution)/shard_map/add | solution.py:324
  (17 shorter events, 0.1 us)
Async XLA Ops:
  0.0 0.8 %copy-start.6 = (bf16[2,4,4096]{2,1,0:T(4,128)(2,1)S(1)}, bf16[2,4,4096]{2,1,0:T(4,128)(2,1)}, u32[]{:S(2)}) copy-start(bf16[2,4,4096]{2,1,0:T(4,128)(2,1)} %param.12) | copy-start | bytes 196612
  0.0 4.9 %copy-start.1 = (bf16[4096,64]{0,1:T(8,128)(2,1)S(1)}, bf16[4096,64]{0,1:T(8,128)(2,1)}, u32[]{:S(2)}) copy-start(bf16[4096,64]{0,1:T(8,128)(2,1)} %param.11) | copy-start | bytes 1572868
  0.0 4.9 %copy-start = (bf16[2,128,4096]{2,1,0:T(8,128)(2,1)S(1)}, bf16[2,128,4096]{2,1,0:T(8,128)(2,1)}, u32[]{:S(2)}) copy-start(bf16[2,128,4096]{2,1,0:T(8,128)(2,1)} %grad.1) | copy-start | bytes 6291460
  0.0 5.6 %copy-start.2 = (bf16[2,128,14336]{2,1,0:T(8,128)(2,1)S(1)}, bf16[2,128,14336]{2,1,0:T(8,128)(2,1)}, u32[]{:S(2)}) copy-start(bf16[2,128,14336]{2,1,0:T(8,128)(2,1)} %act.1) | copy-start | bytes 22020100
  0.8 4.7 %copy-start.3 = (bf16[14336,64]{0,1:T(8,128)(2,1)S(1)}, bf16[14336,64]{0,1:T(8,128)(2,1)}, u32[]{:S(2)}) copy-start(bf16[14336,64]{0,1:T(8,128)(2,1)} %param.10) | copy-start | bytes 5505028
  0.8 4.8 %copy-start.4 = (s32[128]{0:T(128)S(1)}, s32[128]{0:T(128)}, u32[]{:S(2)}) copy-start(s32[128]{0:T(128)} %param.9) | copy-start | bytes 1540
  0.8 4.8 %copy-start.5 = (f32[2]{0:T(128)S(1)}, f32[2]{0:T(128)}, u32[]{:S(2)}) copy-start(f32[2]{0:T(128)} %param.13) | copy-start | bytes 28
  0.8 7.7 %collective-permute-start = (bf16[2,4,4096]{2,1,0:T(4,128)(2,1)S(1)}, bf16[2,4,4096]{2,1,0:T(4,128)(2,1)S(1)}, u32[]{:S(2)}, u32[]{:S(2)}) collective-permute-start(bf16[2,4,4096]{2,1,0:T(4,128)(2,1)S(1)} %copy-done.6), channel_id=1, source_target_pairs={{0,8},{1,9},{2,10},{3,11},{4,12},{5,13},{6,14},{7,15},{8,0},{9,1},... | collective-permute-start | bytes 196616 | tf_op jit(solution)/shard_map/ppermute | solution.py:273
  8.0 1.3 %collective-permute-start.2 = (f32[136,128]{1,0:T(8,128)S(1)}, f32[136,128]{1,0:T(8,128)S(1)}, u32[]{:S(2)}, u32[]{:S(2)}) collective-permute-start(f32[136,128]{1,0:T(8,128)S(1)} %get-tuple-element.22), channel_id=1, source_target_pairs={{0,1},{1,0},{2,3},{3,2},{4,5},{5,4},{6,7},{7,6},{8,9},{9,8},{10,11... | collective-permute-start | bytes 208904 | tf_op jit(solution)/shard_map/ppermute | solution.py:273
  8.6 3.0 %collective-permute-start.1 = (bf16[8,4096]{1,0:T(8,128)(2,1)S(1)}, bf16[8,4096]{1,0:T(8,128)(2,1)S(1)}, u32[]{:S(2)}, u32[]{:S(2)}) collective-permute-start(bf16[8,4096]{1,0:T(8,128)(2,1)S(1)} %get-tuple-element.32), channel_id=1, source_target_pairs={{0,1},{1,0},{2,3},{3,2},{4,5},{5,4},{6,7},{7,6},{8,9},{9,8},{10,11... | collective-permute-start | bytes 196616 | tf_op jit(solution)/shard_map/ppermute | solution.py:273
  9.6 4.0 %collective-permute-start.4 = (f32[64,128]{1,0:T(8,128)S(1)}, f32[64,128]{1,0:T(8,128)S(1)}, u32[]{:S(2)}, u32[]{:S(2)}) collective-permute-start(f32[64,128]{1,0:T(8,128)S(1)} %gram.1.refs_0_), channel_id=1, source_target_pairs={{0,2},{1,3},{2,0},{3,1},{4,6},{5,7},{6,4},{7,5},{8,10},{9,11},{10,... | collective-permute-start | bytes 98312 | tf_op jit(solution)/shard_map/ppermute | solution.py:273
  11.6 5.7 %collective-permute-start.3 = (bf16[16,4096]{1,0:T(8,128)(2,1)S(1)}, bf16[16,4096]{1,0:T(8,128)(2,1)S(1)}, u32[]{:S(2)}, u32[]{:S(2)}) collective-permute-start(bf16[16,4096]{1,0:T(8,128)(2,1)S(1)} %pad_maximum_fusion.2), channel_id=1, source_target_pairs={{0,4},{1,5},{2,6},{3,7},{4,0},{5,1},{6,2},{7,3},{8,12},{9,13},{10,... | collective-permute-start | bytes 393224 | tf_op jit(solution)/shard_map/ppermute | solution.py:273
  13.6 5.2 %collective-permute-start.5 = (f32[64,128]{1,0:T(8,128)S(1)}, f32[64,128]{1,0:T(8,128)S(1)}, u32[]{:S(2)}, u32[]{:S(2)}) collective-permute-start(f32[64,128]{1,0:T(8,128)S(1)} %tick.8.refs_0_), channel_id=1, source_target_pairs={{0,8},{1,9},{2,10},{3,11},{4,12},{5,13},{6,14},{7,15},{8,0},{9,1},... | collective-permute-start | bytes 98312 | tf_op jit(solution)/shard_map/ppermute | solution.py:273
  17.4 7.2 %collective-permute-start.7 = (bf16[32,4096]{1,0:T(8,128)(2,1)S(1)}, bf16[32,4096]{1,0:T(8,128)(2,1)S(1)}, u32[]{:S(2)}, u32[]{:S(2)}) collective-permute-start(bf16[32,4096]{1,0:T(8,128)(2,1)S(1)} %pad_maximum_fusion.1), channel_id=1, source_target_pairs={{0,2},{1,3},{2,0},{3,1},{4,6},{5,7},{6,4},{7,5},{8,10},{9,11},{10,... | collective-permute-start | bytes 786440 | tf_op jit(solution)/shard_map/ppermute | solution.py:273
  18.8 3.9 %collective-permute-start.6 = (f32[64,128]{1,0:T(8,128)S(1)}, f32[64,128]{1,0:T(8,128)S(1)}, u32[]{:S(2)}, u32[]{:S(2)}) collective-permute-start(f32[64,128]{1,0:T(8,128)S(1)} %tick.10.refs_0_), channel_id=1, source_target_pairs={{0,4},{1,5},{2,6},{3,7},{4,0},{5,1},{6,2},{7,3},{8,12},{9,13},{10,... | collective-permute-start | bytes 98312 | tf_op jit(solution)/shard_map/ppermute | solution.py:273
  25.8 1.2 %collective-permute-start.8 = (f32[16,64]{1,0:T(8,128)S(1)}, f32[16,64]{1,0:T(8,128)S(1)}, u32[]{:S(2)}, u32[]{:S(2)}) collective-permute-start(f32[16,64]{1,0:T(8,128)S(1)} %get-tuple-element.30), channel_id=1, source_target_pairs={{0,1},{1,0},{2,3},{3,2},{4,5},{5,4},{6,7},{7,6},{8,9},{9,8},{10,11... | collective-permute-start | bytes 12296 | tf_op jit(solution)/shard_map/ppermute | solution.py:273

commit v6 on v5

--- a/solution.py
+++ b/solution.py
@@ -18,7 +18,10 @@
 
 
 def role(me, devices):
-    return me & 1
+    bit = me
+    for shift in range(1, devices.bit_length() - 1):
+        bit = bit ^ (me >> shift)
+    return bit & 1
 
 
 def nt(x, y, precision=None):
@@ -193,7 +196,7 @@
     return hi, (x - hi.astype(F32)).astype(BF16)
 
 
-def score_kernel(q_rows, masks, inv, mine, other, queries, keep, send):
+def sketch_kernel(inv, mine, other, queries, lhs_out, inner_out):
     rows, lanes = other.shape[0] - 8, other.shape[1]
     side = lanes // 2
     me = lax.axis_index("tok")
@@ -245,9 +248,17 @@
         )
     sketch = jnp.concatenate(parts, axis=0)
     k_hi, k_lo = split(sketch)
-    inner = nt(jnp.concatenate([k_hi, k_lo], axis=0), queries[...])
+    lhs = jnp.concatenate([k_hi, k_lo], axis=0)
+    lhs_out[...] = lhs
+    inner_out[...] = nt(lhs, queries[...])
+
+
+def score_kernel(q_rows, masks, lhs, inner, far, mine, keep, send):
+    rows = mine.shape[0] - 16
+    me = lax.axis_index("tok")
+    inner = jnp.concatenate([inner[...], nt(lhs[...], far[...])], axis=1)
     inner = inner[: 2 * EX_DEV] + inner[2 * EX_DEV :]
-    count = queries.shape[0]
+    count = inner.shape[1]
     src = lax.broadcasted_iota(jnp.int32, (count, count), 0)
     dst = lax.broadcasted_iota(jnp.int32, (count, count), 1)
     shift = q_rows.bit_length() - 1
@@ -273,7 +284,7 @@
         return lax.ppermute(x, "tok", [(i, i ^ mask) for i in range(devices)])
 
     ids = example_ids.reshape(1, rows)
-    first = devices // 2
+    first = devices // 2 | 1
     raw, zero = lax.optimization_barrier((query_sketch, lead()))
     arrived = swap(raw, first)
     mine, send, own = project(devices, inputs_act, out_grads, ids, proj_in.T, proj_out.T, ckpt_weight[None], zero)
@@ -291,16 +302,18 @@
         compiler_params=pltpu.CompilerParams(vmem_limit_bytes=4 * 2**20),
         name="gram",
     )(other, tick(HEAVY, own))
-    far = [devices >> k for k in range(1, devices.bit_length() - 2)]
-    sums = [2, *far]
-    late = [*far[:0:-1], 2]
+    far = [devices >> k | 1 for k in range(1, devices.bit_length() - 2)]
+    sums = [3, *far]
+    late = [*far[:0:-1], 3]
     masks = (first, 1, *late)
     for step, mask in enumerate(sums):
         last = step == len(sums) - 1
         held = g
         if late:
             queries, held = lax.optimization_barrier((queries, tick(HEAVY, g)))
-            queries = jnp.concatenate([queries, swap(queries, late.pop(0))], axis=0)
+            far_rows = swap(queries, late.pop(0))
+            if late:
+                queries = jnp.concatenate([queries, far_rows], axis=0)
         g = tick(HEAVY if held is not g else LIGHT, held, swap(g, mask))
     inv = pl.pallas_call(
         inverse_kernel,
@@ -310,6 +323,18 @@
         compiler_params=pltpu.CompilerParams(vmem_limit_bytes=4 * 2**20),
         name="inverse",
     )(g)
+    near_rows, width = queries.shape
+    lhs, inner = pl.pallas_call(
+        sketch_kernel,
+        out_shape=(
+            jax.ShapeDtypeStruct((4 * EX_DEV, width), BF16),
+            jax.ShapeDtypeStruct((4 * EX_DEV, near_rows), F32),
+        ),
+        in_specs=[VMEM] * 4,
+        out_specs=(VMEM, VMEM),
+        compiler_params=pltpu.CompilerParams(vmem_limit_bytes=16 * 2**20),
+        name="sketch",
+    )(inv, mine, other, queries)
     keep, send = pl.pallas_call(
         functools.partial(score_kernel, q_rows, masks),
         out_shape=(
@@ -318,9 +343,9 @@
         ),
         in_specs=[VMEM] * 4,
         out_specs=(VMEM, VMEM),
-        compiler_params=pltpu.CompilerParams(vmem_limit_bytes=16 * 2**20),
+        compiler_params=pltpu.CompilerParams(vmem_limit_bytes=8 * 2**20),
         name="score",
-    )(inv, mine, other, queries)
+    )(lhs, inner, far_rows, mine)
     return keep + swap(send, 1)
 
 

time: 27.8 us -> 27.4 us (0.986)
  waiting for transfers between devices: 5.83 us -> 4.19 us
  starting transfers between devices: 13.7 us -> 14.6 us
  Pallas kernels: 6.39 us -> 6.78 us
    ppermute x9, waiting for transfers between devices: 5.83 us -> 4.19 us  [swap(): return lax.ppermute(x, 'tok', [(i, i ^ mask) for i in range(devices)])]
    pallas_call x0 -> x1, Pallas kernels: none -> 1.08 us  [local(): pl.pallas_call(sketch_kernel, out_shape=(jax.ShapeDtypeStruct((4 * EX_DEV...]
    ppermute x9, starting transfers between devices: 13.7 us -> 14.6 us  [swap(): return lax.ppermute(x, 'tok', [(i, i ^ mask) for i in range(devices)])]
    pallas_call x1, Pallas kernels: 1.24 us -> 0.52 us  [local(): pl.pallas_call(functools.partial(score_kernel, q_rows, masks), out_shape=...]
  transfers between devices with their start and end apart: 9 -> 9, of which waited for: 7 -> 5; matrix products, arithmetic and copies ran while one was open for 0% -> 0% of each run, Pallas kernels for 19% -> 23%
where the time goes in v6:
time: 27.4 us; the launch traced here: 27.3 us
  starting transfers between devices  14.6 us (53%)
  Pallas kernels  6.78 us (25%)
  waiting for transfers between devices  4.19 us (15%)
  local copies, waits for them, and re-layouts  0.87 us (3%)
  other arithmetic  0.71 us (3%)
    ppermute x9, starting transfers between devices, swap(): return lax.ppermute(x, 'tok', [(i, i ^ mask) for i in range(devices)])  14.6 us
    ppermute x9, waiting for transfers between devices, swap(): return lax.ppermute(x, 'tok', [(i, i ^ mask) for i in range(devices)])  4.19 us
    pallas_call x1, Pallas kernels, project(): pl.pallas_call(functools.partial(project_kernel, devices), out_shape=(jax...  2.38 us
    pallas_call x1, Pallas kernels, local(): pl.pallas_call(inverse_kernel, out_shape=jax.ShapeDtypeStruct((side, 2 *...  1.82 us
    pallas_call x1, Pallas kernels, local(): pl.pallas_call(sketch_kernel, out_shape=(jax.ShapeDtypeStruct((4 * EX_DEV...  1.08 us
    unnamed x14, local copies, waits for them, and re-layouts  0.87 us
    pallas_call x1, Pallas kernels, grad_side(): pl.pallas_call(side_kernel, out_shape=jax.ShapeDtypeStruct((grad.shape[0]...  0.68 us
    add x1, other arithmetic, local(): return keep + swap(send, 1)  0.6 us
  transfers between devices with their start and end apart: 9, of which 5 were waited for; matrix products, arithmetic and copies ran while one was open for 0% of the time, Pallas kernels for 23%

profile of v6, /device:TPU:0, one launch (start us, length us, event | category | flops | bytes accessed | tf_op | source)
XLA Modules:
  0.0 27.3 jit_solution(9700548106201014995)
XLA Ops:
  0.0 0.8 %copy-done.6 = bf16[2,4,4096]{2,1,0:T(4,128)(2,1)S(1)} copy-done((bf16[2,4,4096]{2,1,0:T(4,128)(2,1)S(1)}, bf16[2,4,4096]{2,1,0:T(4,128)(2,1)}, u32[]{:S(2)}) %copy-start.6) | copy-done | bytes 65560
  0.8 3.5 %collective-permute-start = (bf16[2,4,4096]{2,1,0:T(4,128)(2,1)S(1)}, bf16[2,4,4096]{2,1,0:T(4,128)(2,1)S(1)}, u32[]{:S(2)}, u32[]{:S(2)}) collective-permute-start(bf16[2,4,4096]{2,1,0:T(4,128)(2,1)S(1)} %copy-done.6), channel_id=1, source_target_pairs={{0,9},{1,8},{2,11},{3,10},{4,13},{5,12},{6,15},{7,14},{8,1},{9,0},... | collective-permute-start | bytes 196616 | tf_op jit(solution)/shard_map/ppermute | solution.py:284
  4.3 0.0 copy-done.1
  4.3 0.0 copy-done
  4.3 0.7 %grad_side.1.s_all = f32[256,64]{1,0:T(8,128)S(1)} custom-call(bf16[2,128,4096]{2,1,0:T(8,128)(2,1)S(1)} %copy-done, bf16[64,4096]{1,0:T(8,128)(2,1)S(1)} %bitcast.8), custom_call_target="tpu_custom_call" | custom-call | flops 1000000 | bytes 1000 | tf_op jit(solution)/shard_map/grad_side/pallas_call | solution.py:42
  5.0 0.0 copy-done.2
  5.0 0.0 copy-done.3
  5.0 0.0 copy-done.4
  5.1 2.4 %project.1 = (f32[144,128]{1,0:T(8,128)S(1)}, f32[136,128]{1,0:T(8,128)S(1)}, f32[64,128]{1,0:T(8,128)S(1)}) custom-call(bf16[2,128,14336]{2,1,0:T(8,128)(2,1)S(1)} %copy-done.2, s32[1,128]{1,0:T(1,128)S(1)} %bitcast.10, bf16[64,14336]{1,0:T(8,128)(2,1)S(1)} %bitcast.9, f32[256,64]{1,0:T(8,128)S(1)} %grad_side.1.s_all, f32[1,2]{1,0:T(1,128)S(1)} %bitcast.11, ...), custom_call_target="tpu_custom_call" | custom-call | flops 20000000000 | bytes 20000000 | tf_op jit(solution)/shard_map/project/pallas_call | solution.py:87
  7.5 0.7 %collective-permute-start.2 = (f32[136,128]{1,0:T(8,128)S(1)}, f32[136,128]{1,0:T(8,128)S(1)}, u32[]{:S(2)}, u32[]{:S(2)}) collective-permute-start(f32[136,128]{1,0:T(8,128)S(1)} %get-tuple-element.24), channel_id=1, source_target_pairs={{0,1},{1,0},{2,3},{3,2},{4,5},{5,4},{6,7},{7,6},{8,9},{9,8},{10,11... | collective-permute-start | bytes 208904 | tf_op jit(solution)/shard_map/ppermute | solution.py:284
  8.2 0.0 collective-permute-done
  8.2 0.1 select_bitcast_fusion.1
  8.3 0.1 collective-permute-start.1
  8.4 0.7 %collective-permute-done.2.x.other = f32[136,128]{1,0:T(8,128)S(1)} collective-permute-done((f32[136,128]{1,0:T(8,128)S(1)}, f32[136,128]{1,0:T(8,128)S(1)}, u32[]{:S(2)}, u32[]{:S(2)}) %collective-permute-start.2) | collective-permute-done | bytes 69664 | tf_op jit(solution)/shard_map/ppermute | solution.py:284
  9.1 0.3 gram.1.refs_0_
  9.4 2.0 %collective-permute-start.4 = (f32[64,128]{1,0:T(8,128)S(1)}, f32[64,128]{1,0:T(8,128)S(1)}, u32[]{:S(2)}, u32[]{:S(2)}) collective-permute-start(f32[64,128]{1,0:T(8,128)S(1)} %gram.1.refs_0_), channel_id=1, source_target_pairs={{0,3},{1,2},{2,1},{3,0},{4,7},{5,6},{6,5},{7,4},{8,11},{9,10},{10,... | collective-permute-start | bytes 98312 | tf_op jit(solution)/shard_map/ppermute | solution.py:284
  11.4 0.0 collective-permute-done.1
  11.4 1.6 %collective-permute-start.3 = (bf16[16,4096]{1,0:T(8,128)(2,1)S(1)}, bf16[16,4096]{1,0:T(8,128)(2,1)S(1)}, u32[]{:S(2)}, u32[]{:S(2)}) collective-permute-start(bf16[16,4096]{1,0:T(8,128)(2,1)S(1)} %pad_maximum_fusion.1), channel_id=1, source_target_pairs={{0,5},{1,4},{2,7},{3,6},{4,1},{5,0},{6,3},{7,2},{8,13},{9,12},{10,... | collective-permute-start | bytes 393224 | tf_op jit(solution)/shard_map/ppermute | solution.py:284
  13.0 0.0 collective-permute-done.4.refs_1_
  13.0 2.9 %collective-permute-start.5 = (f32[64,128]{1,0:T(8,128)S(1)}, f32[64,128]{1,0:T(8,128)S(1)}, u32[]{:S(2)}, u32[]{:S(2)}) collective-permute-start(f32[64,128]{1,0:T(8,128)S(1)} %tick.8.refs_0_), channel_id=1, source_target_pairs={{0,9},{1,8},{2,11},{3,10},{4,13},{5,12},{6,15},{7,14},{8,1},{9,0},... | collective-permute-start | bytes 98312 | tf_op jit(solution)/shard_map/ppermute | solution.py:284
  15.9 0.9 %collective-permute-done.3 = bf16[16,4096]{1,0:T(8,128)(2,1)S(1)} collective-permute-done((bf16[16,4096]{1,0:T(8,128)(2,1)S(1)}, bf16[16,4096]{1,0:T(8,128)(2,1)S(1)}, u32[]{:S(2)}, u32[]{:S(2)}) %collective-permute-start.3) | collective-permute-done | bytes 131104 | tf_op jit(solution)/shard_map/ppermute | solution.py:284
  16.8 0.6 %collective-permute-start.7 = (bf16[32,4096]{1,0:T(8,128)(2,1)S(1)}, bf16[32,4096]{1,0:T(8,128)(2,1)S(1)}, u32[]{:S(2)}, u32[]{:S(2)}) collective-permute-start(bf16[32,4096]{1,0:T(8,128)(2,1)S(1)} %pad_maximum_fusion.queries), channel_id=1, source_target_pairs={{0,3},{1,2},{2,1},{3,0},{4,7},{5,6},{6,5},{7,4},{8,11},{9,10},{10,... | collective-permute-start | bytes 786440 | tf_op jit(solution)/shard_map/ppermute | solution.py:284
  17.5 0.1 collective-permute-done.5.refs_1_
  17.6 2.4 %collective-permute-start.6 = (f32[64,128]{1,0:T(8,128)S(1)}, f32[64,128]{1,0:T(8,128)S(1)}, u32[]{:S(2)}, u32[]{:S(2)}) collective-permute-start(f32[64,128]{1,0:T(8,128)S(1)} %tick.10.refs_0_), channel_id=1, source_target_pairs={{0,5},{1,4},{2,7},{3,6},{4,1},{5,0},{6,3},{7,2},{8,13},{9,12},{10,... | collective-permute-start | bytes 98312 | tf_op jit(solution)/shard_map/ppermute | solution.py:284
  20.0 1.6 %collective-permute-done.6.refs_1_ = f32[64,128]{1,0:T(8,128)S(1)} collective-permute-done((f32[64,128]{1,0:T(8,128)S(1)}, f32[64,128]{1,0:T(8,128)S(1)}, u32[]{:S(2)}, u32[]{:S(2)}) %collective-permute-start.6) | collective-permute-done | bytes 32800 | tf_op jit(solution)/shard_map/ppermute | solution.py:284
  21.6 1.8 %inverse.1.inv = f32[64,128]{1,0:T(8,128)S(1)} custom-call(f32[64,128]{1,0:T(8,128)S(1)} %tick.11.g), custom_call_target="tpu_custom_call" | custom-call | tf_op jit(solution)/shard_map/inverse/pallas_call | solution.py:318
  23.4 1.1 %sketch.1 = (bf16[64,4096]{1,0:T(8,128)(2,1)S(1)}, f32[64,32]{1,0:T(8,128)S(1)}) custom-call(f32[64,128]{1,0:T(8,128)S(1)} %inverse.1.inv, f32[144,128]{1,0:T(8,128)S(1)} %get-tuple-element.29.mine, f32[136,128]{1,0:T(8,128)S(1)} %collective-permute-done.2.x.other, bf16[32,4096]{1,0:T(8,128)(2,1)S(1)} %pad_maximum_fusion.queries), custom_call_target="tpu_custom_call" | custom-call | tf_op jit(solution)/shard_map/sketch/pallas_call | solution.py:327
  24.5 0.0 collective-permute-done.7.far
  24.5 0.5 %score.1 = (f32[16,64]{1,0:T(8,128)S(1)}, f32[16,64]{1,0:T(8,128)S(1)}) custom-call(bf16[64,4096]{1,0:T(8,128)(2,1)S(1)} %get-tuple-element.31.lhs, f32[64,32]{1,0:T(8,128)S(1)} %get-tuple-element.32.inner, bf16[32,4096]{1,0:T(8,128)(2,1)S(1)} %collective-permute-done.7.far, f32[144,128]{1,0:T(8,128)S(1)} %get-tuple-element.29.mine), custom_call_target="tpu_custom_call" | custom-call | tf_op jit(solution)/shard_map/score/pallas_call | solution.py:338
  25.1 0.8 %collective-permute-start.8 = (f32[16,64]{1,0:T(8,128)S(1)}, f32[16,64]{1,0:T(8,128)S(1)}, u32[]{:S(2)}, u32[]{:S(2)}) collective-permute-start(f32[16,64]{1,0:T(8,128)S(1)} %get-tuple-element.34), channel_id=1, source_target_pairs={{0,1},{1,0},{2,3},{3,2},{4,5},{5,4},{6,7},{7,6},{8,9},{9,8},{10,11... | collective-permute-start | bytes 12296 | tf_op jit(solution)/shard_map/ppermute | solution.py:284
  25.9 0.8 %collective-permute-done.8 = f32[16,64]{1,0:T(8,128)S(1)} collective-permute-done((f32[16,64]{1,0:T(8,128)S(1)}, f32[16,64]{1,0:T(8,128)S(1)}, u32[]{:S(2)}, u32[]{:S(2)}) %collective-permute-start.8) | collective-permute-done | bytes 4128 | tf_op jit(solution)/shard_map/ppermute | solution.py:284
  26.7 0.6 %add.3 = f32[16,64]{1,0:T(8,128)} add(f32[16,64]{1,0:T(8,128)S(1)} %get-tuple-element.33, f32[16,64]{1,0:T(8,128)S(1)} %collective-permute-done.8) | non-fusion elementwise | flops 1024 | bytes 12288 | tf_op jit(solution)/shard_map/add | solution.py:349
  (17 shorter events, 0.1 us)
Async XLA Ops:
  0.0 0.8 %copy-start.6 = (bf16[2,4,4096]{2,1,0:T(4,128)(2,1)S(1)}, bf16[2,4,4096]{2,1,0:T(4,128)(2,1)}, u32[]{:S(2)}) copy-start(bf16[2,4,4096]{2,1,0:T(4,128)(2,1)} %param.12) | copy-start | bytes 196612
  0.0 4.3 %copy-start.1 = (bf16[4096,64]{0,1:T(8,128)(2,1)S(1)}, bf16[4096,64]{0,1:T(8,128)(2,1)}, u32[]{:S(2)}) copy-start(bf16[4096,64]{0,1:T(8,128)(2,1)} %param.11) | copy-start | bytes 1572868
  0.0 4.3 %copy-start = (bf16[2,128,4096]{2,1,0:T(8,128)(2,1)S(1)}, bf16[2,128,4096]{2,1,0:T(8,128)(2,1)}, u32[]{:S(2)}) copy-start(bf16[2,128,4096]{2,1,0:T(8,128)(2,1)} %grad.1) | copy-start | bytes 6291460
  0.0 5.0 %copy-start.2 = (bf16[2,128,14336]{2,1,0:T(8,128)(2,1)S(1)}, bf16[2,128,14336]{2,1,0:T(8,128)(2,1)}, u32[]{:S(2)}) copy-start(bf16[2,128,14336]{2,1,0:T(8,128)(2,1)} %act.1) | copy-start | bytes 22020100
  0.8 4.2 %copy-start.3 = (bf16[14336,64]{0,1:T(8,128)(2,1)S(1)}, bf16[14336,64]{0,1:T(8,128)(2,1)}, u32[]{:S(2)}) copy-start(bf16[14336,64]{0,1:T(8,128)(2,1)} %param.10) | copy-start | bytes 5505028
  0.8 4.2 %copy-start.4 = (s32[128]{0:T(128)S(1)}, s32[128]{0:T(128)}, u32[]{:S(2)}) copy-start(s32[128]{0:T(128)} %param.9) | copy-start | bytes 1540
  0.8 4.2 %copy-start.5 = (f32[2]{0:T(128)S(1)}, f32[2]{0:T(128)}, u32[]{:S(2)}) copy-start(f32[2]{0:T(128)} %param.13) | copy-start | bytes 28
  0.8 7.3 %collective-permute-start = (bf16[2,4,4096]{2,1,0:T(4,128)(2,1)S(1)}, bf16[2,4,4096]{2,1,0:T(4,128)(2,1)S(1)}, u32[]{:S(2)}, u32[]{:S(2)}) collective-permute-start(bf16[2,4,4096]{2,1,0:T(4,128)(2,1)S(1)} %copy-done.6), channel_id=1, source_target_pairs={{0,9},{1,8},{2,11},{3,10},{4,13},{5,12},{6,15},{7,14},{8,1},{9,0},... | collective-permute-start | bytes 196616 | tf_op jit(solution)/shard_map/ppermute | solution.py:284
  7.5 1.6 %collective-permute-start.2 = (f32[136,128]{1,0:T(8,128)S(1)}, f32[136,128]{1,0:T(8,128)S(1)}, u32[]{:S(2)}, u32[]{:S(2)}) collective-permute-start(f32[136,128]{1,0:T(8,128)S(1)} %get-tuple-element.24), channel_id=1, source_target_pairs={{0,1},{1,0},{2,3},{3,2},{4,5},{5,4},{6,7},{7,6},{8,9},{9,8},{10,11... | collective-permute-start | bytes 208904 | tf_op jit(solution)/shard_map/ppermute | solution.py:284
  8.3 3.1 %collective-permute-start.1 = (bf16[8,4096]{1,0:T(8,128)(2,1)S(1)}, bf16[8,4096]{1,0:T(8,128)(2,1)S(1)}, u32[]{:S(2)}, u32[]{:S(2)}) collective-permute-start(bf16[8,4096]{1,0:T(8,128)(2,1)S(1)} %get-tuple-element.36), channel_id=1, source_target_pairs={{0,1},{1,0},{2,3},{3,2},{4,5},{5,4},{6,7},{7,6},{8,9},{9,8},{10,11... | collective-permute-start | bytes 196616 | tf_op jit(solution)/shard_map/ppermute | solution.py:284
  9.4 3.6 %collective-permute-start.4 = (f32[64,128]{1,0:T(8,128)S(1)}, f32[64,128]{1,0:T(8,128)S(1)}, u32[]{:S(2)}, u32[]{:S(2)}) collective-permute-start(f32[64,128]{1,0:T(8,128)S(1)} %gram.1.refs_0_), channel_id=1, source_target_pairs={{0,3},{1,2},{2,1},{3,0},{4,7},{5,6},{6,5},{7,4},{8,11},{9,10},{10,... | collective-permute-start | bytes 98312 | tf_op jit(solution)/shard_map/ppermute | solution.py:284
  11.4 5.4 %collective-permute-start.3 = (bf16[16,4096]{1,0:T(8,128)(2,1)S(1)}, bf16[16,4096]{1,0:T(8,128)(2,1)S(1)}, u32[]{:S(2)}, u32[]{:S(2)}) collective-permute-start(bf16[16,4096]{1,0:T(8,128)(2,1)S(1)} %pad_maximum_fusion.1), channel_id=1, source_target_pairs={{0,5},{1,4},{2,7},{3,6},{4,1},{5,0},{6,3},{7,2},{8,13},{9,12},{10,... | collective-permute-start | bytes 393224 | tf_op jit(solution)/shard_map/ppermute | solution.py:284
  13.0 4.6 %collective-permute-start.5 = (f32[64,128]{1,0:T(8,128)S(1)}, f32[64,128]{1,0:T(8,128)S(1)}, u32[]{:S(2)}, u32[]{:S(2)}) collective-permute-start(f32[64,128]{1,0:T(8,128)S(1)} %tick.8.refs_0_), channel_id=1, source_target_pairs={{0,9},{1,8},{2,11},{3,10},{4,13},{5,12},{6,15},{7,14},{8,1},{9,0},... | collective-permute-start | bytes 98312 | tf_op jit(solution)/shard_map/ppermute | solution.py:284
  16.8 7.7 %collective-permute-start.7 = (bf16[32,4096]{1,0:T(8,128)(2,1)S(1)}, bf16[32,4096]{1,0:T(8,128)(2,1)S(1)}, u32[]{:S(2)}, u32[]{:S(2)}) collective-permute-start(bf16[32,4096]{1,0:T(8,128)(2,1)S(1)} %pad_maximum_fusion.queries), channel_id=1, source_target_pairs={{0,3},{1,2},{2,1},{3,0},{4,7},{5,6},{6,5},{7,4},{8,11},{9,10},{10,... | collective-permute-start | bytes 786440 | tf_op jit(solution)/shard_map/ppermute | solution.py:284
  17.6 4.0 %collective-permute-start.6 = (f32[64,128]{1,0:T(8,128)S(1)}, f32[64,128]{1,0:T(8,128)S(1)}, u32[]{:S(2)}, u32[]{:S(2)}) collective-permute-start(f32[64,128]{1,0:T(8,128)S(1)} %tick.10.refs_0_), channel_id=1, source_target_pairs={{0,5},{1,4},{2,7},{3,6},{4,1},{5,0},{6,3},{7,2},{8,13},{9,12},{10,... | collective-permute-start | bytes 98312 | tf_op jit(solution)/shard_map/ppermute | solution.py:284
  25.1 1.6 %collective-permute-start.8 = (f32[16,64]{1,0:T(8,128)S(1)}, f32[16,64]{1,0:T(8,128)S(1)}, u32[]{:S(2)}, u32[]{:S(2)}) collective-permute-start(f32[16,64]{1,0:T(8,128)S(1)} %get-tuple-element.34), channel_id=1, source_target_pairs={{0,1},{1,0},{2,3},{3,2},{4,5},{5,4},{6,7},{7,6},{8,9},{9,8},{10,11... | collective-permute-start | bytes 12296 | tf_op jit(solution)/shard_map/ppermute | solution.py:284

commit v7 on v6

--- a/solution.py
+++ b/solution.py
@@ -50,7 +50,7 @@
     )(grad, pout)
 
 
-def project_kernel(devices, act, ids, pin, s_all, weight, zero, keep, send, own):
+def project_kernel(devices, act, ids, pin, s_all, weight, zero, keep, send):
     ckpts, rows, _ = act.shape
     side = pin.shape[0]
     half = rows // 2
@@ -77,7 +77,6 @@
     keep[rows + 8 :, :] = jnp.broadcast_to(scale, (8, 2 * side))
     send[0:rows, :] = jnp.where(odd == 0, second, first)
     send[rows : rows + 8, :] = tail
-    own[...] = factors(mine, rows * devices)
 
 
 def project(devices, act, grad, ids, pin, pout, weight, zero):
@@ -89,10 +88,9 @@
         out_shape=(
             jax.ShapeDtypeStruct((rows + 16, 2 * side), F32),
             jax.ShapeDtypeStruct((rows + 8, 2 * side), F32),
-            jax.ShapeDtypeStruct((side, 2 * side), F32),
         ),
         in_specs=[VMEM] * 6,
-        out_specs=(VMEM, VMEM, VMEM),
+        out_specs=(VMEM, VMEM),
         compiler_params=pltpu.CompilerParams(vmem_limit_bytes=24 * 2**20),
         cost_estimate=pl.CostEstimate(flops=HEAVY, bytes_accessed=2 * 10**7, transcendentals=0),
         name="project",
@@ -108,9 +106,9 @@
     return jnp.where(lane < side, g[:side], g[side:]) * (1.0 / total)
 
 
-def gram_kernel(total, x, own, out):
-    rows = x.shape[0] - 8
-    out[...] = own[...] + factors(x[0:rows, :], total)
+def gram_kernel(total, mine, other, out):
+    rows = other.shape[0] - 8
+    out[...] = factors(jnp.concatenate([mine[0:rows, :], other[0:rows, :]], axis=0), total)
 
 
 def lead_kernel(out):
@@ -287,7 +285,7 @@
     first = devices // 2 | 1
     raw, zero = lax.optimization_barrier((query_sketch, lead()))
     arrived = swap(raw, first)
-    mine, send, own = project(devices, inputs_act, out_grads, ids, proj_in.T, proj_out.T, ckpt_weight[None], zero)
+    mine, send = project(devices, inputs_act, out_grads, ids, proj_in.T, proj_out.T, ckpt_weight[None], zero)
     other = swap(send, 1)
     arrived, mine = lax.optimization_barrier((arrived, mine))
     both = jnp.concatenate([query_sketch, arrived], axis=1)
@@ -301,7 +299,7 @@
         out_specs=VMEM,
         compiler_params=pltpu.CompilerParams(vmem_limit_bytes=4 * 2**20),
         name="gram",
-    )(other, tick(HEAVY, own))
+    )(mine, other)
     far = [devices >> k | 1 for k in range(1, devices.bit_length() - 2)]
     sums = [3, *far]
     late = [*far[:0:-1], 3]

time: 27.4 us -> 27.2 us (level)
    pallas_call x1, Pallas kernels: 2.38 us -> 2.06 us  [project(): pl.pallas_call(functools.partial(project_kernel, devices), out_shape=(jax...]
  transfers between devices with their start and end apart: 9 -> 9, of which waited for: 5 -> 5; matrix products, arithmetic and copies ran while one was open for 0% -> 0% of each run, Pallas kernels for 23% -> 22%
where the time goes in v7:
time: 27.2 us; the launch traced here: 27 us
  starting transfers between devices  14.6 us (54%)
  Pallas kernels  6.51 us (24%)
  waiting for transfers between devices  4.21 us (15%)
  local copies, waits for them, and re-layouts  0.87 us (3%)
  other arithmetic  0.71 us (3%)
    ppermute x9, starting transfers between devices, swap(): return lax.ppermute(x, 'tok', [(i, i ^ mask) for i in range(devices)])  14.6 us
    ppermute x9, waiting for transfers between devices, swap(): return lax.ppermute(x, 'tok', [(i, i ^ mask) for i in range(devices)])  4.21 us
    pallas_call x1, Pallas kernels, project(): pl.pallas_call(functools.partial(project_kernel, devices), out_shape=(jax...  2.06 us
    pallas_call x1, Pallas kernels, local(): pl.pallas_call(inverse_kernel, out_shape=jax.ShapeDtypeStruct((side, 2 *...  1.82 us
    pallas_call x1, Pallas kernels, local(): pl.pallas_call(sketch_kernel, out_shape=(jax.ShapeDtypeStruct((4 * EX_DEV...  1.08 us
    unnamed x14, local copies, waits for them, and re-layouts  0.87 us
    pallas_call x1, Pallas kernels, grad_side(): pl.pallas_call(side_kernel, out_shape=jax.ShapeDtypeStruct((grad.shape[0]...  0.68 us
    add x1, other arithmetic, local(): return keep + swap(send, 1)  0.6 us
  transfers between devices with their start and end apart: 9, of which 5 were waited for; matrix products, arithmetic and copies ran while one was open for 0% of the time, Pallas kernels for 22%

profile of v7, /device:TPU:0, one launch (start us, length us, event | category | flops | bytes accessed | tf_op | source)
XLA Modules:
  0.0 27.0 jit_solution(1863738519690082952)
XLA Ops:
  0.0 0.8 %copy-done.6 = bf16[2,4,4096]{2,1,0:T(4,128)(2,1)S(1)} copy-done((bf16[2,4,4096]{2,1,0:T(4,128)(2,1)S(1)}, bf16[2,4,4096]{2,1,0:T(4,128)(2,1)}, u32[]{:S(2)}) %copy-start.6) | copy-done | bytes 65560
  0.8 3.5 %collective-permute-start = (bf16[2,4,4096]{2,1,0:T(4,128)(2,1)S(1)}, bf16[2,4,4096]{2,1,0:T(4,128)(2,1)S(1)}, u32[]{:S(2)}, u32[]{:S(2)}) collective-permute-start(bf16[2,4,4096]{2,1,0:T(4,128)(2,1)S(1)} %copy-done.6), channel_id=1, source_target_pairs={{0,9},{1,8},{2,11},{3,10},{4,13},{5,12},{6,15},{7,14},{8,1},{9,0},... | collective-permute-start | bytes 196616 | tf_op jit(solution)/shard_map/ppermute | solution.py:282
  4.3 0.0 copy-done.1
  4.3 0.7 %grad_side.1.s_all = f32[256,64]{1,0:T(8,128)S(1)} custom-call(bf16[2,128,4096]{2,1,0:T(8,128)(2,1)S(1)} %copy-done, bf16[64,4096]{1,0:T(8,128)(2,1)S(1)} %bitcast.8), custom_call_target="tpu_custom_call" | custom-call | flops 1000000 | bytes 1000 | tf_op jit(solution)/shard_map/grad_side/pallas_call | solution.py:42
  5.0 0.0 copy-done.2
  5.0 0.0 copy-done.3
  5.0 0.0 copy-done.4
  5.1 0.0 copy-done.5
  5.1 2.1 %project.1 = (f32[144,128]{1,0:T(8,128)S(1)}, f32[136,128]{1,0:T(8,128)S(1)}) custom-call(bf16[2,128,14336]{2,1,0:T(8,128)(2,1)S(1)} %copy-done.2, s32[1,128]{1,0:T(1,128)S(1)} %bitcast.10, bf16[64,14336]{1,0:T(8,128)(2,1)S(1)} %bitcast.9, f32[256,64]{1,0:T(8,128)S(1)} %grad_side.1.s_all, f32[1,2]{1,0:T(1,128)S(1)} %bitcast.11, f32[8,128]{1,0:T(8,128)S(1)} %lead.1.zero), custom_call_target="tpu_custom_call" | custom-call | flops 20000000000 | bytes 20000000 | tf_op jit(solution)/shard_map/project/pallas_call | solution.py:86
  7.1 0.7 %collective-permute-start.2 = (f32[136,128]{1,0:T(8,128)S(1)}, f32[136,128]{1,0:T(8,128)S(1)}, u32[]{:S(2)}, u32[]{:S(2)}) collective-permute-start(f32[136,128]{1,0:T(8,128)S(1)} %get-tuple-element.24), channel_id=1, source_target_pairs={{0,1},{1,0},{2,3},{3,2},{4,5},{5,4},{6,7},{7,6},{8,9},{9,8},{10,11... | collective-permute-start | bytes 208904 | tf_op jit(solution)/shard_map/ppermute | solution.py:282
  7.9 0.0 collective-permute-done
  7.9 0.1 select_bitcast_fusion.1
  8.0 0.1 collective-permute-start.1
  8.1 0.7 %collective-permute-done.2.other = f32[136,128]{1,0:T(8,128)S(1)} collective-permute-done((f32[136,128]{1,0:T(8,128)S(1)}, f32[136,128]{1,0:T(8,128)S(1)}, u32[]{:S(2)}, u32[]{:S(2)}) %collective-permute-start.2) | collective-permute-done | bytes 69664 | tf_op jit(solution)/shard_map/ppermute | solution.py:282
  8.8 0.3 %gram.1.refs_0_ = f32[64,128]{1,0:T(8,128)S(1)} custom-call(f32[144,128]{1,0:T(8,128)S(1)} %get-tuple-element.23.mine, f32[136,128]{1,0:T(8,128)S(1)} %collective-permute-done.2.other), custom_call_target="tpu_custom_call" | custom-call | tf_op jit(solution)/shard_map/gram/pallas_call | solution.py:295
  9.1 2.0 %collective-permute-start.4 = (f32[64,128]{1,0:T(8,128)S(1)}, f32[64,128]{1,0:T(8,128)S(1)}, u32[]{:S(2)}, u32[]{:S(2)}) collective-permute-start(f32[64,128]{1,0:T(8,128)S(1)} %gram.1.refs_0_), channel_id=1, source_target_pairs={{0,3},{1,2},{2,1},{3,0},{4,7},{5,6},{6,5},{7,4},{8,11},{9,10},{10,... | collective-permute-start | bytes 98312 | tf_op jit(solution)/shard_map/ppermute | solution.py:282
  11.1 0.0 collective-permute-done.1
  11.1 1.6 %collective-permute-start.3 = (bf16[16,4096]{1,0:T(8,128)(2,1)S(1)}, bf16[16,4096]{1,0:T(8,128)(2,1)S(1)}, u32[]{:S(2)}, u32[]{:S(2)}) collective-permute-start(bf16[16,4096]{1,0:T(8,128)(2,1)S(1)} %pad_maximum_fusion.1), channel_id=1, source_target_pairs={{0,5},{1,4},{2,7},{3,6},{4,1},{5,0},{6,3},{7,2},{8,13},{9,12},{10,... | collective-permute-start | bytes 393224 | tf_op jit(solution)/shard_map/ppermute | solution.py:282
  12.8 0.0 collective-permute-done.4.refs_1_
  12.8 2.9 %collective-permute-start.5 = (f32[64,128]{1,0:T(8,128)S(1)}, f32[64,128]{1,0:T(8,128)S(1)}, u32[]{:S(2)}, u32[]{:S(2)}) collective-permute-start(f32[64,128]{1,0:T(8,128)S(1)} %tick.6.refs_0_), channel_id=1, source_target_pairs={{0,9},{1,8},{2,11},{3,10},{4,13},{5,12},{6,15},{7,14},{8,1},{9,0},... | collective-permute-start | bytes 98312 | tf_op jit(solution)/shard_map/ppermute | solution.py:282
  15.6 0.9 %collective-permute-done.3 = bf16[16,4096]{1,0:T(8,128)(2,1)S(1)} collective-permute-done((bf16[16,4096]{1,0:T(8,128)(2,1)S(1)}, bf16[16,4096]{1,0:T(8,128)(2,1)S(1)}, u32[]{:S(2)}, u32[]{:S(2)}) %collective-permute-start.3) | collective-permute-done | bytes 131104 | tf_op jit(solution)/shard_map/ppermute | solution.py:282
  16.6 0.6 %collective-permute-start.7 = (bf16[32,4096]{1,0:T(8,128)(2,1)S(1)}, bf16[32,4096]{1,0:T(8,128)(2,1)S(1)}, u32[]{:S(2)}, u32[]{:S(2)}) collective-permute-start(bf16[32,4096]{1,0:T(8,128)(2,1)S(1)} %pad_maximum_fusion.queries), channel_id=1, source_target_pairs={{0,3},{1,2},{2,1},{3,0},{4,7},{5,6},{6,5},{7,4},{8,11},{9,10},{10,... | collective-permute-start | bytes 786440 | tf_op jit(solution)/shard_map/ppermute | solution.py:282
  17.2 0.1 collective-permute-done.5.refs_1_
  17.3 2.4 %collective-permute-start.6 = (f32[64,128]{1,0:T(8,128)S(1)}, f32[64,128]{1,0:T(8,128)S(1)}, u32[]{:S(2)}, u32[]{:S(2)}) collective-permute-start(f32[64,128]{1,0:T(8,128)S(1)} %tick.8.refs_0_), channel_id=1, source_target_pairs={{0,5},{1,4},{2,7},{3,6},{4,1},{5,0},{6,3},{7,2},{8,13},{9,12},{10,... | collective-permute-start | bytes 98312 | tf_op jit(solution)/shard_map/ppermute | solution.py:282
  19.7 1.6 %collective-permute-done.6.refs_1_ = f32[64,128]{1,0:T(8,128)S(1)} collective-permute-done((f32[64,128]{1,0:T(8,128)S(1)}, f32[64,128]{1,0:T(8,128)S(1)}, u32[]{:S(2)}, u32[]{:S(2)}) %collective-permute-start.6) | collective-permute-done | bytes 32800 | tf_op jit(solution)/shard_map/ppermute | solution.py:282
  21.3 1.8 %inverse.1.inv = f32[64,128]{1,0:T(8,128)S(1)} custom-call(f32[64,128]{1,0:T(8,128)S(1)} %tick.9.g), custom_call_target="tpu_custom_call" | custom-call | tf_op jit(solution)/shard_map/inverse/pallas_call | solution.py:316
  23.2 1.1 %sketch.1 = (bf16[64,4096]{1,0:T(8,128)(2,1)S(1)}, f32[64,32]{1,0:T(8,128)S(1)}) custom-call(f32[64,128]{1,0:T(8,128)S(1)} %inverse.1.inv, f32[144,128]{1,0:T(8,128)S(1)} %get-tuple-element.23.mine, f32[136,128]{1,0:T(8,128)S(1)} %collective-permute-done.2.other, bf16[32,4096]{1,0:T(8,128)(2,1)S(1)} %pad_maximum_fusion.queries), custom_call_target="tpu_custom_call" | custom-call | tf_op jit(solution)/shard_map/sketch/pallas_call | solution.py:325
  24.2 0.0 collective-permute-done.7.far
  24.3 0.5 %score.1 = (f32[16,64]{1,0:T(8,128)S(1)}, f32[16,64]{1,0:T(8,128)S(1)}) custom-call(bf16[64,4096]{1,0:T(8,128)(2,1)S(1)} %get-tuple-element.29.lhs, f32[64,32]{1,0:T(8,128)S(1)} %get-tuple-element.30.inner, bf16[32,4096]{1,0:T(8,128)(2,1)S(1)} %collective-permute-done.7.far, f32[144,128]{1,0:T(8,128)S(1)} %get-tuple-element.23.mine), custom_call_target="tpu_custom_call" | custom-call | tf_op jit(solution)/shard_map/score/pallas_call | solution.py:336
  24.8 0.8 %collective-permute-start.8 = (f32[16,64]{1,0:T(8,128)S(1)}, f32[16,64]{1,0:T(8,128)S(1)}, u32[]{:S(2)}, u32[]{:S(2)}) collective-permute-start(f32[16,64]{1,0:T(8,128)S(1)} %get-tuple-element.32), channel_id=1, source_target_pairs={{0,1},{1,0},{2,3},{3,2},{4,5},{5,4},{6,7},{7,6},{8,9},{9,8},{10,11... | collective-permute-start | bytes 12296 | tf_op jit(solution)/shard_map/ppermute | solution.py:282
  25.6 0.8 %collective-permute-done.8 = f32[16,64]{1,0:T(8,128)S(1)} collective-permute-done((f32[16,64]{1,0:T(8,128)S(1)}, f32[16,64]{1,0:T(8,128)S(1)}, u32[]{:S(2)}, u32[]{:S(2)}) %collective-permute-start.8) | collective-permute-done | bytes 4128 | tf_op jit(solution)/shard_map/ppermute | solution.py:282
  26.4 0.6 %add.3 = f32[16,64]{1,0:T(8,128)} add(f32[16,64]{1,0:T(8,128)S(1)} %get-tuple-element.31, f32[16,64]{1,0:T(8,128)S(1)} %collective-permute-done.8) | non-fusion elementwise | flops 1024 | bytes 12288 | tf_op jit(solution)/shard_map/add | solution.py:347
  (16 shorter events, 0.1 us)
Async XLA Ops:
  0.0 0.8 %copy-start.6 = (bf16[2,4,4096]{2,1,0:T(4,128)(2,1)S(1)}, bf16[2,4,4096]{2,1,0:T(4,128)(2,1)}, u32[]{:S(2)}) copy-start(bf16[2,4,4096]{2,1,0:T(4,128)(2,1)} %param.12) | copy-start | bytes 196612
  0.0 4.3 %copy-start.1 = (bf16[4096,64]{0,1:T(8,128)(2,1)S(1)}, bf16[4096,64]{0,1:T(8,128)(2,1)}, u32[]{:S(2)}) copy-start(bf16[4096,64]{0,1:T(8,128)(2,1)} %param.11) | copy-start | bytes 1572868
  0.0 4.3 %copy-start = (bf16[2,128,4096]{2,1,0:T(8,128)(2,1)S(1)}, bf16[2,128,4096]{2,1,0:T(8,128)(2,1)}, u32[]{:S(2)}) copy-start(bf16[2,128,4096]{2,1,0:T(8,128)(2,1)} %grad.1) | copy-start | bytes 6291460
  0.0 5.0 %copy-start.2 = (bf16[2,128,14336]{2,1,0:T(8,128)(2,1)S(1)}, bf16[2,128,14336]{2,1,0:T(8,128)(2,1)}, u32[]{:S(2)}) copy-start(bf16[2,128,14336]{2,1,0:T(8,128)(2,1)} %act.1) | copy-start | bytes 22020100
  0.8 4.2 %copy-start.3 = (bf16[14336,64]{0,1:T(8,128)(2,1)S(1)}, bf16[14336,64]{0,1:T(8,128)(2,1)}, u32[]{:S(2)}) copy-start(bf16[14336,64]{0,1:T(8,128)(2,1)} %param.10) | copy-start | bytes 5505028
  0.8 4.2 %copy-start.4 = (s32[128]{0:T(128)S(1)}, s32[128]{0:T(128)}, u32[]{:S(2)}) copy-start(s32[128]{0:T(128)} %param.9) | copy-start | bytes 1540
  0.8 4.2 %copy-start.5 = (f32[2]{0:T(128)S(1)}, f32[2]{0:T(128)}, u32[]{:S(2)}) copy-start(f32[2]{0:T(128)} %param.13) | copy-start | bytes 28
  0.8 7.0 %collective-permute-start = (bf16[2,4,4096]{2,1,0:T(4,128)(2,1)S(1)}, bf16[2,4,4096]{2,1,0:T(4,128)(2,1)S(1)}, u32[]{:S(2)}, u32[]{:S(2)}) collective-permute-start(bf16[2,4,4096]{2,1,0:T(4,128)(2,1)S(1)} %copy-done.6), channel_id=1, source_target_pairs={{0,9},{1,8},{2,11},{3,10},{4,13},{5,12},{6,15},{7,14},{8,1},{9,0},... | collective-permute-start | bytes 196616 | tf_op jit(solution)/shard_map/ppermute | solution.py:282
  7.1 1.6 %collective-permute-start.2 = (f32[136,128]{1,0:T(8,128)S(1)}, f32[136,128]{1,0:T(8,128)S(1)}, u32[]{:S(2)}, u32[]{:S(2)}) collective-permute-start(f32[136,128]{1,0:T(8,128)S(1)} %get-tuple-element.24), channel_id=1, source_target_pairs={{0,1},{1,0},{2,3},{3,2},{4,5},{5,4},{6,7},{7,6},{8,9},{9,8},{10,11... | collective-permute-start | bytes 208904 | tf_op jit(solution)/shard_map/ppermute | solution.py:282
  8.0 3.2 %collective-permute-start.1 = (bf16[8,4096]{1,0:T(8,128)(2,1)S(1)}, bf16[8,4096]{1,0:T(8,128)(2,1)S(1)}, u32[]{:S(2)}, u32[]{:S(2)}) collective-permute-start(bf16[8,4096]{1,0:T(8,128)(2,1)S(1)} %get-tuple-element.34), channel_id=1, source_target_pairs={{0,1},{1,0},{2,3},{3,2},{4,5},{5,4},{6,7},{7,6},{8,9},{9,8},{10,11... | collective-permute-start | bytes 196616 | tf_op jit(solution)/shard_map/ppermute | solution.py:282
  9.1 3.6 %collective-permute-start.4 = (f32[64,128]{1,0:T(8,128)S(1)}, f32[64,128]{1,0:T(8,128)S(1)}, u32[]{:S(2)}, u32[]{:S(2)}) collective-permute-start(f32[64,128]{1,0:T(8,128)S(1)} %gram.1.refs_0_), channel_id=1, source_target_pairs={{0,3},{1,2},{2,1},{3,0},{4,7},{5,6},{6,5},{7,4},{8,11},{9,10},{10,... | collective-permute-start | bytes 98312 | tf_op jit(solution)/shard_map/ppermute | solution.py:282
  11.1 5.4 %collective-permute-start.3 = (bf16[16,4096]{1,0:T(8,128)(2,1)S(1)}, bf16[16,4096]{1,0:T(8,128)(2,1)S(1)}, u32[]{:S(2)}, u32[]{:S(2)}) collective-permute-start(bf16[16,4096]{1,0:T(8,128)(2,1)S(1)} %pad_maximum_fusion.1), channel_id=1, source_target_pairs={{0,5},{1,4},{2,7},{3,6},{4,1},{5,0},{6,3},{7,2},{8,13},{9,12},{10,... | collective-permute-start | bytes 393224 | tf_op jit(solution)/shard_map/ppermute | solution.py:282
  12.8 4.6 %collective-permute-start.5 = (f32[64,128]{1,0:T(8,128)S(1)}, f32[64,128]{1,0:T(8,128)S(1)}, u32[]{:S(2)}, u32[]{:S(2)}) collective-permute-start(f32[64,128]{1,0:T(8,128)S(1)} %tick.6.refs_0_), channel_id=1, source_target_pairs={{0,9},{1,8},{2,11},{3,10},{4,13},{5,12},{6,15},{7,14},{8,1},{9,0},... | collective-permute-start | bytes 98312 | tf_op jit(solution)/shard_map/ppermute | solution.py:282
  16.6 7.7 %collective-permute-start.7 = (bf16[32,4096]{1,0:T(8,128)(2,1)S(1)}, bf16[32,4096]{1,0:T(8,128)(2,1)S(1)}, u32[]{:S(2)}, u32[]{:S(2)}) collective-permute-start(bf16[32,4096]{1,0:T(8,128)(2,1)S(1)} %pad_maximum_fusion.queries), channel_id=1, source_target_pairs={{0,3},{1,2},{2,1},{3,0},{4,7},{5,6},{6,5},{7,4},{8,11},{9,10},{10,... | collective-permute-start | bytes 786440 | tf_op jit(solution)/shard_map/ppermute | solution.py:282
  17.3 4.0 %collective-permute-start.6 = (f32[64,128]{1,0:T(8,128)S(1)}, f32[64,128]{1,0:T(8,128)S(1)}, u32[]{:S(2)}, u32[]{:S(2)}) collective-permute-start(f32[64,128]{1,0:T(8,128)S(1)} %tick.8.refs_0_), channel_id=1, source_target_pairs={{0,5},{1,4},{2,7},{3,6},{4,1},{5,0},{6,3},{7,2},{8,13},{9,12},{10,... | collective-permute-start | bytes 98312 | tf_op jit(solution)/shard_map/ppermute | solution.py:282
  24.8 1.6 %collective-permute-start.8 = (f32[16,64]{1,0:T(8,128)S(1)}, f32[16,64]{1,0:T(8,128)S(1)}, u32[]{:S(2)}, u32[]{:S(2)}) collective-permute-start(f32[16,64]{1,0:T(8,128)S(1)} %get-tuple-element.32), channel_id=1, source_target_pairs={{0,1},{1,0},{2,3},{3,2},{4,5},{5,4},{6,7},{7,6},{8,9},{9,8},{10,11... | collective-permute-start | bytes 12296 | tf_op jit(solution)/shard_map/ppermute | solution.py:282
